TPU v7x, 32 devices: a whole 2x2x4 slice. The times are simulated.
32 devices in a mesh: island: 2 (over y), fsdp: 4 (over z), tensor: 4 (over x, core).
Axes of the slice: x: 2, y: 2, z: 4, core: 2. Of those that a mesh axis runs over, the one named last changes fastest.
Arguments:
- tokens: bfloat16 [1024, 6144], P(('island', 'fsdp')), may hold values from -6 to 6
- key_weight: bfloat16 [2, 6144, 1024], P('island', 'fsdp', 'tensor'), may hold values from -0.078125 to 0.078125
- key_cotangent: bfloat16 [1024, 1024], P(('island', 'fsdp'), 'tensor'), may hold values from -6 to 6
- local_frag: bfloat16 [2, 2, 6144, 2048], P('island', None, 'fsdp', 'tensor'), may hold values from -6 to 6
- outer_frag: float32 [2, 6144, 2048], P(None, 'fsdp', 'tensor'), may hold values from -6 to 6
- momentum: float32 [2, 6144, 2048], P(None, 'fsdp', 'tensor'), may hold values from -6 to 6
Outputs:
- keys: bfloat16 [1024, 1024], P(('island', 'fsdp'), 'tensor')
- input_grad: bfloat16 [1024, 6144], P(('island', 'fsdp', 'tensor'))
- weight_grad: bfloat16 [2, 6144, 1024], P('island', 'fsdp', 'tensor')
- new_outer: float32 [2, 6144, 2048], P(None, 'fsdp', 'tensor')
- new_momentum: float32 [2, 6144, 2048], P(None, 'fsdp', 'tensor')
All inputs are finite; a program needn't handle non-finite values.
Results may differ from a plain program's by a relative error of at most 0.015.
Values may be sent and summed in bfloat16 or wider, within the bound.
No kernel may reach another device: no remote copies, remote signals or barrier semaphores. Data moves between devices by JAX's collectives and lax.ppermute only.
A program may use at most 128 MiB of HBM per device.

v0:
```python
import jax
import jax.numpy as jnp
from jax import lax
from jax.sharding import PartitionSpec as P

outer_rate = 0.7
beta_outer = 0.9


def body(tokens, key_weight, key_cotangent, local_frag, outer_frag, momentum):
    own_shard = key_weight[0]
    gathered = lax.all_gather(own_shard, "fsdp", axis=0, tiled=True)
    keys = jnp.dot(tokens, gathered, preferred_element_type=jnp.float32).astype(jnp.bfloat16)
    input_grad = lax.psum_scatter(
        lax.dot_general(
            key_cotangent, gathered, (((1,), (1,)), ((), ())), preferred_element_type=jnp.float32
        ).astype(jnp.bfloat16),
        "tensor",
        scatter_dimension=0,
        tiled=True,
    )
    weight_grad = lax.psum_scatter(
        lax.dot_general(
            tokens, key_cotangent, (((0,), (0,)), ((), ())), preferred_element_type=jnp.float32
        ).astype(jnp.bfloat16),
        "fsdp",
        scatter_dimension=0,
        tiled=True,
    )
    own_frag = local_frag[0]
    islands = lax.axis_size("island")
    average = outer_frag - lax.psum(own_frag, "island").astype(jnp.float32) / islands
    new_momentum = beta_outer * momentum + average
    new_outer = outer_frag - outer_rate * (average + beta_outer * new_momentum)
    return (keys, input_grad, weight_grad[None], new_outer, new_momentum)


def solution(mesh):
    return jax.shard_map(
        body,
        mesh=mesh,
        in_specs=(
            P(("island", "fsdp"), None),
            P("island", "fsdp", "tensor"),
            P(("island", "fsdp"), "tensor"),
            P("island", None, "fsdp", "tensor"),
            P(None, "fsdp", "tensor"),
            P(None, "fsdp", "tensor"),
        ),
        out_specs=(
            P(("island", "fsdp"), "tensor"),
            P(("island", "fsdp", "tensor"), None),
            P("island", "fsdp", "tensor"),
            P(None, "fsdp", "tensor"),
            P(None, "fsdp", "tensor"),
        ),
        check_vma=False,
    )
```

profile of v0, /device:TPU:0, one launch (start us, length us, event | category | flops | bytes accessed | tf_op | source)
XLA Modules:
  0.0 177.0 jit_solution(4143809098860287838)
XLA Ops:
  8.0 0.0 copy-start
  8.0 0.0 copy-start.2
  8.0 0.0 all-gather.3.cloned.1.call-start
  8.1 0.7 all-gather.3.cloned.1.call-update
  8.8 0.0 all-reduce.2.cloned.1.call-start
  8.8 0.5 all-reduce.2.cloned.1.call-update
  9.3 0.0 reduce-scatter.5.cloned.1.call-start
  9.4 0.0 copy-done
  9.4 0.0 copy-done.2
  9.4 2.7 %convolution_convert_fusion = bf16[6144,256]{1,0:T(8,128)(2,1)} fusion(bf16[128,6144]{1,0:T(8,128)(2,1)S(1)} %copy-done, bf16[128,256]{1,0:T(8,128)(2,1)S(1)} %copy-done.2), kind=kOutput, calls=%fused_computation | convolution fusion | flops 404226048 | bytes 4784128 | tf_op jit(solution)/shard_map/dot_general | solution.py:23
  12.1 0.0 reduce-scatter.5.cloned.1.call-update
  12.1 0.0 reduce-scatter.3.cloned.1.call-start
  12.2 64.5 %all-gather.3.cloned.1.call-done = bf16[1,6144,256]{2,1,0:T(8,128)(2,1)} async-done(((bf16[1,1536,256]{2,1,0:T(8,128)(2,1)}), bf16[1,6144,256]{2,1,0:T(8,128)(2,1)}) %all-gather.3.cloned.1.call-update) | async-done | bytes 3145744 | tf_op jit(solution)/shard_map/all_gather | solution.py:12
  76.7 4.2 %convolution_convert_fusion.1 = bf16[128,6144]{1,0:T(8,128)(2,1)} fusion(bf16[128,256]{1,0:T(8,128)(2,1)S(1)} %copy-done.2, bf16[1,6144,256]{2,1,0:T(8,128)(2,1)} %all-gather.3.cloned.1.call-done), kind=kOutput, calls=%fused_computation.1 | convolution fusion | flops 403439616 | bytes 4784128 | tf_op jit(solution)/shard_map/dot_general | solution.py:15
  80.9 0.0 reduce-scatter.3.cloned.1.call-update
  80.9 19.0 %all-reduce.2.cloned.1.call-done = bf16[2,1536,512]{2,1,0:T(8,128)(2,1)} async-done(((bf16[2,1536,512]{2,1,0:T(8,128)(2,1)}), bf16[2,1536,512]{2,1,0:T(8,128)(2,1)}) %all-reduce.2.cloned.1.call-update) | async-done | bytes 3145744 | tf_op jit(solution)/shard_map/psum | solution.py:32
  99.9 0.0 copy-start.1
  99.9 9.8 %multiply_subtract_fusion = (f32[2,1536,512]{2,1,0:T(8,128)}, f32[2,1536,512]{2,1,0:T(8,128)}) fusion(f32[2,1536,512]{2,1,0:T(8,128)} %param.10, bf16[2,1536,512]{2,1,0:T(8,128)(2,1)} %all-reduce.2.cloned.1.call-done, f32[2,1536,512]{2,1,0:T(8,128)} %param.11), kind=kLoop, calls=%fused_computation.2 | loop fusion | flops 14155776 | bytes 28311552 | tf_op jit(solution)/shard_map/sub | solution.py:34
  109.7 0.0 copy-done.1
  109.8 1.2 fusion.3
  111.0 27.5 %reduce-scatter.5.cloned.1.call-done = bf16[1536,256]{1,0:T(8,128)(2,1)} async-done(((bf16[6144,256]{1,0:T(8,128)(2,1)}), bf16[1536,256]{1,0:T(8,128)(2,1)}) %reduce-scatter.5.cloned.1.call-update) | async-done | bytes 786448 | tf_op jit(solution)/shard_map/reduce_scatter | solution.py:22
  138.5 31.4 %reduce-scatter.3.cloned.1.call-done = bf16[32,6144]{1,0:T(8,128)(2,1)} async-done(((bf16[128,6144]{1,0:T(8,128)(2,1)}), bf16[32,6144]{1,0:T(8,128)(2,1)}) %reduce-scatter.3.cloned.1.call-update) | async-done | bytes 393232 | tf_op jit(solution)/shard_map/reduce_scatter | solution.py:14
Async XLA Ops:
  8.0 1.4 copy-start
  8.0 1.4 copy-start.2
  8.0 68.6 %all-gather.3.cloned.1.call-start = ((), (), s32[]{:S(2)}) async-start(), calls=%async_computation.5 | async-start | bytes 3932160 | tf_op jit(solution)/shard_map/all_gather | solution.py:12
  8.8 91.1 %all-reduce.2.cloned.1.call-start = ((), (), s32[]{:S(2)}) async-start(), calls=%async_computation.4 | async-start | bytes 6291456 | tf_op jit(solution)/shard_map/psum | solution.py:32
  9.3 129.1 %reduce-scatter.5.cloned.1.call-start = ((), (), s32[]{:S(2)}) async-start(), calls=%async_computation.3 | async-start | bytes 3932160 | tf_op jit(solution)/shard_map/reduce_scatter | solution.py:22
  12.1 157.7 %reduce-scatter.3.cloned.1.call-start = ((), (), s32[]{:S(2)}) async-start(), calls=%async_computation.2 | async-start | bytes 1966080 | tf_op jit(solution)/shard_map/reduce_scatter | solution.py:14
  99.9 9.8 %copy-start.1 = (bf16[1,6144,256]{2,1,0:T(8,128)(2,1)S(1)}, bf16[1,6144,256]{2,1,0:T(8,128)(2,1)}, u32[]{:S(2)}) copy-start(bf16[1,6144,256]{2,1,0:T(8,128)(2,1)} %all-gather.3.cloned.1.call-done) | copy-start | bytes 9437188
Sparse Core Ops, SparseCore 0:
  10.4 66.1 all-gather.2
  79.5 58.8 reduce-scatter.4
  141.6 28.1 reduce-scatter.2
Sparse Core Ops, SparseCore 1:
  11.6 88.2 all-reduce.1
where the time goes:
time: 177 us
  waiting for transfers between devices  144 us (81%)
  between operations  15.2 us (9%)
  other arithmetic  9.84 us (6%)
  matrix products  8.13 us (5%)
    all_gather x1, waiting for transfers between devices, body(): gathered = lax.all_gather(own_shard, 'fsdp', axis=0, tiled=True)  64.5 us
    reduce_scatter x1, waiting for transfers between devices, body(): lax.psum_scatter(lax.dot_general(key_cotangent, gathered, (((1,), (1,)),...  31.4 us
    reduce_scatter x1, waiting for transfers between devices, body(): lax.psum_scatter(lax.dot_general(tokens, key_cotangent, (((0,), (0,)), ((...  27.5 us
    psum x1, waiting for transfers between devices, body(): lax.psum(own_frag, 'island').astype(jnp.float32) / islands  19 us
    sub x1, other arithmetic, body(): new_outer = outer_frag - outer_rate * (average + beta_outer * new_momentum)  9.84 us
    dot_general x1, matrix products, body(): lax.dot_general(key_cotangent, gathered, (((1,), (1,)), ((), ())), prefer...  4.2 us
  transfers between devices with their start and end apart: 4, of which 4 were waited for; matrix products, arithmetic and copies ran while one was open for 10% of the time, Pallas kernels for 0%

commit v1 on v0

v1 whole, which is shorter than its diff:
```python
import functools

import jax
import jax.numpy as jnp
from jax import lax
from jax.experimental import pallas as pl
from jax.experimental.pallas import tpu as pltpu
from jax.sharding import PartitionSpec as P

outer_rate = 0.7
beta_outer = 0.9
F32 = jnp.float32
BF16 = jnp.bfloat16


def nesterov(frag_sum, outer, momentum, islands):
    average = outer - frag_sum / islands
    new_momentum = beta_outer * momentum + average
    return outer - outer_rate * (average + beta_outer * new_momentum), new_momentum


def update_kernel(islands, theirs, ours, outer, momentum, *refs):
    new_outer, new_momentum = refs[-2:]
    frag_sum = ours[...].astype(F32) + theirs[...].astype(F32)
    new_outer[...], new_momentum[...] = nesterov(frag_sum, outer[...], momentum[...], islands)


def update_chunk(theirs, ours, outer, momentum, done, first, block, islands):
    rows, cols = theirs.shape
    here = pl.BlockSpec((block, cols), lambda i: (i, 0))
    there = pl.BlockSpec((block, cols), lambda i: (i + first // block, 0))
    kept = [pl.BlockSpec(memory_space=pl.ANY)] * len(done)
    return pl.pallas_call(
        functools.partial(update_kernel, islands),
        grid=(rows // block,),
        in_specs=[here, there, there, there] + kept,
        out_specs=[there, there],
        out_shape=[jax.ShapeDtypeStruct(outer.shape, F32)] * 2,
        input_output_aliases={4 + i: i for i in range(len(done))},
        cost_estimate=pl.CostEstimate(flops=10 * rows * cols, bytes_accessed=20 * rows * cols, transcendentals=0),
    )(theirs, ours, outer, momentum, *done)


def outer_step(local_frag, outer_frag, momentum):
    islands = lax.axis_size("island")
    if islands != 2:
        return nesterov(lax.psum(local_frag[0], "island").astype(F32), outer_frag, momentum, islands)
    cols = local_frag.shape[-1]
    ours, outer, held = (a.reshape(-1, cols) for a in (local_frag, outer_frag, momentum))
    units = 16
    block = ours.shape[0] // units
    sizes = [1, 2, 2, 2, 2, 2, 2, 2, 1]
    starts = [sum(sizes[:k]) * block for k in range(len(sizes))]
    swap = [(0, 1), (1, 0)]
    source = ours
    arrived = []
    for size, first in zip(sizes, starts):
        piece = lax.slice_in_dim(source, first, first + size * block)
        if first == 0:
            piece, source = lax.optimization_barrier((piece, source))
        arrived.append(lax.ppermute(piece, "island", swap))
    done = ()
    for theirs, first in zip(arrived, starts):
        done = update_chunk(theirs, ours, outer, held, done, first, block, islands)
    return tuple(a.reshape(outer_frag.shape) for a in done)


def shifted(x, axis, step):
    n = lax.axis_size(axis)
    return lax.ppermute(x, axis, [(i, (i + step) % n) for i in range(n)])


def sum_scatter(part_of, axis):
    n = lax.axis_size(axis)
    if n & (n - 1):
        me = lax.axis_index(axis)
        stacked = jnp.concatenate([part_of([lax.rem(me + k, n)])[None] for k in range(n)]).astype(BF16)
        return lax.psum_scatter(jnp.roll(stacked, me, axis=0), axis, scatter_dimension=0)[0].astype(F32)
    me = lax.axis_index(axis)
    received = {k: [] for k in range(n)}
    bit = 1
    while bit < n:
        leaving = [k for k in range(bit, n, 2 * bit)]
        part = part_of([me ^ k for k in leaving])
        if any(received[k] for k in leaving):
            part = part + sum(jnp.concatenate(r) for r in zip(*(received[k] for k in leaving)))
        came = lax.ppermute(part.astype(BF16), axis, [(i, i ^ bit) for i in range(n)])
        for slot, block in zip(leaving, jnp.split(came.astype(F32), len(leaving))):
            received[slot ^ bit].append(block)
        bit *= 2
    return part_of([me]) + sum(received[0])


def projection_step(tokens, weight, cotangent):
    shards, heads = lax.axis_size("fsdp"), lax.axis_size("tensor")
    me = lax.axis_index("fsdp")
    width = weight.shape[0]
    rows = tokens.shape[0]
    cots = [cotangent] + [shifted(cotangent, "fsdp", s) for s in range(1, shards)]
    toks = []
    for s in range(shards):
        piece = lax.dynamic_slice_in_dim(tokens, lax.rem(me + s, shards) * width, width, 1)
        toks.append(shifted(piece, "fsdp", s) if s else piece)

    share = rows // heads
    all_cots = jnp.stack(cots)

    def part_of(members):
        mine = jnp.concatenate([lax.dynamic_slice_in_dim(all_cots, m * share, share, 1) for m in members])
        return lax.dot_general(mine.reshape(-1, mine.shape[-1]), weight, (((1,), (1,)), ((), ())), preferred_element_type=F32)

    summed = sum_scatter(part_of, "tensor").astype(BF16).reshape(shards, share, width)
    pieces = [summed[0]] + [shifted(summed[s], "fsdp", -s) for s in range(1, shards)]
    input_grad = jnp.roll(jnp.concatenate(pieces, axis=1), me * width, axis=1)

    weight_grad = lax.dot_general(
        jnp.concatenate(toks), jnp.concatenate(cots), (((0,), (0,)), ((), ())), preferred_element_type=F32
    ).astype(BF16)

    keys = jnp.dot(toks[0], weight, preferred_element_type=F32)
    for s in range(1, shards):
        part = jnp.dot(toks[s], weight, preferred_element_type=F32).astype(BF16)
        keys = keys + shifted(part, "fsdp", -s).astype(F32)
    return keys.astype(BF16), input_grad, weight_grad


def body(tokens, key_weight, key_cotangent, local_frag, outer_frag, momentum):
    new_outer, new_momentum = outer_step(local_frag, outer_frag, momentum)
    keys, input_grad, weight_grad = projection_step(tokens, key_weight[0], key_cotangent)
    return (keys, input_grad, weight_grad[None], new_outer, new_momentum)


def solution(mesh):
    return jax.shard_map(
        body,
        mesh=mesh,
        in_specs=(
            P(("island", "fsdp"), None),
            P("island", "fsdp", "tensor"),
            P(("island", "fsdp"), "tensor"),
            P("island", None, "fsdp", "tensor"),
            P(None, "fsdp", "tensor"),
            P(None, "fsdp", "tensor"),
        ),
        out_specs=(
            P(("island", "fsdp"), "tensor"),
            P(("island", "fsdp", "tensor"), None),
            P("island", "fsdp", "tensor"),
            P(None, "fsdp", "tensor"),
            P(None, "fsdp", "tensor"),
        ),
        check_vma=False,
    )
```

time: 177 us -> 103 us (0.58)
  waiting for transfers between devices: 144 us -> 24.9 us
  starting transfers between devices: 0.16 us -> 25.9 us
  Pallas kernels: 0 us -> 23.6 us
  between operations: 15.2 us -> 0.82 us
  local copies, waits for them, and re-layouts: 0.04 us -> 9.52 us
  other arithmetic: 9.84 us -> 5.01 us
  matrix products: 8.13 us -> 12.2 us
    all_gather x1 -> x0, waiting for transfers between devices: 64.5 us -> none  [body(): gathered = lax.all_gather(own_shard, 'fsdp', axis=0, tiled=True)]
    reduce_scatter x2 -> x0, waiting for transfers between devices: 58.8 us -> none  [the longest x1 31.4 us: body(): lax.psum_scatter(lax.dot_general(key_cotangent, gathered, (((1,), (1,)),...]
    ppermute x0 -> x23, starting transfers between devices: none -> 25.9 us  [the longest x12 15.6 us: shifted(): return lax.ppermute(x, axis, [(i, (i + step) % n) for i in range(n)])]
    ppermute x0 -> x23, waiting for transfers between devices: none -> 24.9 us  [the longest x9 19.3 us: outer_step(): arrived.append(lax.ppermute(piece, 'island', swap))]
    pallas_call x0 -> x9, Pallas kernels: none -> 23.6 us  [update_chunk(): pl.pallas_call(functools.partial(update_kernel, islands), grid=(rows // b...]
    psum x1 -> x0, waiting for transfers between devices: 19 us -> none  [body(): lax.psum(own_frag, 'island').astype(jnp.float32) / islands]
    sub x1 -> x0, other arithmetic: 9.84 us -> none  [body(): new_outer = outer_frag - outer_rate * (average + beta_outer * new_momentum)]
    slice x0 -> x4, local copies, waits for them, and re-layouts: none -> 6.39 us  [the longest x3 6.37 us: outer_step(): piece = lax.slice_in_dim(source, first, first + size * block)]
  transfers between devices with their start and end apart: 4 -> 23, of which waited for: 4 -> 5; matrix products, arithmetic and copies ran while one was open for 10% -> 25% of each run, Pallas kernels for 0% -> 23%
where the time goes in v1:
time: 103 us; the launch traced here: 102 us
  starting transfers between devices  25.9 us (25%)
  waiting for transfers between devices  24.9 us (24%)
  Pallas kernels  23.6 us (23%)
  matrix products  12.2 us (12%)
  local copies, waits for them, and re-layouts  9.52 us (9%)
  other arithmetic  5.01 us (5%)
    pallas_call x9, Pallas kernels, update_chunk(): pl.pallas_call(functools.partial(update_kernel, islands), grid=(rows // b...  23.6 us
    ppermute x9, waiting for transfers between devices, outer_step(): arrived.append(lax.ppermute(piece, 'island', swap))  19.3 us
    ppermute x12, starting transfers between devices, shifted(): return lax.ppermute(x, axis, [(i, (i + step) % n) for i in range(n)])  15.6 us
    ppermute x9, starting transfers between devices, outer_step(): arrived.append(lax.ppermute(piece, 'island', swap))  8.75 us
    slice x3, local copies, waits for them, and re-layouts, outer_step(): piece = lax.slice_in_dim(source, first, first + size * block)  6.37 us
    dot_general x3, matrix products, projection_step(): part = jnp.dot(toks[s], weight, preferred_element_type=F32).astype(BF16)  5.69 us
    ppermute x12, waiting for transfers between devices, shifted(): return lax.ppermute(x, axis, [(i, (i + step) % n) for i in range(n)])  5.57 us
    dot_general x3, matrix products, part_of(): lax.dot_general(mine.reshape(-1, mine.shape[-1]), weight, (((1,), (1,)),...  2.78 us
  transfers between devices with their start and end apart: 23, of which 5 were waited for; matrix products, arithmetic and copies ran while one was open for 25% of the time, Pallas kernels for 23%

profile of v1, /device:TPU:0, one launch (start us, length us, event | category | flops | bytes accessed | tf_op | source)
XLA Modules:
  0.0 101.9 jit_solution(15997621457561086632)
XLA Ops:
  0.7 3.1 %collective-permute-start.6 = (bf16[128,256]{1,0:T(8,128)(2,1)}, bf16[128,256]{1,0:T(8,128)(2,1)}, u32[]{:S(2)}, u32[]{:S(2)}) collective-permute-start(bf16[128,256]{1,0:T(8,128)(2,1)} %param.8), channel_id=1, source_target_pairs={{0,4},{4,8},{8,12},{12,0},{1,5},{5,9},{9,13},{13,1},{2,6},{6,10},{... | collective-permute-start | bytes 196616 | tf_op jit(solution)/shard_map/ppermute | solution.py:70
  3.7 2.6 %collective-permute-start.7 = (bf16[128,256]{1,0:T(8,128)(2,1)}, bf16[128,256]{1,0:T(8,128)(2,1)}, u32[]{:S(2)}, u32[]{:S(2)}) collective-permute-start(bf16[128,256]{1,0:T(8,128)(2,1)} %param.8), channel_id=1, source_target_pairs={{0,8},{4,12},{8,0},{12,4},{1,9},{5,13},{9,1},{13,5},{2,10},{6,14},... | collective-permute-start | bytes 196616 | tf_op jit(solution)/shard_map/ppermute | solution.py:70
  10.8 3.1 %fusion.31 = (bf16[384,512]{1,0:T(8,128)(2,1)S(1)}, bf16[384,512]{1,0:T(8,128)(2,1)}, bf16[384,512]{1,0:T(8,128)(2,1)}, bf16[384,512]{1,0:T(8,128)(2,1)}, bf16[3...) fusion(bf16[3072,512]{1,0:T(8,128)(2,1)} %bitcast.59), kind=kLoop, calls=%fused_computation.56 | loop fusion | bytes 5505024 | tf_op jit(solution)/shard_map/slice | solution.py:58
  22.9 3.1 %collective-permute-done.21.theirs = bf16[384,512]{1,0:T(8,128)(2,1)S(1)} collective-permute-done((bf16[384,512]{1,0:T(8,128)(2,1)S(1)}, bf16[384,512]{1,0:T(8,128)(2,1)S(1)}, u32[]{:S(2)}, u32[]{:S(2)}) %collective-permute-start.21) | collective-permute-done | bytes 393248 | tf_op jit(solution)/shard_map/ppermute | solution.py:61
  27.1 2.3 %shard_map.101 = (f32[3072,512]{1,0:T(8,128)}, f32[3072,512]{1,0:T(8,128)}) custom-call(bf16[192,512]{1,0:T(8,128)(2,1)} %collective-permute-done.22.theirs, bf16[3072,512]{1,0:T(8,128)(2,1)} %bitcast.61, f32[3072,512]{1,0:T(8,128)} %bitcast.38, f32[3072,512]{1,0:T(8,128)} %bitcast.47), custom_call_target="tpu_custom_call" | custom-call | flops 983040 | bytes 1966080 | tf_op jit(solution)/shard_map/pallas_call | solution.py:33
  29.5 4.9 %collective-permute-done.20.theirs = bf16[384,512]{1,0:T(8,128)(2,1)S(1)} collective-permute-done((bf16[384,512]{1,0:T(8,128)(2,1)}, bf16[384,512]{1,0:T(8,128)(2,1)S(1)}, u32[]{:S(2)}, u32[]{:S(2)}) %collective-permute-start.20) | collective-permute-done | bytes 393248 | tf_op jit(solution)/shard_map/ppermute | solution.py:61
  34.9 8.0 %collective-permute-done.19.theirs = bf16[384,512]{1,0:T(8,128)(2,1)} collective-permute-done((bf16[384,512]{1,0:T(8,128)(2,1)}, bf16[384,512]{1,0:T(8,128)(2,1)}, u32[]{:S(2)}, u32[]{:S(2)}) %collective-permute-start.19) | collective-permute-done | bytes 393248 | tf_op jit(solution)/shard_map/ppermute | solution.py:61
  45.0 1.9 %convolution_convert_fusion.4 = bf16[128,256]{1,0:T(8,128)(2,1)} fusion(bf16[128,1536]{1,0:T(8,128)(2,1)} %collective-permute-done, bf16[1,1536,256]{2,1,0:T(8,128)(2,1)S(1)} %copy-done), kind=kOutput, calls=%fused_computation.12 | convolution fusion | flops 100696064 | bytes 1245184 | tf_op jit(solution)/shard_map/dot_general | solution.py:122
  47.3 1.9 %convolution_convert_fusion.3 = bf16[128,256]{1,0:T(8,128)(2,1)} fusion(bf16[128,1536]{1,0:T(8,128)(2,1)} %collective-permute-done.2, bf16[1,1536,256]{2,1,0:T(8,128)(2,1)S(1)} %copy-done), kind=kOutput, calls=%fused_computation.11 | convolution fusion | flops 100696064 | bytes 1245184 | tf_op jit(solution)/shard_map/dot_general | solution.py:122
  49.2 2.7 %shard_map.102 = (f32[3072,512]{1,0:T(8,128)}, f32[3072,512]{1,0:T(8,128)}) custom-call(bf16[384,512]{1,0:T(8,128)(2,1)} %copy-done.3, bf16[3072,512]{1,0:T(8,128)(2,1)} %bitcast.62, f32[3072,512]{1,0:T(8,128)} %bitcast.39, f32[3072,512]{1,0:T(8,128)} %bitcast.48, ...), custom_call_target="tpu_custom_call", output_to_operand_aliasing={{0}: (4, {}), {1}: (5, {})} | custom-call | flops 1966080 | bytes 3932160 | tf_op jit(solution)/shard_map/pallas_call | solution.py:33
  51.9 2.7 %shard_map.103 = (f32[3072,512]{1,0:T(8,128)}, f32[3072,512]{1,0:T(8,128)}) custom-call(bf16[384,512]{1,0:T(8,128)(2,1)} %copy-done.4, bf16[3072,512]{1,0:T(8,128)(2,1)} %bitcast.63, f32[3072,512]{1,0:T(8,128)} %bitcast.40, f32[3072,512]{1,0:T(8,128)} %bitcast.49, ...), custom_call_target="tpu_custom_call", output_to_operand_aliasing={{0}: (4, {}), {1}: (5, {})} | custom-call | flops 1966080 | bytes 3932160 | tf_op jit(solution)/shard_map/pallas_call | solution.py:33
  54.7 2.7 %shard_map.104 = (f32[3072,512]{1,0:T(8,128)}, f32[3072,512]{1,0:T(8,128)}) custom-call(bf16[384,512]{1,0:T(8,128)(2,1)} %collective-permute-done.19.theirs, bf16[3072,512]{1,0:T(8,128)(2,1)} %bitcast.64, f32[3072,512]{1,0:T(8,128)} %bitcast.41, f32[3072,512]{1,0:T(8,128)} %bitcast.50, ...), custom_call_target="tpu_custom_call", output_to_operand_aliasing={{0}: (4, {}), {1}: (5, {})} | custom-call | flops 1966080 | bytes 3932160 | tf_op jit(solution)/shard_map/pallas_call | solution.py:33
  58.0 2.7 %shard_map.105 = (f32[3072,512]{1,0:T(8,128)}, f32[3072,512]{1,0:T(8,128)}) custom-call(bf16[384,512]{1,0:T(8,128)(2,1)} %collective-permute-done.18.theirs, bf16[3072,512]{1,0:T(8,128)(2,1)} %bitcast.65, f32[3072,512]{1,0:T(8,128)} %bitcast.42, f32[3072,512]{1,0:T(8,128)} %bitcast.51, ...), custom_call_target="tpu_custom_call", output_to_operand_aliasing={{0}: (4, {}), {1}: (5, {})} | custom-call | flops 1966080 | bytes 3932160 | tf_op jit(solution)/shard_map/pallas_call | solution.py:33
  62.3 2.7 %shard_map.106 = (f32[3072,512]{1,0:T(8,128)}, f32[3072,512]{1,0:T(8,128)}) custom-call(bf16[384,512]{1,0:T(8,128)(2,1)} %collective-permute-done.17.theirs, bf16[3072,512]{1,0:T(8,128)(2,1)} %bitcast.66, f32[3072,512]{1,0:T(8,128)} %bitcast.43, f32[3072,512]{1,0:T(8,128)} %bitcast.52, ...), custom_call_target="tpu_custom_call", output_to_operand_aliasing={{0}: (4, {}), {1}: (5, {})} | custom-call | flops 1966080 | bytes 3932160 | tf_op jit(solution)/shard_map/pallas_call | solution.py:33
  65.0 3.3 %collective-permute-done.16.theirs = bf16[384,512]{1,0:T(8,128)(2,1)} collective-permute-done((bf16[384,512]{1,0:T(8,128)(2,1)}, bf16[384,512]{1,0:T(8,128)(2,1)}, u32[]{:S(2)}, u32[]{:S(2)}) %collective-permute-start.16) | collective-permute-done | bytes 393248 | tf_op jit(solution)/shard_map/ppermute | solution.py:61
  68.7 2.7 %shard_map.107 = (f32[3072,512]{1,0:T(8,128)}, f32[3072,512]{1,0:T(8,128)}) custom-call(bf16[384,512]{1,0:T(8,128)(2,1)} %collective-permute-done.16.theirs, bf16[3072,512]{1,0:T(8,128)(2,1)} %bitcast.67, f32[3072,512]{1,0:T(8,128)} %bitcast.44, f32[3072,512]{1,0:T(8,128)} %bitcast.53, ...), custom_call_target="tpu_custom_call", output_to_operand_aliasing={{0}: (4, {}), {1}: (5, {})} | custom-call | flops 1966080 | bytes 3932160 | tf_op jit(solution)/shard_map/pallas_call | solution.py:33
  71.4 1.8 %collective-permute-start.3 = (bf16[128,256]{1,0:T(8,128)(2,1)}, bf16[128,256]{1,0:T(8,128)(2,1)}, u32[]{:S(2)}, u32[]{:S(2)}) collective-permute-start(bf16[128,256]{1,0:T(8,128)(2,1)} %convolution_convert_fusion.3), channel_id=1, source_target_pairs={{0,8},{4,12},{8,0},{12,4},{1,9},{5,13},{9,1},{13,5},{2,10},{6,14},... | collective-permute-start | bytes 196616 | tf_op jit(solution)/shard_map/ppermute | solution.py:70
  74.5 2.0 %fusion.8 = bf16[128,1536]{1,0:T(8,128)(2,1)} fusion(f32[256,1536]{1,0:T(8,128)S(1)} %convert_element_type.47, bf16[128,256]{1,0:T(8,128)(2,1)} %bitcast.71, bf16[1,1536,256]{2,1,0:T(8,128)(2,1)S(1)} %copy-done), kind=kOutput, calls=%fused_computation.14 | convolution fusion | flops 101056512 | bytes 2031616 | tf_op jit(solution)/shard_map/dot_general | solution.py:110
  77.9 1.9 %convolution_convert_fusion.2 = bf16[128,256]{1,0:T(8,128)(2,1)} fusion(bf16[128,1536]{1,0:T(8,128)(2,1)} %collective-permute-done.4, bf16[1,1536,256]{2,1,0:T(8,128)(2,1)S(1)} %copy-done), kind=kOutput, calls=%fused_computation.10 | convolution fusion | flops 100696064 | bytes 1245184 | tf_op jit(solution)/shard_map/dot_general | solution.py:122
  80.1 2.7 %shard_map.108 = (f32[3072,512]{1,0:T(8,128)}, f32[3072,512]{1,0:T(8,128)}) custom-call(bf16[384,512]{1,0:T(8,128)(2,1)} %collective-permute-done.15.theirs, bf16[3072,512]{1,0:T(8,128)(2,1)} %bitcast.68, f32[3072,512]{1,0:T(8,128)} %bitcast.45, f32[3072,512]{1,0:T(8,128)} %bitcast.54, ...), custom_call_target="tpu_custom_call", output_to_operand_aliasing={{0}: (4, {}), {1}: (5, {})} | custom-call | flops 1966080 | bytes 3932160 | tf_op jit(solution)/shard_map/pallas_call | solution.py:33
  82.8 2.3 %shard_map.109 = (f32[3072,512]{1,0:T(8,128)}, f32[3072,512]{1,0:T(8,128)}) custom-call(bf16[192,512]{1,0:T(8,128)(2,1)} %collective-permute-done.14.theirs, bf16[3072,512]{1,0:T(8,128)(2,1)} %bitcast.69, f32[3072,512]{1,0:T(8,128)} %bitcast.46, f32[3072,512]{1,0:T(8,128)} %bitcast.55, ...), custom_call_target="tpu_custom_call", output_to_operand_aliasing={{0}: (4, {}), {1}: (5, {})} | custom-call | flops 983040 | bytes 1966080 | tf_op jit(solution)/shard_map/pallas_call | solution.py:33
  85.1 2.8 %fusion = bf16[1,1536,256]{2,1,0:T(8,128)(2,1)} fusion(bf16[128,1536]{1,0:T(8,128)(2,1)} %collective-permute-done.4, bf16[128,1536]{1,0:T(8,128)(2,1)} %collective-permute-done.2, bf16[128,1536]{1,0:T(8,128)(2,1)} %collective-permute-done, bf16[128,1536]{1,0:T(8,128)(2,1)S(1)} %get-tuple-element.53, bf16[128,256]{1,0:T(8,128)(2,1)} %collective-permute-done.8, ...), kind=kOutput, calls=%fused_computation.2 | convolution fusion | flops 410386432 | bytes 2621440 | tf_op jit(solution)/shard_map/dot_general | solution.py:116
  89.1 3.7 %collective-permute-start.11 = (bf16[32,1536]{1,0:T(8,128)(2,1)S(1)}, bf16[32,1536]{1,0:T(8,128)(2,1)S(1)}, u32[]{:S(2)}, u32[]{:S(2)}) collective-permute-start(bf16[32,1536]{1,0:T(8,128)(2,1)S(1)} %get-tuple-element.59), channel_id=1, source_target_pairs={{0,12},{4,0},{8,4},{12,8},{1,13},{5,1},{9,5},{13,9},{2,14},{6,2},{... | collective-permute-start | bytes 294920 | tf_op jit(solution)/shard_map/ppermute | solution.py:70
  95.3 5.5 %collective-permute-done.12 = bf16[32,1536]{1,0:T(8,128)(2,1)S(1)} collective-permute-done((bf16[32,1536]{1,0:T(8,128)(2,1)S(1)}, bf16[32,1536]{1,0:T(8,128)(2,1)S(1)}, u32[]{:S(2)}, u32[]{:S(2)}) %collective-permute-start.12) | collective-permute-done | bytes 98336 | tf_op jit(solution)/shard_map/ppermute | solution.py:70
  (68 shorter events, 28.0 us)
Async XLA Ops:
  0.6 19.2 %copy-start = (bf16[1,1536,256]{2,1,0:T(8,128)(2,1)S(1)}, bf16[1,1536,256]{2,1,0:T(8,128)(2,1)}, u32[]{:S(2)}) copy-start(bf16[1,1536,256]{2,1,0:T(8,128)(2,1)} %param.7) | copy-start | bytes 2359300
  0.7 14.8 %collective-permute-start.6 = (bf16[128,256]{1,0:T(8,128)(2,1)}, bf16[128,256]{1,0:T(8,128)(2,1)}, u32[]{:S(2)}, u32[]{:S(2)}) collective-permute-start(bf16[128,256]{1,0:T(8,128)(2,1)} %param.8), channel_id=1, source_target_pairs={{0,4},{4,8},{8,12},{12,0},{1,5},{5,9},{9,13},{13,1},{2,6},{6,10},{... | collective-permute-start | bytes 196616 | tf_op jit(solution)/shard_map/ppermute | solution.py:70
  3.7 13.3 %collective-permute-start.7 = (bf16[128,256]{1,0:T(8,128)(2,1)}, bf16[128,256]{1,0:T(8,128)(2,1)}, u32[]{:S(2)}, u32[]{:S(2)}) collective-permute-start(bf16[128,256]{1,0:T(8,128)(2,1)} %param.8), channel_id=1, source_target_pairs={{0,8},{4,12},{8,0},{12,4},{1,9},{5,13},{9,1},{13,5},{2,10},{6,14},... | collective-permute-start | bytes 196616 | tf_op jit(solution)/shard_map/ppermute | solution.py:70
  6.3 11.2 %collective-permute-start.8 = (bf16[128,256]{1,0:T(8,128)(2,1)}, bf16[128,256]{1,0:T(8,128)(2,1)}, u32[]{:S(2)}, u32[]{:S(2)}) collective-permute-start(bf16[128,256]{1,0:T(8,128)(2,1)} %param.8), channel_id=1, source_target_pairs={{0,12},{4,0},{8,4},{12,8},{1,13},{5,1},{9,5},{13,9},{2,14},{6,2},{... | collective-permute-start | bytes 196616 | tf_op jit(solution)/shard_map/ppermute | solution.py:70
  9.3 11.0 %collective-permute-start.22 = (bf16[192,512]{1,0:T(8,128)(2,1)}, bf16[192,512]{1,0:T(8,128)(2,1)}, u32[]{:S(2)}, u32[]{:S(2)}) collective-permute-start(bf16[192,512]{1,0:T(8,128)(2,1)} %slice.60), channel_id=1, source_target_pairs={{0,16},{16,0},{1,17},{17,1},{2,18},{18,2},{3,19},{19,3},{4,20},{20... | collective-permute-start | bytes 589832 | tf_op jit(solution)/shard_map/ppermute | solution.py:61
  13.9 12.1 %collective-permute-start.21 = (bf16[384,512]{1,0:T(8,128)(2,1)S(1)}, bf16[384,512]{1,0:T(8,128)(2,1)S(1)}, u32[]{:S(2)}, u32[]{:S(2)}) collective-permute-start(bf16[384,512]{1,0:T(8,128)(2,1)S(1)} %get-tuple-element.45), channel_id=1, source_target_pairs={{0,16},{16,0},{1,17},{17,1},{2,18},{18,2},{3,19},{19,3},{4,20},{20... | collective-permute-start | bytes 1179656 | tf_op jit(solution)/shard_map/ppermute | solution.py:61
  15.5 18.9 %collective-permute-start.20 = (bf16[384,512]{1,0:T(8,128)(2,1)}, bf16[384,512]{1,0:T(8,128)(2,1)S(1)}, u32[]{:S(2)}, u32[]{:S(2)}) collective-permute-start(bf16[384,512]{1,0:T(8,128)(2,1)} %get-tuple-element.46), channel_id=1, source_target_pairs={{0,16},{16,0},{1,17},{17,1},{2,18},{18,2},{3,19},{19,3},{4,20},{20... | collective-permute-start | bytes 1179656 | tf_op jit(solution)/shard_map/ppermute | solution.py:61
  17.0 25.9 %collective-permute-start.19 = (bf16[384,512]{1,0:T(8,128)(2,1)}, bf16[384,512]{1,0:T(8,128)(2,1)}, u32[]{:S(2)}, u32[]{:S(2)}) collective-permute-start(bf16[384,512]{1,0:T(8,128)(2,1)} %get-tuple-element.47), channel_id=1, source_target_pairs={{0,16},{16,0},{1,17},{17,1},{2,18},{18,2},{3,19},{19,3},{4,20},{20... | collective-permute-start | bytes 1179656 | tf_op jit(solution)/shard_map/ppermute | solution.py:61
  17.5 25.9 %collective-permute-start = (bf16[128,1536]{1,0:T(8,128)(2,1)}, bf16[128,1536]{1,0:T(8,128)(2,1)}, u32[]{:S(2)}, u32[]{:S(2)}) collective-permute-start(bf16[128,1536]{1,0:T(8,128)(2,1)} %get-tuple-element.52), channel_id=1, source_target_pairs={{0,4},{4,8},{8,12},{12,0},{1,5},{5,9},{9,13},{13,1},{2,6},{6,10},{... | collective-permute-start | bytes 1179656 | tf_op jit(solution)/shard_map/ppermute | solution.py:70
  20.3 51.1 %collective-permute-start.9 = (bf16[256,1536]{1,0:T(8,128)(2,1)S(1)}, bf16[256,1536]{1,0:T(8,128)(2,1)}, u32[]{:S(2)}, u32[]{:S(2)}) collective-permute-start(bf16[256,1536]{1,0:T(8,128)(2,1)S(1)} %convolution_convert_fusion), channel_id=1, source_target_pairs={{0,1},{1,0},{2,3},{3,2},{4,5},{5,4},{6,7},{7,6},{8,9},{9,8},{10,11... | collective-permute-start | bytes 2359304 | tf_op jit(solution)/shard_map/ppermute | solution.py:87
  26.0 20.9 %collective-permute-start.2 = (bf16[128,1536]{1,0:T(8,128)(2,1)}, bf16[128,1536]{1,0:T(8,128)(2,1)}, u32[]{:S(2)}, u32[]{:S(2)}) collective-permute-start(bf16[128,1536]{1,0:T(8,128)(2,1)} %get-tuple-element.55), channel_id=1, source_target_pairs={{0,8},{4,12},{8,0},{12,4},{1,9},{5,13},{9,1},{13,5},{2,10},{6,14},... | collective-permute-start | bytes 1179656 | tf_op jit(solution)/shard_map/ppermute | solution.py:70
  34.4 23.0 %collective-permute-start.18 = (bf16[384,512]{1,0:T(8,128)(2,1)}, bf16[384,512]{1,0:T(8,128)(2,1)}, u32[]{:S(2)}, u32[]{:S(2)}) collective-permute-start(bf16[384,512]{1,0:T(8,128)(2,1)} %get-tuple-element.48), channel_id=1, source_target_pairs={{0,16},{16,0},{1,17},{17,1},{2,18},{18,2},{3,19},{19,3},{4,20},{20... | collective-permute-start | bytes 1179656 | tf_op jit(solution)/shard_map/ppermute | solution.py:61
  43.0 17.7 %collective-permute-start.17 = (bf16[384,512]{1,0:T(8,128)(2,1)}, bf16[384,512]{1,0:T(8,128)(2,1)}, u32[]{:S(2)}, u32[]{:S(2)}) collective-permute-start(bf16[384,512]{1,0:T(8,128)(2,1)} %get-tuple-element.49), channel_id=1, source_target_pairs={{0,16},{16,0},{1,17},{17,1},{2,18},{18,2},{3,19},{19,3},{4,20},{20... | collective-permute-start | bytes 1179656 | tf_op jit(solution)/shard_map/ppermute | solution.py:61
  43.5 24.8 %collective-permute-start.16 = (bf16[384,512]{1,0:T(8,128)(2,1)}, bf16[384,512]{1,0:T(8,128)(2,1)}, u32[]{:S(2)}, u32[]{:S(2)}) collective-permute-start(bf16[384,512]{1,0:T(8,128)(2,1)} %get-tuple-element.50), channel_id=1, source_target_pairs={{0,16},{16,0},{1,17},{17,1},{2,18},{18,2},{3,19},{19,3},{4,20},{20... | collective-permute-start | bytes 1179656 | tf_op jit(solution)/shard_map/ppermute | solution.py:61
  46.9 29.6 %collective-permute-start.4 = (bf16[128,1536]{1,0:T(8,128)(2,1)}, bf16[128,1536]{1,0:T(8,128)(2,1)}, u32[]{:S(2)}, u32[]{:S(2)}) collective-permute-start(bf16[128,1536]{1,0:T(8,128)(2,1)} %get-tuple-element.54), channel_id=1, source_target_pairs={{0,12},{4,0},{8,4},{12,8},{1,13},{5,1},{9,5},{13,9},{2,14},{6,2},{... | collective-permute-start | bytes 1179656 | tf_op jit(solution)/shard_map/ppermute | solution.py:70
  57.4 22.4 %collective-permute-start.15 = (bf16[384,512]{1,0:T(8,128)(2,1)}, bf16[384,512]{1,0:T(8,128)(2,1)}, u32[]{:S(2)}, u32[]{:S(2)}) collective-permute-start(bf16[384,512]{1,0:T(8,128)(2,1)} %get-tuple-element.51), channel_id=1, source_target_pairs={{0,16},{16,0},{1,17},{17,1},{2,18},{18,2},{3,19},{19,3},{4,20},{20... | collective-permute-start | bytes 1179656 | tf_op jit(solution)/shard_map/ppermute | solution.py:61
  60.7 22.1 %collective-permute-start.14 = (bf16[192,512]{1,0:T(8,128)(2,1)}, bf16[192,512]{1,0:T(8,128)(2,1)}, u32[]{:S(2)}, u32[]{:S(2)}) collective-permute-start(bf16[192,512]{1,0:T(8,128)(2,1)} %slice.48), channel_id=1, source_target_pairs={{0,16},{16,0},{1,17},{17,1},{2,18},{18,2},{3,19},{19,3},{4,20},{20... | collective-permute-start | bytes 589832 | tf_op jit(solution)/shard_map/ppermute | solution.py:61
  68.2 24.5 %collective-permute-start.1 = (bf16[128,256]{1,0:T(8,128)(2,1)}, bf16[128,256]{1,0:T(8,128)(2,1)}, u32[]{:S(2)}, u32[]{:S(2)}) collective-permute-start(bf16[128,256]{1,0:T(8,128)(2,1)} %convolution_convert_fusion.4), channel_id=1, source_target_pairs={{0,12},{4,0},{8,4},{12,8},{1,13},{5,1},{9,5},{13,9},{2,14},{6,2},{... | collective-permute-start | bytes 196616 | tf_op jit(solution)/shard_map/ppermute | solution.py:70
  71.4 21.3 %collective-permute-start.3 = (bf16[128,256]{1,0:T(8,128)(2,1)}, bf16[128,256]{1,0:T(8,128)(2,1)}, u32[]{:S(2)}, u32[]{:S(2)}) collective-permute-start(bf16[128,256]{1,0:T(8,128)(2,1)} %convolution_convert_fusion.3), channel_id=1, source_target_pairs={{0,8},{4,12},{8,0},{12,4},{1,9},{5,13},{9,1},{13,5},{2,10},{6,14},... | collective-permute-start | bytes 196616 | tf_op jit(solution)/shard_map/ppermute | solution.py:70
  76.4 11.4 %collective-permute-start.10 = (bf16[128,1536]{1,0:T(8,128)(2,1)}, bf16[128,1536]{1,0:T(8,128)(2,1)}, u32[]{:S(2)}, u32[]{:S(2)}) collective-permute-start(bf16[128,1536]{1,0:T(8,128)(2,1)} %fusion.8), channel_id=1, source_target_pairs={{0,2},{1,3},{2,0},{3,1},{4,6},{5,7},{6,4},{7,5},{8,10},{9,11},{10,... | collective-permute-start | bytes 1179656 | tf_op jit(solution)/shard_map/ppermute | solution.py:87
  79.8 12.9 %collective-permute-start.5 = (bf16[128,256]{1,0:T(8,128)(2,1)}, bf16[128,256]{1,0:T(8,128)(2,1)}, u32[]{:S(2)}, u32[]{:S(2)}) collective-permute-start(bf16[128,256]{1,0:T(8,128)(2,1)} %convolution_convert_fusion.2), channel_id=1, source_target_pairs={{0,4},{4,8},{8,12},{12,0},{1,5},{5,9},{9,13},{13,1},{2,6},{6,10},{... | collective-permute-start | bytes 196616 | tf_op jit(solution)/shard_map/ppermute | solution.py:70
  89.1 6.3 %collective-permute-start.11 = (bf16[32,1536]{1,0:T(8,128)(2,1)S(1)}, bf16[32,1536]{1,0:T(8,128)(2,1)S(1)}, u32[]{:S(2)}, u32[]{:S(2)}) collective-permute-start(bf16[32,1536]{1,0:T(8,128)(2,1)S(1)} %get-tuple-element.59), channel_id=1, source_target_pairs={{0,12},{4,0},{8,4},{12,8},{1,13},{5,1},{9,5},{13,9},{2,14},{6,2},{... | collective-permute-start | bytes 294920 | tf_op jit(solution)/shard_map/ppermute | solution.py:70
  94.3 6.6 %collective-permute-start.12 = (bf16[32,1536]{1,0:T(8,128)(2,1)S(1)}, bf16[32,1536]{1,0:T(8,128)(2,1)S(1)}, u32[]{:S(2)}, u32[]{:S(2)}) collective-permute-start(bf16[32,1536]{1,0:T(8,128)(2,1)S(1)} %get-tuple-element.58), channel_id=1, source_target_pairs={{0,8},{4,12},{8,0},{12,4},{1,9},{5,13},{9,1},{13,5},{2,10},{6,14},... | collective-permute-start | bytes 294920 | tf_op jit(solution)/shard_map/ppermute | solution.py:70
  94.3 6.6 %collective-permute-start.13 = (bf16[32,1536]{1,0:T(8,128)(2,1)S(1)}, bf16[32,1536]{1,0:T(8,128)(2,1)S(1)}, u32[]{:S(2)}, u32[]{:S(2)}) collective-permute-start(bf16[32,1536]{1,0:T(8,128)(2,1)S(1)} %get-tuple-element.56), channel_id=1, source_target_pairs={{0,4},{4,8},{8,12},{12,0},{1,5},{5,9},{9,13},{13,1},{2,6},{6,10},{... | collective-permute-start | bytes 294920 | tf_op jit(solution)/shard_map/ppermute | solution.py:70
  (4 other events, 36.9 us)

commit v2 on v0

v2 whole, which is shorter than its diff:
```python
import functools

import jax
import jax.numpy as jnp
from jax import lax
from jax.experimental import pallas as pl
from jax.experimental.pallas import tpu as pltpu
from jax.sharding import PartitionSpec as P

outer_rate = 0.7
beta_outer = 0.9
F32 = jnp.float32
BF16 = jnp.bfloat16
units = 32
chunk_units = ((0, 9), (9, 11), (20, 9), (29, 3))


def nesterov(frag_sum, outer, momentum, islands):
    average = outer - frag_sum / islands
    new_momentum = beta_outer * momentum + average
    return outer - outer_rate * (average + beta_outer * new_momentum), new_momentum


def unwritten(like):
    return pl.pallas_call(
        lambda *_: None,
        out_specs=[pl.BlockSpec(memory_space=pltpu.HBM)] * 2,
        out_shape=[jax.ShapeDtypeStruct(like.shape, like.dtype)] * 2,
        cost_estimate=pl.CostEstimate(flops=0, bytes_accessed=0, transcendentals=0),
    )()


def update(k, theirs, local_frag, outer_frag, momentum, done):
    ours, outer, held = (a.reshape(-1, a.shape[-1]) for a in (local_frag, outer_frag, momentum))
    if done is None:
        done = unwritten(outer)
    first = chunk_units[k][0] * (ours.shape[0] // units)
    ours, outer, held = (lax.slice_in_dim(a, first, first + theirs.shape[0]) for a in (ours, outer, held))
    results = nesterov(ours.astype(F32) + theirs.astype(F32), outer, held, lax.axis_size("island"))
    return [lax.dynamic_update_slice(whole, part, (first, 0)) for whole, part in zip(done, results)]


def piece_kernel(firsts, ours, *refs):
    pieces, buffers, loads, stores = refs[: len(firsts)], refs[len(firsts) : -2], refs[-2], refs[-1]
    inward = [
        pltpu.make_async_copy(ours.at[pl.ds(first, piece.shape[0])], buffer, loads.at[k])
        for k, (first, piece, buffer) in enumerate(zip(firsts, pieces, buffers))
    ]
    outward = [pltpu.make_async_copy(buffer, piece, stores.at[k]) for k, (piece, buffer) in enumerate(zip(pieces, buffers))]
    for copy in inward:
        copy.start()
    for load, store in zip(inward, outward):
        load.wait()
        store.start()
    for copy in outward:
        copy.wait()


def pieces_of(local_frag, members):
    ours = local_frag.reshape(-1, local_frag.shape[-1])
    unit, cols = ours.shape[0] // units, ours.shape[1]
    firsts = [chunk_units[k][0] * unit for k in members]
    shapes = [(chunk_units[k][1] * unit, cols) for k in members]
    return pl.pallas_call(
        functools.partial(piece_kernel, firsts),
        in_specs=[pl.BlockSpec(memory_space=pltpu.HBM)],
        out_specs=[pl.BlockSpec(memory_space=pltpu.HBM)] * len(members),
        out_shape=[jax.ShapeDtypeStruct(s, BF16) for s in shapes],
        scratch_shapes=[pltpu.VMEM(s, BF16) for s in shapes] + [pltpu.SemaphoreType.DMA((len(members),))] * 2,
        compiler_params=pltpu.CompilerParams(vmem_limit_bytes=16 * 1024 * 1024),
        cost_estimate=pl.CostEstimate(flops=0, bytes_accessed=0, transcendentals=0),
    )(ours)


def swapped(piece):
    return lax.ppermute(piece, "island", [(0, 1), (1, 0)])


def together(f, *operands):
    shapes = jax.eval_shape(f, *operands)
    return lax.cond(
        lax.axis_index("fsdp") >= 0, f, lambda *_: jax.tree.map(lambda s: jnp.zeros(s.shape, s.dtype), shapes), *operands
    )


def shifted(x, axis, step):
    n = lax.axis_size(axis)
    return lax.ppermute(x, axis, [(i, (i + step) % n) for i in range(n)])


def paired(x, axis, bit):
    return lax.ppermute(x, axis, [(i, i ^ bit) for i in range(lax.axis_size(axis))])


def leaving_at(axis, bit):
    return [lax.axis_index(axis) ^ k for k in range(bit, lax.axis_size(axis), 2 * bit)]


def input_terms(cots, weight):
    share = cots.shape[1] // lax.axis_size("tensor")

    def part_of(members):
        rows_of = jnp.concatenate([lax.dynamic_slice_in_dim(cots, m * share, share, 1) for m in members])
        return lax.dot_general(
            rows_of.reshape(-1, cots.shape[2]), weight, (((1,), (1,)), ((), ())), preferred_element_type=F32
        )

    return part_of


def sum_scatter(part, part_of, axis):
    n = lax.axis_size(axis)
    received = {k: [] for k in range(n)}
    bit = 1
    while bit < n:
        leaving = list(range(bit, n, 2 * bit))
        if bit > 1:
            part = part_of(leaving_at(axis, bit))
            for terms in zip(*(received[k] for k in leaving)):
                part = part + jnp.concatenate([t.astype(F32) for t in terms])
        came = paired(part.astype(BF16), axis, bit)
        for slot, block in zip(leaving, jnp.split(came, len(leaving))):
            received[slot ^ bit].append(block)
        bit *= 2
    return part_of([lax.axis_index(axis)]) + sum(t.astype(F32) for t in received[0])


def keys_kernel(place, own, *refs):
    peers = (len(refs) - 3) // 3
    mine, other = refs[:peers], refs[peers : 2 * peers]
    weight, summed, keys_own, *packets = refs[2 * peers :]
    core = place[1]
    half, cols = own.shape[0] // 2, weight.shape[1]
    share = summed.shape[0] // (peers + 1)
    keys_own[...] = jnp.dot(own[...], weight[...], preferred_element_type=F32)
    for blocks, at in ((mine, core), (other, 1 - core)):
        for block, packet in zip(blocks, packets):
            part = jnp.dot(block[...], weight[...], preferred_element_type=F32)
            packet[pl.ds(pl.multiple_of(at * half, half), half), :] = part.astype(BF16)
    for s, packet in enumerate(packets, 1):
        for j in range(summed.shape[1] // cols):
            top = 2 * half + j * share
            packet[top : top + share, :] = summed[s * share : (s + 1) * share, j * cols : (j + 1) * cols]


def finish_kernel(place, keys_own, summed, *refs):
    packets, (keys, input_grad) = refs[:-2], refs[-2:]
    shards = len(packets) + 1
    rows, cols = keys.shape
    share, width = input_grad.shape[0], summed.shape[1]
    total = keys_own[...]
    for packet in packets:
        total = total + packet[:rows, :].astype(F32)
    keys[...] = total.astype(BF16)
    input_grad[:, pl.ds(pl.multiple_of(place[0] * width, width), width)] = summed[:share, :]
    for s, packet in enumerate(packets, 1):
        origin = lax.rem(place[0] + s, shards) * width
        for j in range(width // cols):
            top = rows + j * share
            input_grad[:, pl.ds(pl.multiple_of(origin + j * cols, cols), cols)] = packet[top : top + share, :]


def weight_grad_kernel(place, own, *refs):
    peers = (len(refs) - 2) // 2
    mine, other, (cots, weight_grad) = refs[:peers], refs[peers : 2 * peers], refs[2 * peers :]
    core = place[1]
    half = own.shape[0] // 2
    tokens, rows = [own[...]], [cots[0]]
    for blocks, at in ((mine, core), (other, 1 - core)):
        for s, block in enumerate(blocks, 1):
            tokens.append(block[...])
            rows.append(cots[s, pl.ds(pl.multiple_of(at * half, half), half), :])
    total = lax.dot_general(
        jnp.concatenate(tokens), jnp.concatenate(rows), (((0,), (0,)), ((), ())), preferred_element_type=F32
    )
    weight_grad[...] = total.astype(BF16)


def local_call(kernel, out_shape, place, tokens, *operands, flops=0):
    whole = pl.BlockSpec(memory_space=pltpu.VMEM)
    first = [] if tokens is None else [tokens]
    width = first[0].shape[1] // lax.axis_size("fsdp") if first else 0
    columns = [pl.BlockSpec((a.shape[0], width), lambda i, place: (0, place[0])) for a in first]
    return pl.pallas_call(
        kernel,
        grid_spec=pltpu.PrefetchScalarGridSpec(
            num_scalar_prefetch=1, grid=(1,), in_specs=columns + [whole] * len(operands), out_specs=[whole] * len(out_shape)
        ),
        out_shape=out_shape,
        compiler_params=pltpu.CompilerParams(vmem_limit_bytes=32 * 1024 * 1024),
        cost_estimate=pl.CostEstimate(flops=flops, bytes_accessed=0, transcendentals=0),
    )(place, *first, *operands)


def place_of():
    return lax.axis_index("fsdp"), lax.rem(lax.axis_index("tensor"), 2)


def gather(tokens, weight, cotangent):
    me, core = place_of()
    shards = lax.axis_size("fsdp")
    width, half = weight.shape[0], tokens.shape[0] // 2
    leaving = [
        lax.dynamic_slice(tokens, (core * half, lax.rem(me + s, shards) * width), (half, width)) for s in range(1, shards)
    ]
    cots = [cotangent] + [shifted(cotangent, "fsdp", s) for s in range(1, shards)]
    mine = shifted(leaving[0], "fsdp", 1)
    mine, cots = lax.optimization_barrier((mine, cots))
    cots = jnp.stack(cots)
    return cots, input_terms(cots, weight)(leaving_at("tensor", 1)).astype(BF16), mine, leaving[1:]


def combine(cots, part, mine, leaving, tokens, weight):
    place = jnp.stack(place_of()).astype(jnp.int32)
    shards, heads = lax.axis_size("fsdp"), lax.axis_size("tensor")
    width, cols = weight.shape
    rows = tokens.shape[0]
    share = rows // heads

    mine = [mine] + [shifted(block, "fsdp", s) for s, block in enumerate(leaving, 2)]
    other = [paired(block, "tensor", 1) for block in mine]
    summed = sum_scatter(part, input_terms(cots, weight), "tensor").astype(BF16)
    packet = jax.ShapeDtypeStruct((rows + share * width // cols, cols), BF16)
    keys_own, *packets = local_call(
        keys_kernel,
        [jax.ShapeDtypeStruct((rows, cols), F32)] + [packet] * (shards - 1),
        place, tokens, *mine, *other, weight, summed,
    )
    return (cots, mine, other), (keys_own, summed), packets


def finish(gathered, own, packets, tokens, weight):
    place = jnp.stack(place_of()).astype(jnp.int32)
    cots, mine, other = gathered
    keys_own, summed = own
    shards, rows, cols = cots.shape
    packets = [shifted(p, "fsdp", -s) for s, p in enumerate(packets, 1)]
    (weight_grad,) = local_call(
        weight_grad_kernel, [jax.ShapeDtypeStruct(weight.shape, BF16)], place, tokens, *mine, *other, cots
    )
    keys, input_grad = local_call(
        finish_kernel,
        [jax.ShapeDtypeStruct((rows, cols), BF16), jax.ShapeDtypeStruct((summed.shape[0] // shards, tokens.shape[1]), BF16)],
        place, None, keys_own, summed, *packets,
    )
    return keys, input_grad, weight_grad


def body(tokens, key_weight, key_cotangent, local_frag, outer_frag, momentum):
    weight = key_weight[0]
    islands = lax.axis_size("island")
    if islands != 2:
        state = combine(*gather(tokens, weight, key_cotangent), tokens, weight)
        keys, input_grad, weight_grad = finish(*state, tokens, weight)
        frag_sum = lax.psum(local_frag[0], "island").astype(F32)
        new_outer, new_momentum = nesterov(frag_sum, outer_frag, momentum, islands)
        return (keys, input_grad, weight_grad[None], new_outer, new_momentum)

    frag = (local_frag, outer_frag, momentum)
    theirs = [swapped(*pieces_of(local_frag, [0]))]

    def step_one(tokens, weight, key_cotangent, local_frag):
        return gather(tokens, weight, key_cotangent), pieces_of(local_frag, [1])

    state, (piece,) = together(step_one, tokens, weight, key_cotangent, local_frag)
    theirs.append(swapped(piece))
    theirs[0], state = lax.optimization_barrier((theirs[0], state))

    def step_two(theirs, state, tokens, weight, *frag):
        pieces = pieces_of(frag[0], range(2, len(chunk_units)))
        return combine(*state, tokens, weight), pieces, update(0, theirs, *frag, None)

    state, pieces, done = together(step_two, theirs[0], state, tokens, weight, *frag)
    theirs.append(swapped(pieces[0]))
    theirs[1], state, done = lax.optimization_barrier((theirs[1], state, done))

    def step_three(theirs, state, done, tokens, weight, *frag):
        return finish(*state, tokens, weight), update(1, theirs, *frag, done)

    (keys, input_grad, weight_grad), done = together(step_three, theirs[1], state, done, tokens, weight, *frag)
    theirs += [swapped(piece) for piece in pieces[1:]]
    for k in range(2, len(theirs)):
        theirs[k], done = lax.optimization_barrier((theirs[k], done))
        done = update(k, theirs[k], *frag, done)
    new_outer, new_momentum = (a.reshape(outer_frag.shape) for a in done)
    return (keys, input_grad, weight_grad[None], new_outer, new_momentum)


def solution(mesh):
    return jax.shard_map(
        body,
        mesh=mesh,
        in_specs=(
            P(("island", "fsdp"), None),
            P("island", "fsdp", "tensor"),
            P(("island", "fsdp"), "tensor"),
            P("island", None, "fsdp", "tensor"),
            P(None, "fsdp", "tensor"),
            P(None, "fsdp", "tensor"),
        ),
        out_specs=(
            P(("island", "fsdp"), "tensor"),
            P(("island", "fsdp", "tensor"), None),
            P("island", "fsdp", "tensor"),
            P(None, "fsdp", "tensor"),
            P(None, "fsdp", "tensor"),
        ),
        check_vma=False,
    )
```

time: 177 us -> 80.9 us (0.46)
  waiting for transfers between devices: 144 us -> 12.9 us
  starting transfers between devices: 0.16 us -> 23 us
  Pallas kernels: 0 us -> 14.6 us
  between operations: 15.2 us -> 0.67 us
  other arithmetic: 9.84 us -> 21.4 us
  matrix products: 8.13 us -> 3.2 us
  local copies, waits for them, and re-layouts: 0.04 us -> 4.65 us
    all_gather x1 -> x0, waiting for transfers between devices: 64.5 us -> none  [body(): gathered = lax.all_gather(own_shard, 'fsdp', axis=0, tiled=True)]
    reduce_scatter x2 -> x0, waiting for transfers between devices: 58.8 us -> none  [the longest x1 31.4 us: body(): lax.psum_scatter(lax.dot_general(key_cotangent, gathered, (((1,), (1,)),...]
    ppermute x0 -> x18, starting transfers between devices: none -> 23 us  [the longest x9 15.3 us: shifted(): return lax.ppermute(x, axis, [(i, (i + step) % n) for i in range(n)])]
    psum x1 -> x0, waiting for transfers between devices: 19 us -> none  [body(): lax.psum(own_frag, 'island').astype(jnp.float32) / islands]
    dynamic_update_slice x0 -> x4, other arithmetic: none -> 18.5 us  [update(): lax.dynamic_update_slice(whole, part, (first, 0))]
    pallas_call x0 -> x7, Pallas kernels: none -> 14.6 us  [the longest x3 9.54 us: local_call(): pl.pallas_call(kernel, grid_spec=pltpu.PrefetchScalarGridSpec(num_scalar_...]
    ppermute x0 -> x18, waiting for transfers between devices: none -> 12.9 us  [the longest x9 8.71 us: shifted(): return lax.ppermute(x, axis, [(i, (i + step) % n) for i in range(n)])]
    sub x1 -> x0, other arithmetic: 9.84 us -> none  [body(): new_outer = outer_frag - outer_rate * (average + beta_outer * new_momentum)]
  transfers between devices with their start and end apart: 4 -> 18, of which waited for: 4 -> 6; matrix products, arithmetic and copies ran while one was open for 10% -> 33% of each run, Pallas kernels for 0% -> 16%
where the time goes in v2:
time: 80.9 us; the launch traced here: 80.4 us
  starting transfers between devices  23 us (28%)
  other arithmetic  21.4 us (26%)
  Pallas kernels  14.6 us (18%)
  waiting for transfers between devices  12.9 us (16%)
  local copies, waits for them, and re-layouts  4.65 us (6%)
  matrix products  3.2 us (4%)
    dynamic_update_slice x4, other arithmetic, update(): lax.dynamic_update_slice(whole, part, (first, 0))  18.5 us
    ppermute x9, starting transfers between devices, shifted(): return lax.ppermute(x, axis, [(i, (i + step) % n) for i in range(n)])  15.3 us
    pallas_call x3, Pallas kernels, local_call(): pl.pallas_call(kernel, grid_spec=pltpu.PrefetchScalarGridSpec(num_scalar_...  9.54 us
    ppermute x9, waiting for transfers between devices, shifted(): return lax.ppermute(x, axis, [(i, (i + step) % n) for i in range(n)])  8.71 us
    ppermute x4, starting transfers between devices, swapped(): return lax.ppermute(piece, 'island', [(0, 1), (1, 0)])  5.63 us
    pallas_call x3, Pallas kernels, pieces_of(): pl.pallas_call(functools.partial(piece_kernel, firsts), in_specs=[pl.Bloc...  5.02 us
    ppermute x4, waiting for transfers between devices, swapped(): return lax.ppermute(piece, 'island', [(0, 1), (1, 0)])  3.6 us
    dot_general x3, matrix products, part_of(): lax.dot_general(rows_of.reshape(-1, cots.shape[2]), weight, (((1,), (1,))...  3.2 us
  transfers between devices with their start and end apart: 18, of which 6 were waited for; matrix products, arithmetic and copies ran while one was open for 33% of the time, Pallas kernels for 16%

profile of v2, /device:TPU:0, one launch (start us, length us, event | category | flops | bytes accessed | tf_op | source)
XLA Modules:
  0.0 80.4 jit_solution(12216457320652271501)
XLA Ops:
  2.1 3.0 %collective-permute-start.15 = (bf16[864,512]{1,0:T(8,128)(2,1)S(1)}, bf16[864,512]{1,0:T(8,128)(2,1)S(1)}, u32[]{:S(2)}, u32[]{:S(2)}) collective-permute-start(bf16[864,512]{1,0:T(8,128)(2,1)S(1)} %shard_map.102), channel_id=1, source_target_pairs={{0,16},{16,0},{1,17},{17,1},{2,18},{18,2},{3,19},{19,3},{4,20},{20... | collective-permute-start | bytes 2654216 | tf_op jit(solution)/shard_map/ppermute | solution.py:76
  5.1 17.8 %conditional.3 = (bf16[4,128,256]{2,1,0:T(8,128)(2,1)}, bf16[256,1536]{1,0:T(8,128)(2,1)S(1)}, bf16[64,1536]{1,0:T(8,128)(2,1)}, bf16[64,1536]{1,0:T(8,128)(2,1)...) conditional(s32[]{:T(128)} %convert_element_type.47, () %tuple.40, (bf16[128,6144]{1,0:T(8,128)(2,1)}, ...), branch_computations={%region_0.0_spmd, %region_1.0_spmd} | conditional | flops 202178576 | bytes 5505896 | solution.py:81
  5.1 1.9 %fusion.8 = (bf16[64,1536]{1,0:T(8,128)(2,1)}, bf16[64,1536]{1,0:T(8,128)(2,1)}, bf16[64,1536]{1,0:T(8,128)(2,1)S(1)}) fusion(bf16[128,6144]{1,0:T(8,128)(2,1)} %get-tuple-element.69, s32[]{:T(128)S(6)} %select_n.16, s32[]{:T(128)S(6)} %select_n.23, s32[]{:T(128)S(6)} %select_n.22, s32[]{:T(128)S(6)} %select_n.17), kind=kLoop, calls=%fused_computation.31 | loop fusion | bytes 1179664 | tf_op jit(solution)/shard_map/cond/branch_1_fun/dynamic_slice | solution.py:204
  7.1 1.6 %collective-permute-start.3 = (bf16[64,1536]{1,0:T(8,128)(2,1)S(1)}, bf16[64,1536]{1,0:T(8,128)(2,1)}, u32[]{:S(2)}, u32[]{:S(2)}) collective-permute-start(bf16[64,1536]{1,0:T(8,128)(2,1)S(1)} %get-tuple-element.235), channel_id=1, source_target_pairs={{0,4},{4,8},{8,12},{12,0},{1,5},{5,9},{9,13},{13,1},{2,6},{6,10},{... | collective-permute-start | bytes 589832 | tf_op jit(solution)/shard_map/cond/branch_1_fun/ppermute | solution.py:88
  8.6 2.2 %collective-permute-start.6 = (bf16[128,256]{1,0:T(8,128)(2,1)S(1)}, bf16[128,256]{1,0:T(8,128)(2,1)S(1)}, u32[]{:S(2)}, u32[]{:S(2)}) collective-permute-start(bf16[128,256]{1,0:T(8,128)(2,1)S(1)} %get-tuple-element.71), channel_id=1, source_target_pairs={{0,12},{4,0},{8,4},{12,8},{1,13},{5,1},{9,5},{13,9},{2,14},{6,2},{... | collective-permute-start | bytes 196616 | tf_op jit(solution)/shard_map/cond/branch_1_fun/ppermute | solution.py:88
  11.7 1.6 %collective-permute-start.4 = (bf16[128,256]{1,0:T(8,128)(2,1)S(1)}, bf16[128,256]{1,0:T(8,128)(2,1)S(1)}, u32[]{:S(2)}, u32[]{:S(2)}) collective-permute-start(bf16[128,256]{1,0:T(8,128)(2,1)S(1)} %get-tuple-element.71), channel_id=1, source_target_pairs={{0,4},{4,8},{8,12},{12,0},{1,5},{5,9},{9,13},{13,1},{2,6},{6,10},{... | collective-permute-start | bytes 196616 | tf_op jit(solution)/shard_map/cond/branch_1_fun/ppermute | solution.py:88
  13.2 2.3 %branch_1_fun.6 = bf16[1056,512]{1,0:T(8,128)(2,1)} custom-call(bf16[3072,512]{1,0:T(8,128)(2,1)} %bitcast.34), custom_call_target="tpu_custom_call" | custom-call | tf_op jit(solution)/shard_map/cond/branch_1_fun/pallas_call | solution.py:64
  15.5 5.4 %collective-permute-done.5 = bf16[128,256]{1,0:T(8,128)(2,1)S(1)} collective-permute-done((bf16[128,256]{1,0:T(8,128)(2,1)S(1)}, bf16[128,256]{1,0:T(8,128)(2,1)S(1)}, u32[]{:S(2)}, u32[]{:S(2)}) %collective-permute-start.5) | collective-permute-done | bytes 65568 | tf_op jit(solution)/shard_map/cond/branch_1_fun/ppermute | solution.py:88
  24.8 25.1 %conditional.4 = (bf16[4,128,256]{2,1,0:T(8,128)(2,1)}, bf16[64,1536]{1,0:T(8,128)(2,1)S(1)}, bf16[64,1536]{1,0:T(8,128)(2,1)}, bf16[64,1536]{1,0:T(8,128)(2,1)}...) conditional(s32[]{:T(128)} %convert_element_type.47, () %tuple.42, ...), branch_computations={%region_2.0_spmd, %region_3.0_spmd} | conditional | flops 207765536 | bytes 55247664 | solution.py:81
  24.8 4.0 %collective-permute-start.7 = (bf16[64,1536]{1,0:T(8,128)(2,1)}, bf16[64,1536]{1,0:T(8,128)(2,1)}, u32[]{:S(2)}, u32[]{:S(2)}) collective-permute-start(bf16[64,1536]{1,0:T(8,128)(2,1)} %get-tuple-element.80), channel_id=1, source_target_pairs={{0,8},{4,12},{8,0},{12,4},{1,9},{5,13},{9,1},{13,5},{2,10},{6,14},... | collective-permute-start | bytes 589832 | tf_op jit(solution)/shard_map/cond/branch_1_fun/ppermute | solution.py:88
  33.7 5.2 %fusion.1 = (f32[3072,512]{1,0:T(8,128)}, f32[3072,512]{1,0:T(8,128)}) fusion(f32[3072,512]{1,0:T(8,128)} %get-tuple-element.96, f32[3072,512]{1,0:T(8,128)} %bitcast.46, bf16[864,512]{1,0:T(8,128)(2,1)} %copy-done.6, bf16[3072,512]{1,0:T(8,128)(2,1)} %bitcast.35, f32[3072,512]{1,0:T(8,128)} %bitcast.42, f32[3072,512]{1,0:T(8,128)} %get-tuple-element.92), kind=kLoop, calls=%fused_computation.9 | loop fusion | flops 4866048 | bytes 8847360 | tf_op jit(solution)/shard_map/cond/branch_1_fun/dynamic_update_slice | solution.py:40
  41.2 1.7 %fusion.9 = f32[128,1536]{1,0:T(8,128)S(1)} fusion(bf16[128,256]{1,0:T(8,128)(2,1)S(1)} %bitcast.49, bf16[1536,256]{1,0:T(8,128)(2,1)} %copy-done.2), kind=kOutput, calls=%fused_computation.32 | convolution fusion | flops 100663296 | bytes 1638400 | tf_op jit(solution)/shard_map/cond/branch_1_fun/dot_general | solution.py:104
  44.1 2.0 %add_convert_fusion.refs_7_ = bf16[128,1536]{1,0:T(8,128)(2,1)} fusion(f32[128,1536]{1,0:T(8,128)S(1)} %fusion.9, bf16[128,1536]{1,0:T(8,128)(2,1)} %collective-permute-done.13, bf16[256,1536]{1,0:T(8,128)(2,1)} %copy-done.7), kind=kLoop, calls=%fused_computation.10 | loop fusion | flops 983040 | bytes 1966080 | tf_op jit(solution)/shard_map/cond/branch_1_fun/convert_element_type | solution.py:222
  46.1 3.8 %branch_1_fun.7 = (f32[128,256]{1,0:T(8,128)S(1)}, bf16[320,256]{1,0:T(8,128)(2,1)}, bf16[320,256]{1,0:T(8,128)(2,1)}, bf16[320,256]{1,0:T(8,128)(2,1)}) custom-call(s32[2]{0:T(128)S(1)} %pad_add_fusion.place, bf16[128,6144]{1,0:T(8,128)(2,1)S(1)} %copy-done.4, bf16[64,1536]{1,0:T(8,128)(2,1)} %get-tuple-element.277.refs_0_, ...), custom_call_target="tpu_custom_call" | custom-call | tf_op jit(solution)/shard_map/cond/branch_1_fun/pallas_call | solution.py:184
  49.9 1.5 %collective-permute-start.17 = (bf16[864,512]{1,0:T(8,128)(2,1)}, bf16[864,512]{1,0:T(8,128)(2,1)S(1)}, u32[]{:S(2)}, u32[]{:S(2)}) collective-permute-start(bf16[864,512]{1,0:T(8,128)(2,1)} %get-tuple-element.222), channel_id=1, source_target_pairs={{0,16},{16,0},{1,17},{17,1},{2,18},{18,2},{3,19},{19,3},{4,20},{20... | collective-permute-start | bytes 2654216 | tf_op jit(solution)/shard_map/ppermute | solution.py:76
  51.9 18.8 %conditional.5 = (bf16[128,256]{1,0:T(8,128)(2,1)S(1)}, bf16[32,6144]{1,0:T(8,128)(2,1)}, f32[3072,512]{1,0:T(8,128)}, f32[3072,512]{1,0:T(8,128)}, bf16[1,1536,256]{2,1,0:T(8,128)(2,1)}) conditional(s32[]{:T(128)} %convert_element_type.47, () %tuple.39, (bf16[320,256]{1,0:T(8,128)(2,1)}, bf16[320,256]{1,0:T(8,128)(2,1)}, bf16[320,256]{1,0:T(8,128)(2,1)}, ...), branch_computations={%region_4.0_spmd, %region_5.0_spmd} | conditional | flops 5947405 | bytes 19071296 | solution.py:81
  51.9 3.1 %collective-permute-start = (bf16[320,256]{1,0:T(8,128)(2,1)}, bf16[320,256]{1,0:T(8,128)(2,1)S(1)}, u32[]{:S(2)}, u32[]{:S(2)}) collective-permute-start(bf16[320,256]{1,0:T(8,128)(2,1)} %get-tuple-element.99), channel_id=1, source_target_pairs={{0,12},{4,0},{8,4},{12,8},{1,13},{5,1},{9,5},{13,9},{2,14},{6,2},{... | collective-permute-start | bytes 491528 | tf_op jit(solution)/shard_map/cond/branch_1_fun/ppermute | solution.py:88
  55.6 5.9 %fusion.3 = (f32[3072,512]{1,0:T(8,128)}, f32[3072,512]{1,0:T(8,128)}) fusion(f32[3072,512]{1,0:T(8,128)} %get-tuple-element.109, f32[3072,512]{1,0:T(8,128)} %bitcast.47, bf16[1056,512]{1,0:T(8,128)(2,1)} %get-tuple-element.107, bf16[3072,512]{1,0:T(8,128)(2,1)} %bitcast.37, f32[3072,512]{1,0:T(8,128)} %bitcast.43, f32[3072,512]{1,0:T(8,128)} %get-tuple-element.104), kind=kLoop, calls=%fused_computation.19 | loop fusion | flops 5947392 | bytes 10813440 | tf_op jit(solution)/shard_map/cond/branch_1_fun/dynamic_update_slice | solution.py:40
  61.6 3.4 %branch_1_fun.11 = bf16[1536,256]{1,0:T(8,128)(2,1)} custom-call(s32[2]{0:T(128)S(1)} %pad_add_fusion.1.place, bf16[128,6144]{1,0:T(8,128)(2,1)S(1)} %copy-done.5, bf16[64,1536]{1,0:T(8,128)(2,1)S(1)} %get-tuple-element.111.refs_0_, bf16[64,1536]{1,0:T(8,128)(2,1)} %get-tuple-element.112.refs_1_, bf16[64,1536]{1,0:T(8,128)(2,1)} %get-tuple-element.113.refs_2_, ...), custom_call_target="tpu_custom_call" | custom-call | tf_op jit(solution)/shard_map/cond/branch_1_fun/pallas_call | solution.py:184
  65.0 3.3 %collective-permute-done.1.refs_1_ = bf16[320,256]{1,0:T(8,128)(2,1)S(1)} collective-permute-done((bf16[320,256]{1,0:T(8,128)(2,1)}, bf16[320,256]{1,0:T(8,128)(2,1)S(1)}, u32[]{:S(2)}, u32[]{:S(2)}) %collective-permute-start.1) | collective-permute-done | bytes 163872 | tf_op jit(solution)/shard_map/cond/branch_1_fun/ppermute | solution.py:88
  68.4 2.3 %branch_1_fun.10 = (bf16[128,256]{1,0:T(8,128)(2,1)S(1)}, bf16[32,6144]{1,0:T(8,128)(2,1)}) custom-call(s32[2]{0:T(128)S(1)} %pad_add_fusion.1.place, f32[128,256]{1,0:T(8,128)S(1)} %get-tuple-element.97.keys_own, bf16[128,1536]{1,0:T(8,128)(2,1)} %get-tuple-element.98.summed, bf16[320,256]{1,0:T(8,128)(2,1)S(1)} %collective-permute-done.refs_0_, ...), custom_call_target="tpu_custom_call" | custom-call | tf_op jit(solution)/shard_map/cond/branch_1_fun/pallas_call | solution.py:184
  70.7 1.9 %collective-permute-done.17 = bf16[864,512]{1,0:T(8,128)(2,1)S(1)} collective-permute-done((bf16[864,512]{1,0:T(8,128)(2,1)}, bf16[864,512]{1,0:T(8,128)(2,1)S(1)}, u32[]{:S(2)}, u32[]{:S(2)}) %collective-permute-start.17) | collective-permute-done | bytes 884768 | tf_op jit(solution)/shard_map/ppermute | solution.py:76
  72.6 4.7 %fusion.5 = (f32[3072,512]{1,0:T(8,128)}, f32[3072,512]{1,0:T(8,128)}) fusion(f32[3072,512]{1,0:T(8,128)} %get-tuple-element.227, f32[3072,512]{1,0:T(8,128)} %bitcast.44, bf16[864,512]{1,0:T(8,128)(2,1)S(1)} %collective-permute-done.17, bf16[3072,512]{1,0:T(8,128)(2,1)} %bitcast.32, f32[3072,512]{1,0:T(8,128)} %bitcast.40, f32[3072,512]{1,0:T(8,128)} %get-tuple-element.225), kind=kLoop, calls=%fused_computation.25 | loop fusion | flops 4866048 | bytes 8847360 | tf_op jit(solution)/shard_map/dynamic_update_slice | solution.py:40
  77.8 2.7 %fusion.7 = (f32[3072,512]{1,0:T(8,128)}, f32[3072,512]{1,0:T(8,128)}) fusion(f32[3072,512]{1,0:T(8,128)} %get-tuple-element.230, f32[3072,512]{1,0:T(8,128)} %bitcast.45, bf16[288,512]{1,0:T(8,128)(2,1)} %collective-permute-done.16, bf16[3072,512]{1,0:T(8,128)(2,1)} %bitcast.33, f32[3072,512]{1,0:T(8,128)} %bitcast.41, f32[3072,512]{1,0:T(8,128)} %get-tuple-element.228), kind=kLoop, calls=%fused_computation.30 | loop fusion | flops 1622016 | bytes 2949120 | tf_op jit(solution)/shard_map/dynamic_update_slice | solution.py:40
  (58 shorter events, 16.1 us)
Async XLA Ops:
  2.1 22.7 %collective-permute-start.15 = (bf16[864,512]{1,0:T(8,128)(2,1)S(1)}, bf16[864,512]{1,0:T(8,128)(2,1)S(1)}, u32[]{:S(2)}, u32[]{:S(2)}) collective-permute-start(bf16[864,512]{1,0:T(8,128)(2,1)S(1)} %shard_map.102), channel_id=1, source_target_pairs={{0,16},{16,0},{1,17},{17,1},{2,18},{18,2},{3,19},{19,3},{4,20},{20... | collective-permute-start | bytes 2654216 | tf_op jit(solution)/shard_map/ppermute | solution.py:76
  7.1 13.8 %collective-permute-start.3 = (bf16[64,1536]{1,0:T(8,128)(2,1)S(1)}, bf16[64,1536]{1,0:T(8,128)(2,1)}, u32[]{:S(2)}, u32[]{:S(2)}) collective-permute-start(bf16[64,1536]{1,0:T(8,128)(2,1)S(1)} %get-tuple-element.235), channel_id=1, source_target_pairs={{0,4},{4,8},{8,12},{12,0},{1,5},{5,9},{9,13},{13,1},{2,6},{6,10},{... | collective-permute-start | bytes 589832 | tf_op jit(solution)/shard_map/cond/branch_1_fun/ppermute | solution.py:88
  8.6 6.9 %collective-permute-start.6 = (bf16[128,256]{1,0:T(8,128)(2,1)S(1)}, bf16[128,256]{1,0:T(8,128)(2,1)S(1)}, u32[]{:S(2)}, u32[]{:S(2)}) collective-permute-start(bf16[128,256]{1,0:T(8,128)(2,1)S(1)} %get-tuple-element.71), channel_id=1, source_target_pairs={{0,12},{4,0},{8,4},{12,8},{1,13},{5,1},{9,5},{13,9},{2,14},{6,2},{... | collective-permute-start | bytes 196616 | tf_op jit(solution)/shard_map/cond/branch_1_fun/ppermute | solution.py:88
  10.9 10.0 %collective-permute-start.5 = (bf16[128,256]{1,0:T(8,128)(2,1)S(1)}, bf16[128,256]{1,0:T(8,128)(2,1)S(1)}, u32[]{:S(2)}, u32[]{:S(2)}) collective-permute-start(bf16[128,256]{1,0:T(8,128)(2,1)S(1)} %get-tuple-element.71), channel_id=1, source_target_pairs={{0,8},{4,12},{8,0},{12,4},{1,9},{5,13},{9,1},{13,5},{2,10},{6,14},... | collective-permute-start | bytes 196616 | tf_op jit(solution)/shard_map/cond/branch_1_fun/ppermute | solution.py:88
  11.7 9.2 %collective-permute-start.4 = (bf16[128,256]{1,0:T(8,128)(2,1)S(1)}, bf16[128,256]{1,0:T(8,128)(2,1)S(1)}, u32[]{:S(2)}, u32[]{:S(2)}) collective-permute-start(bf16[128,256]{1,0:T(8,128)(2,1)S(1)} %get-tuple-element.71), channel_id=1, source_target_pairs={{0,4},{4,8},{8,12},{12,0},{1,5},{5,9},{9,13},{13,1},{2,6},{6,10},{... | collective-permute-start | bytes 196616 | tf_op jit(solution)/shard_map/cond/branch_1_fun/ppermute | solution.py:88
  23.0 28.9 %collective-permute-start.14 = (bf16[1056,512]{1,0:T(8,128)(2,1)}, bf16[1056,512]{1,0:T(8,128)(2,1)}, u32[]{:S(2)}, u32[]{:S(2)}) collective-permute-start(bf16[1056,512]{1,0:T(8,128)(2,1)} %get-tuple-element.177), channel_id=1, source_target_pairs={{0,16},{16,0},{1,17},{17,1},{2,18},{18,2},{3,19},{19,3},{4,20},{20... | collective-permute-start | bytes 3244040 | tf_op jit(solution)/shard_map/ppermute | solution.py:76
  24.8 8.9 %copy-start.2 = (bf16[1536,256]{1,0:T(8,128)(2,1)}, bf16[1536,256]{1,0:T(8,128)(2,1)S(1)}, u32[]{:S(2)}) copy-start(bf16[1536,256]{1,0:T(8,128)(2,1)S(1)} %get-tuple-element.83.refs_6_) | copy-start | bytes 2359300 | tf_op jit(solution)/shard_map/cond
  24.8 8.9 %copy-start.6 = (bf16[864,512]{1,0:T(8,128)(2,1)}, bf16[864,512]{1,0:T(8,128)(2,1)S(1)}, u32[]{:S(2)}) copy-start(bf16[864,512]{1,0:T(8,128)(2,1)S(1)} %get-tuple-element.94) | copy-start | bytes 2654212 | tf_op jit(solution)/shard_map/cond
  24.8 6.3 %collective-permute-start.12 = (bf16[256,1536]{1,0:T(8,128)(2,1)S(1)}, bf16[256,1536]{1,0:T(8,128)(2,1)S(1)}, u32[]{:S(2)}, u32[]{:S(2)}) collective-permute-start(bf16[256,1536]{1,0:T(8,128)(2,1)S(1)} %get-tuple-element.84), channel_id=1, source_target_pairs={{0,1},{1,0},{2,3},{3,2},{4,5},{5,4},{6,7},{7,6},{8,9},{9,8},{10,11... | collective-permute-start | bytes 2359304 | tf_op jit(solution)/shard_map/cond/branch_1_fun/ppermute | solution.py:92
  24.8 18.1 %collective-permute-start.7 = (bf16[64,1536]{1,0:T(8,128)(2,1)}, bf16[64,1536]{1,0:T(8,128)(2,1)}, u32[]{:S(2)}, u32[]{:S(2)}) collective-permute-start(bf16[64,1536]{1,0:T(8,128)(2,1)} %get-tuple-element.80), channel_id=1, source_target_pairs={{0,8},{4,12},{8,0},{12,4},{1,9},{5,13},{9,1},{13,5},{2,10},{6,14},... | collective-permute-start | bytes 589832 | tf_op jit(solution)/shard_map/cond/branch_1_fun/ppermute | solution.py:88
  28.8 14.4 %collective-permute-start.8 = (bf16[64,1536]{1,0:T(8,128)(2,1)}, bf16[64,1536]{1,0:T(8,128)(2,1)}, u32[]{:S(2)}, u32[]{:S(2)}) collective-permute-start(bf16[64,1536]{1,0:T(8,128)(2,1)} %get-tuple-element.81), channel_id=1, source_target_pairs={{0,12},{4,0},{8,4},{12,8},{1,13},{5,1},{9,5},{13,9},{2,14},{6,2},{... | collective-permute-start | bytes 589832 | tf_op jit(solution)/shard_map/cond/branch_1_fun/ppermute | solution.py:88
  30.2 15.9 %collective-permute-start.9 = (bf16[64,1536]{1,0:T(8,128)(2,1)}, bf16[64,1536]{1,0:T(8,128)(2,1)}, u32[]{:S(2)}, u32[]{:S(2)}) collective-permute-start(bf16[64,1536]{1,0:T(8,128)(2,1)} %get-tuple-element.277.refs_0_), channel_id=1, source_target_pairs={{0,1},{1,0},{2,3},{3,2},{4,5},{5,4},{6,7},{7,6},{8,9},{9,8},{10,11... | collective-permute-start | bytes 589832 | tf_op jit(solution)/shard_map/cond/branch_1_fun/ppermute | solution.py:92
  32.2 11.8 %collective-permute-start.13 = (bf16[128,1536]{1,0:T(8,128)(2,1)}, bf16[128,1536]{1,0:T(8,128)(2,1)}, u32[]{:S(2)}, u32[]{:S(2)}) collective-permute-start(bf16[128,1536]{1,0:T(8,128)(2,1)} %add_convert_fusion.1), channel_id=1, source_target_pairs={{0,2},{1,3},{2,0},{3,1},{4,6},{5,7},{6,4},{7,5},{8,10},{9,11},{10,... | collective-permute-start | bytes 1179656 | tf_op jit(solution)/shard_map/cond/branch_1_fun/ppermute | solution.py:92
  33.7 6.1 %copy-start = (bf16[1,2,1536,512]{3,2,1,0:T(8,128)(2,1)S(1)}, bf16[1,2,1536,512]{3,2,1,0:T(8,128)(2,1)}, u32[]{:S(2)}) copy-start(bf16[1,2,1536,512]{3,2,1,0:T(8,128)(2,1)} %get-tuple-element.89) | copy-start | bytes 9437188 | tf_op jit(solution)/shard_map/cond
  41.1 4.9 %copy-start.3 = (bf16[1536,256]{1,0:T(8,128)(2,1)S(1)}, bf16[1536,256]{1,0:T(8,128)(2,1)}, u32[]{:S(2)}) copy-start(bf16[1536,256]{1,0:T(8,128)(2,1)} %copy-done.2) | copy-start | bytes 2359300 | tf_op jit(solution)/shard_map/cond
  42.9 3.1 %collective-permute-start.10 = (bf16[64,1536]{1,0:T(8,128)(2,1)}, bf16[64,1536]{1,0:T(8,128)(2,1)}, u32[]{:S(2)}, u32[]{:S(2)}) collective-permute-start(bf16[64,1536]{1,0:T(8,128)(2,1)} %collective-permute-done.7.refs_1_), channel_id=1, source_target_pairs={{0,1},{1,0},{2,3},{3,2},{4,5},{5,4},{6,7},{7,6},{8,9},{9,8},{10,11... | collective-permute-start | bytes 589832 | tf_op jit(solution)/shard_map/cond/branch_1_fun/ppermute | solution.py:92
  43.2 2.8 %collective-permute-start.11 = (bf16[64,1536]{1,0:T(8,128)(2,1)}, bf16[64,1536]{1,0:T(8,128)(2,1)}, u32[]{:S(2)}, u32[]{:S(2)}) collective-permute-start(bf16[64,1536]{1,0:T(8,128)(2,1)} %collective-permute-done.8.refs_2_), channel_id=1, source_target_pairs={{0,1},{1,0},{2,3},{3,2},{4,5},{5,4},{6,7},{7,6},{8,9},{9,8},{10,11... | collective-permute-start | bytes 589832 | tf_op jit(solution)/shard_map/cond/branch_1_fun/ppermute | solution.py:92
  49.9 22.8 %collective-permute-start.17 = (bf16[864,512]{1,0:T(8,128)(2,1)}, bf16[864,512]{1,0:T(8,128)(2,1)S(1)}, u32[]{:S(2)}, u32[]{:S(2)}) collective-permute-start(bf16[864,512]{1,0:T(8,128)(2,1)} %get-tuple-element.222), channel_id=1, source_target_pairs={{0,16},{16,0},{1,17},{17,1},{2,18},{18,2},{3,19},{19,3},{4,20},{20... | collective-permute-start | bytes 2654216 | tf_op jit(solution)/shard_map/ppermute | solution.py:76
  51.4 26.4 %collective-permute-start.16 = (bf16[288,512]{1,0:T(8,128)(2,1)}, bf16[288,512]{1,0:T(8,128)(2,1)}, u32[]{:S(2)}, u32[]{:S(2)}) collective-permute-start(bf16[288,512]{1,0:T(8,128)(2,1)} %get-tuple-element.221), channel_id=1, source_target_pairs={{0,16},{16,0},{1,17},{17,1},{2,18},{18,2},{3,19},{19,3},{4,20},{20... | collective-permute-start | bytes 884744 | tf_op jit(solution)/shard_map/ppermute | solution.py:76
  51.9 13.1 %collective-permute-start = (bf16[320,256]{1,0:T(8,128)(2,1)}, bf16[320,256]{1,0:T(8,128)(2,1)S(1)}, u32[]{:S(2)}, u32[]{:S(2)}) collective-permute-start(bf16[320,256]{1,0:T(8,128)(2,1)} %get-tuple-element.99), channel_id=1, source_target_pairs={{0,12},{4,0},{8,4},{12,8},{1,13},{5,1},{9,5},{13,9},{2,14},{6,2},{... | collective-permute-start | bytes 491528 | tf_op jit(solution)/shard_map/cond/branch_1_fun/ppermute | solution.py:88
  55.0 13.4 %collective-permute-start.1 = (bf16[320,256]{1,0:T(8,128)(2,1)}, bf16[320,256]{1,0:T(8,128)(2,1)S(1)}, u32[]{:S(2)}, u32[]{:S(2)}) collective-permute-start(bf16[320,256]{1,0:T(8,128)(2,1)} %get-tuple-element.100), channel_id=1, source_target_pairs={{0,8},{4,12},{8,0},{12,4},{1,9},{5,13},{9,1},{13,5},{2,10},{6,14},... | collective-permute-start | bytes 491528 | tf_op jit(solution)/shard_map/cond/branch_1_fun/ppermute | solution.py:88
  55.0 13.4 %collective-permute-start.2 = (bf16[320,256]{1,0:T(8,128)(2,1)}, bf16[320,256]{1,0:T(8,128)(2,1)S(1)}, u32[]{:S(2)}, u32[]{:S(2)}) collective-permute-start(bf16[320,256]{1,0:T(8,128)(2,1)} %get-tuple-element.101), channel_id=1, source_target_pairs={{0,4},{4,8},{8,12},{12,0},{1,5},{5,9},{9,13},{13,1},{2,6},{6,10},{... | collective-permute-start | bytes 491528 | tf_op jit(solution)/shard_map/cond/branch_1_fun/ppermute | solution.py:88
  55.6 6.0 %copy-start.5 = (bf16[128,6144]{1,0:T(8,128)(2,1)S(1)}, bf16[128,6144]{1,0:T(8,128)(2,1)}, u32[]{:S(2)}) copy-start(bf16[128,6144]{1,0:T(8,128)(2,1)} %get-tuple-element.110.own) | copy-start | bytes 4718596 | tf_op jit(solution)/shard_map/cond
  70.7 6.7 %copy-start.8 = (bf16[128,256]{1,0:T(8,128)(2,1)}, bf16[128,256]{1,0:T(8,128)(2,1)S(1)}, u32[]{:S(2)}) copy-start(bf16[128,256]{1,0:T(8,128)(2,1)S(1)} %get-tuple-element.172) | copy-start | bytes 196612
  (4 other events, 16.6 us)

commit v3 on v2

--- a/solution.py
+++ b/solution.py
@@ -12,7 +12,7 @@
 F32 = jnp.float32
 BF16 = jnp.bfloat16
 units = 32
-chunk_units = ((0, 9), (9, 11), (20, 9), (29, 3))
+chunk_units = ((0, 19, 4), (19, 10, 2), (29, 3, None))
 
 
 def nesterov(frag_sum, outer, momentum, islands):
@@ -21,32 +21,66 @@
     return outer - outer_rate * (average + beta_outer * new_momentum), new_momentum
 
 
-def unwritten(like):
+def update_kernel(islands, first, cuts, theirs, ours, outer, momentum, *refs):
+    new_outer, new_momentum, their_rows, our_rows, outer_rows, momentum_rows, loads, stores = refs[-8:]
+    arriving, leaving = [], []
+    for k, (top, bottom) in enumerate(zip(cuts, cuts[1:])):
+        here, there = pl.ds(top, bottom - top), pl.ds(first + top, bottom - top)
+        sources = (theirs.at[here], ours.at[there], outer.at[there], momentum.at[there])
+        buffers = (their_rows, our_rows, outer_rows, momentum_rows)
+        arriving.append([pltpu.make_async_copy(s, b.at[here], loads.at[i, k]) for i, (s, b) in enumerate(zip(sources, buffers))])
+        results = ((outer_rows, new_outer), (momentum_rows, new_momentum))
+        leaving.append([pltpu.make_async_copy(b.at[here], d.at[there], stores.at[i, k]) for i, (b, d) in enumerate(results)])
+    for copies in arriving:
+        for copy in copies:
+            copy.start()
+    for (top, bottom), copies, results in zip(zip(cuts, cuts[1:]), arriving, leaving):
+        for copy in copies:
+            copy.wait()
+        rows = slice(top, bottom)
+        frag_sum = our_rows[rows].astype(F32) + their_rows[rows].astype(F32)
+        outer_rows[rows], momentum_rows[rows] = nesterov(frag_sum, outer_rows[rows], momentum_rows[rows], islands)
+        for copy in results:
+            copy.start()
+    for copies in leaving:
+        for copy in copies:
+            copy.wait()
+
+
+def update(k, theirs, local_frag, outer_frag, momentum, done):
+    islands = lax.axis_size("island")
+    ours, outer, held = (a.reshape(-1, a.shape[-1]) for a in (local_frag, outer_frag, momentum))
+    unit = ours.shape[0] // units
+    (first, size, parts), cols = chunk_units[k], ours.shape[1]
+    first, rows = first * unit, size * unit
+    if parts is None:
+        ours, outer, held = (lax.slice_in_dim(a, first, first + rows) for a in (ours, outer, held))
+        results = nesterov(ours.astype(F32) + theirs.astype(F32), outer, held, islands)
+        return [lax.dynamic_update_slice(whole, part, (first, 0)) for whole, part in zip(done, results)]
+    cuts = [rows * i // parts // 16 * 16 for i in range(parts)] + [rows]
+    hbm = pl.BlockSpec(memory_space=pltpu.HBM)
     return pl.pallas_call(
-        lambda *_: None,
-        out_specs=[pl.BlockSpec(memory_space=pltpu.HBM)] * 2,
-        out_shape=[jax.ShapeDtypeStruct(like.shape, like.dtype)] * 2,
+        functools.partial(update_kernel, islands, first, cuts),
+        in_specs=[hbm] * (4 + len(done)),
+        out_specs=[hbm] * 2,
+        out_shape=[jax.ShapeDtypeStruct(outer.shape, F32)] * 2,
+        scratch_shapes=[pltpu.VMEM((rows, cols), BF16)] * 2
+        + [pltpu.VMEM((rows, cols), F32)] * 2
+        + [pltpu.SemaphoreType.DMA((4, parts)), pltpu.SemaphoreType.DMA((2, parts))],
+        input_output_aliases={4 + i: i for i in range(len(done))},
+        compiler_params=pltpu.CompilerParams(vmem_limit_bytes=32 * 1024 * 1024),
         cost_estimate=pl.CostEstimate(flops=0, bytes_accessed=0, transcendentals=0),
-    )()
-
-
-def update(k, theirs, local_frag, outer_frag, momentum, done):
-    ours, outer, held = (a.reshape(-1, a.shape[-1]) for a in (local_frag, outer_frag, momentum))
-    if done is None:
-        done = unwritten(outer)
-    first = chunk_units[k][0] * (ours.shape[0] // units)
-    ours, outer, held = (lax.slice_in_dim(a, first, first + theirs.shape[0]) for a in (ours, outer, held))
-    results = nesterov(ours.astype(F32) + theirs.astype(F32), outer, held, lax.axis_size("island"))
-    return [lax.dynamic_update_slice(whole, part, (first, 0)) for whole, part in zip(done, results)]
-
-
-def piece_kernel(firsts, ours, *refs):
-    pieces, buffers, loads, stores = refs[: len(firsts)], refs[len(firsts) : -2], refs[-2], refs[-1]
-    inward = [
-        pltpu.make_async_copy(ours.at[pl.ds(first, piece.shape[0])], buffer, loads.at[k])
-        for k, (first, piece, buffer) in enumerate(zip(firsts, pieces, buffers))
-    ]
-    outward = [pltpu.make_async_copy(buffer, piece, stores.at[k]) for k, (piece, buffer) in enumerate(zip(pieces, buffers))]
+    )(theirs, ours, outer, held, *done)
+
+
+def piece_kernel(parts, ours, *refs):
+    pieces, buffers, loads, stores = refs[: len(parts)], refs[len(parts) : -2], refs[-2], refs[-1]
+    inward, outward = [], []
+    for (first, cuts), piece, buffer in zip(parts, pieces, buffers):
+        for top, bottom in zip(cuts, cuts[1:]):
+            rows, k = pl.ds(top, bottom - top), len(inward)
+            inward.append(pltpu.make_async_copy(ours.at[pl.ds(first + top, bottom - top)], buffer.at[rows], loads.at[k]))
+            outward.append(pltpu.make_async_copy(buffer.at[rows], piece.at[rows], stores.at[k]))
     for copy in inward:
         copy.start()
     for load, store in zip(inward, outward):
@@ -56,19 +90,23 @@
         copy.wait()
 
 
-def pieces_of(local_frag, members):
+def pieces_of(local_frag, members, hint=0):
     ours = local_frag.reshape(-1, local_frag.shape[-1])
     unit, cols = ours.shape[0] // units, ours.shape[1]
-    firsts = [chunk_units[k][0] * unit for k in members]
     shapes = [(chunk_units[k][1] * unit, cols) for k in members]
+    parts = []
+    for k, (rows, _) in zip(members, shapes):
+        cuts = list(range(0, rows, 4 * unit)) + [rows]
+        parts.append((chunk_units[k][0] * unit, cuts))
+    copies = sum(len(cuts) - 1 for _, cuts in parts)
     return pl.pallas_call(
-        functools.partial(piece_kernel, firsts),
+        functools.partial(piece_kernel, parts),
         in_specs=[pl.BlockSpec(memory_space=pltpu.HBM)],
         out_specs=[pl.BlockSpec(memory_space=pltpu.HBM)] * len(members),
         out_shape=[jax.ShapeDtypeStruct(s, BF16) for s in shapes],
-        scratch_shapes=[pltpu.VMEM(s, BF16) for s in shapes] + [pltpu.SemaphoreType.DMA((len(members),))] * 2,
+        scratch_shapes=[pltpu.VMEM(s, BF16) for s in shapes] + [pltpu.SemaphoreType.DMA((copies,))] * 2,
         compiler_params=pltpu.CompilerParams(vmem_limit_bytes=16 * 1024 * 1024),
-        cost_estimate=pl.CostEstimate(flops=0, bytes_accessed=0, transcendentals=0),
+        cost_estimate=pl.CostEstimate(flops=hint, bytes_accessed=0, transcendentals=0),
     )(ours)
 
 
@@ -108,7 +146,7 @@
     return part_of
 
 
-def sum_scatter(part, part_of, axis):
+def sum_scatter(came, part_of, axis):
     n = lax.axis_size(axis)
     received = {k: [] for k in range(n)}
     bit = 1
@@ -118,7 +156,7 @@
             part = part_of(leaving_at(axis, bit))
             for terms in zip(*(received[k] for k in leaving)):
                 part = part + jnp.concatenate([t.astype(F32) for t in terms])
-        came = paired(part.astype(BF16), axis, bit)
+            came = paired(part.astype(BF16), axis, bit)
         for slot, block in zip(leaving, jnp.split(came, len(leaving))):
             received[slot ^ bit].append(block)
         bit *= 2
@@ -132,11 +170,13 @@
     core = place[1]
     half, cols = own.shape[0] // 2, weight.shape[1]
     share = summed.shape[0] // (peers + 1)
-    keys_own[...] = jnp.dot(own[...], weight[...], preferred_element_type=F32)
-    for blocks, at in ((mine, core), (other, 1 - core)):
-        for block, packet in zip(blocks, packets):
-            part = jnp.dot(block[...], weight[...], preferred_element_type=F32)
-            packet[pl.ds(pl.multiple_of(at * half, half), half), :] = part.astype(BF16)
+    rows = jnp.concatenate([own[...]] + [block[...] for block in (*mine, *other)])
+    part = jnp.dot(rows, weight[...], preferred_element_type=F32)
+    keys_own[...] = part[: 2 * half]
+    part = part.astype(BF16)
+    for s, packet in enumerate(packets):
+        for top, at in ((2 + s) * half, core), ((2 + peers + s) * half, 1 - core):
+            packet[pl.ds(pl.multiple_of(at * half, half), half), :] = part[top : top + half]
     for s, packet in enumerate(packets, 1):
         for j in range(summed.shape[1] // cols):
             top = 2 * half + j * share
@@ -196,28 +236,27 @@
     return lax.axis_index("fsdp"), lax.rem(lax.axis_index("tensor"), 2)
 
 
+def columns_for(tokens, s, width):
+    me, core = place_of()
+    half = tokens.shape[0] // 2
+    return lax.dynamic_slice(tokens, (core * half, lax.rem(me + s, lax.axis_size("fsdp")) * width), (half, width))
+
+
 def gather(tokens, weight, cotangent):
-    me, core = place_of()
-    shards = lax.axis_size("fsdp")
-    width, half = weight.shape[0], tokens.shape[0] // 2
-    leaving = [
-        lax.dynamic_slice(tokens, (core * half, lax.rem(me + s, shards) * width), (half, width)) for s in range(1, shards)
-    ]
-    cots = [cotangent] + [shifted(cotangent, "fsdp", s) for s in range(1, shards)]
-    mine = shifted(leaving[0], "fsdp", 1)
-    mine, cots = lax.optimization_barrier((mine, cots))
-    cots = jnp.stack(cots)
-    return cots, input_terms(cots, weight)(leaving_at("tensor", 1)).astype(BF16), mine, leaving[1:]
-
-
-def combine(cots, part, mine, leaving, tokens, weight):
+    cots = jnp.stack([cotangent] + [shifted(cotangent, "fsdp", s) for s in range(1, lax.axis_size("fsdp"))])
+    part = input_terms(cots, weight)(leaving_at("tensor", 1)).astype(BF16)
+    return cots, part, shifted(columns_for(tokens, 1, weight.shape[0]), "fsdp", 1)
+
+
+def combine(cots, part, mine, tokens, weight):
     place = jnp.stack(place_of()).astype(jnp.int32)
     shards, heads = lax.axis_size("fsdp"), lax.axis_size("tensor")
     width, cols = weight.shape
     rows = tokens.shape[0]
     share = rows // heads
 
-    mine = [mine] + [shifted(block, "fsdp", s) for s, block in enumerate(leaving, 2)]
+    part = paired(part, "tensor", 1)
+    mine = [mine] + [shifted(columns_for(tokens, s, width), "fsdp", s) for s in range(2, shards)]
     other = [paired(block, "tensor", 1) for block in mine]
     summed = sum_scatter(part, input_terms(cots, weight), "tensor").astype(BF16)
     packet = jax.ShapeDtypeStruct((rows + share * width // cols, cols), BF16)
@@ -226,12 +265,12 @@
         [jax.ShapeDtypeStruct((rows, cols), F32)] + [packet] * (shards - 1),
         place, tokens, *mine, *other, weight, summed,
     )
-    return (cots, mine, other), (keys_own, summed), packets
-
-
-def finish(gathered, own, packets, tokens, weight):
+    return mine[1:], other, (keys_own, summed), packets
+
+
+def finish(cots, mine, more, other, own, packets, tokens, weight):
     place = jnp.stack(place_of()).astype(jnp.int32)
-    cots, mine, other = gathered
+    mine = [mine, *more]
     keys_own, summed = own
     shards, rows, cols = cots.shape
     packets = [shifted(p, "fsdp", -s) for s, p in enumerate(packets, 1)]
@@ -250,38 +289,33 @@
     weight = key_weight[0]
     islands = lax.axis_size("island")
     if islands != 2:
-        state = combine(*gather(tokens, weight, key_cotangent), tokens, weight)
-        keys, input_grad, weight_grad = finish(*state, tokens, weight)
+        cots, part, mine = gather(tokens, weight, key_cotangent)
+        state = combine(cots, part, mine, tokens, weight)
+        keys, input_grad, weight_grad = finish(cots, mine, *state, tokens, weight)
         frag_sum = lax.psum(local_frag[0], "island").astype(F32)
         new_outer, new_momentum = nesterov(frag_sum, outer_frag, momentum, islands)
         return (keys, input_grad, weight_grad[None], new_outer, new_momentum)
 
-    frag = (local_frag, outer_frag, momentum)
     theirs = [swapped(*pieces_of(local_frag, [0]))]
-
-    def step_one(tokens, weight, key_cotangent, local_frag):
-        return gather(tokens, weight, key_cotangent), pieces_of(local_frag, [1])
-
-    state, (piece,) = together(step_one, tokens, weight, key_cotangent, local_frag)
-    theirs.append(swapped(piece))
+    cots, part, mine = together(gather, tokens, weight, key_cotangent)
+
+    def step_two(cots, part, mine, tokens, weight, local_frag):
+        return combine(cots, part, mine, tokens, weight), pieces_of(local_frag, range(1, len(chunk_units)), hint=6 * 10**9)
+
+    state, pieces = together(step_two, cots, part, mine, tokens, weight, local_frag)
+    theirs += [swapped(piece) for piece in pieces]
     theirs[0], state = lax.optimization_barrier((theirs[0], state))
 
-    def step_two(theirs, state, tokens, weight, *frag):
-        pieces = pieces_of(frag[0], range(2, len(chunk_units)))
-        return combine(*state, tokens, weight), pieces, update(0, theirs, *frag, None)
-
-    state, pieces, done = together(step_two, theirs[0], state, tokens, weight, *frag)
-    theirs.append(swapped(pieces[0]))
-    theirs[1], state, done = lax.optimization_barrier((theirs[1], state, done))
-
-    def step_three(theirs, state, done, tokens, weight, *frag):
-        return finish(*state, tokens, weight), update(1, theirs, *frag, done)
-
-    (keys, input_grad, weight_grad), done = together(step_three, theirs[1], state, done, tokens, weight, *frag)
-    theirs += [swapped(piece) for piece in pieces[1:]]
-    for k in range(2, len(theirs)):
+    def step_three(theirs, cots, mine, state, tokens, weight, *frag):
+        return finish(cots, mine, *state, tokens, weight), update(0, theirs, *frag, ())
+
+    results, done = together(
+        step_three, theirs[0], cots, mine, state, tokens, weight, local_frag, outer_frag, momentum
+    )
+    keys, input_grad, weight_grad = results
+    for k in range(1, len(theirs)):
         theirs[k], done = lax.optimization_barrier((theirs[k], done))
-        done = update(k, theirs[k], *frag, done)
+        done = update(k, theirs[k], local_frag, outer_frag, momentum, done)
     new_outer, new_momentum = (a.reshape(outer_frag.shape) for a in done)
     return (keys, input_grad, weight_grad[None], new_outer, new_momentum)
 

time: 80.9 us -> 76.8 us (0.949)
  other arithmetic: 21.4 us -> 5.17 us
  Pallas kernels: 14.6 us -> 24.5 us
  waiting for transfers between devices: 12.9 us -> 15.6 us
  starting transfers between devices: 23 us -> 21.9 us
    dynamic_update_slice x4 -> x1, other arithmetic: 18.5 us -> 2.57 us  [update(): lax.dynamic_update_slice(whole, part, (first, 0))]
    pallas_call x4, Pallas kernels: 5.02 us -> 16.1 us  [the longest x2 12 us: update(): pl.pallas_call(functools.partial(update_kernel, islands, first, cuts), in...]
    ppermute x9, waiting for transfers between devices: 8.71 us -> 10.7 us  [shifted(): return lax.ppermute(x, axis, [(i, (i + step) % n) for i in range(n)])]
    pallas_call x3, Pallas kernels: 9.54 us -> 8.35 us  [local_call(): pl.pallas_call(kernel, grid_spec=pltpu.PrefetchScalarGridSpec(num_scalar_...]
    convert_element_type x1, other arithmetic: 1.98 us -> 0.86 us  [combine(): summed = sum_scatter(part, input_terms(cots, weight), 'tensor').astype(BF16)]
    cond x15 -> x10, local copies, waits for them, and re-layouts: 0.96 us -> 0.02 us
    another operation x1, other arithmetic: 0.75 us -> 1.56 us  [gather(): jnp.stack([cotangent] + [shifted(cotangent, 'fsdp', s) for s in range(1,...]
    dynamic_slice x1 -> x2, local copies, waits for them, and re-layouts: 1.92 us -> 2.73 us  [columns_for(): lax.dynamic_slice(tokens, (core * half, lax.rem(me + s, lax.axis_size('fs...]
  transfers between devices with their start and end apart: 18 -> 17, of which waited for: 6 -> 9; matrix products, arithmetic and copies ran while one was open for 33% -> 14% of each run, Pallas kernels for 16% -> 30%
where the time goes in v3:
time: 76.8 us; the launch traced here: 76.2 us
  Pallas kernels  24.5 us (32%)
  starting transfers between devices  21.9 us (29%)
  waiting for transfers between devices  15.6 us (20%)
  other arithmetic  5.17 us (7%)
  local copies, waits for them, and re-layouts  4.51 us (6%)
  matrix products  3.73 us (5%)
    ppermute x9, starting transfers between devices, shifted(): return lax.ppermute(x, axis, [(i, (i + step) % n) for i in range(n)])  14.7 us
    pallas_call x2, Pallas kernels, update(): pl.pallas_call(functools.partial(update_kernel, islands, first, cuts), in...  12 us
    ppermute x9, waiting for transfers between devices, shifted(): return lax.ppermute(x, axis, [(i, (i + step) % n) for i in range(n)])  10.7 us
    pallas_call x3, Pallas kernels, local_call(): pl.pallas_call(kernel, grid_spec=pltpu.PrefetchScalarGridSpec(num_scalar_...  8.35 us
    ppermute x3, starting transfers between devices, swapped(): return lax.ppermute(piece, 'island', [(0, 1), (1, 0)])  5.06 us
    pallas_call x2, Pallas kernels, pieces_of(): pl.pallas_call(functools.partial(piece_kernel, parts), in_specs=[pl.Block...  4.19 us
    dot_general x3, matrix products, part_of(): lax.dot_general(rows_of.reshape(-1, cots.shape[2]), weight, (((1,), (1,))...  3.73 us
    ppermute x3, waiting for transfers between devices, swapped(): return lax.ppermute(piece, 'island', [(0, 1), (1, 0)])  3.68 us
  transfers between devices with their start and end apart: 17, of which 9 were waited for; matrix products, arithmetic and copies ran while one was open for 14% of the time, Pallas kernels for 30%

profile of v3, /device:TPU:0, one launch (start us, length us, event | category | flops | bytes accessed | tf_op | source)
XLA Modules:
  0.0 76.2 jit_solution(16456787305068545733)
XLA Ops:
  0.6 1.9 %shard_map.102 = bf16[1824,512]{1,0:T(8,128)(2,1)S(1)} custom-call(bf16[3072,512]{1,0:T(8,128)(2,1)} %bitcast.28), custom_call_target="tpu_custom_call" | custom-call | tf_op jit(solution)/shard_map/pallas_call | solution.py:102
  2.5 3.0 %collective-permute-start.14 = (bf16[1824,512]{1,0:T(8,128)(2,1)S(1)}, bf16[1824,512]{1,0:T(8,128)(2,1)}, u32[]{:S(2)}, u32[]{:S(2)}) collective-permute-start(bf16[1824,512]{1,0:T(8,128)(2,1)S(1)} %shard_map.102), channel_id=1, source_target_pairs={{0,16},{16,0},{1,17},{17,1},{2,18},{18,2},{3,19},{19,3},{4,20},{20... | collective-permute-start | bytes 5603336 | tf_op jit(solution)/shard_map/ppermute | solution.py:114
  5.6 15.0 %conditional.3 = (bf16[4,128,256]{2,1,0:T(8,128)(2,1)}, bf16[256,1536]{1,0:T(8,128)(2,1)S(1)}, bf16[64,1536]{1,0:T(8,128)(2,1)}) conditional(s32[]{:T(128)} %convert_element_type.29, () %tuple.39, (bf16[128,256]{1,0:T(8,128)(2,1)}, bf16[1536,256]{1,0:T(8,128)(2,1)}, bf16[128,6144]{1,0:T(8,128)(2,1)}) %tuple.57), branch_computations={%region_0.0_spmd, %region_1.0_spmd} | conditional | flops 202178576 | bytes 4719186 | solution.py:119
  5.6 2.6 %collective-permute-start.4 = (bf16[128,256]{1,0:T(8,128)(2,1)}, bf16[128,256]{1,0:T(8,128)(2,1)S(1)}, u32[]{:S(2)}, u32[]{:S(2)}) collective-permute-start(bf16[128,256]{1,0:T(8,128)(2,1)} %get-tuple-element.173), channel_id=1, source_target_pairs={{0,8},{4,12},{8,0},{12,4},{1,9},{5,13},{9,1},{13,5},{2,10},{6,14},... | collective-permute-start | bytes 196616 | tf_op jit(solution)/shard_map/cond/branch_1_fun/ppermute | solution.py:126
  8.2 1.6 %collective-permute-start.3 = (bf16[128,256]{1,0:T(8,128)(2,1)}, bf16[128,256]{1,0:T(8,128)(2,1)S(1)}, u32[]{:S(2)}, u32[]{:S(2)}) collective-permute-start(bf16[128,256]{1,0:T(8,128)(2,1)} %get-tuple-element.173), channel_id=1, source_target_pairs={{0,4},{4,8},{8,12},{12,0},{1,5},{5,9},{9,13},{13,1},{2,6},{6,10},{... | collective-permute-start | bytes 196616 | tf_op jit(solution)/shard_map/cond/branch_1_fun/ppermute | solution.py:126
  9.7 2.2 %collective-permute-start.5 = (bf16[128,256]{1,0:T(8,128)(2,1)}, bf16[128,256]{1,0:T(8,128)(2,1)S(1)}, u32[]{:S(2)}, u32[]{:S(2)}) collective-permute-start(bf16[128,256]{1,0:T(8,128)(2,1)} %get-tuple-element.173), channel_id=1, source_target_pairs={{0,12},{4,0},{8,4},{12,8},{1,13},{5,1},{9,5},{13,9},{2,14},{6,2},{... | collective-permute-start | bytes 196616 | tf_op jit(solution)/shard_map/cond/branch_1_fun/ppermute | solution.py:126
  13.0 1.6 %collective-permute-done.3 = bf16[128,256]{1,0:T(8,128)(2,1)S(1)} collective-permute-done((bf16[128,256]{1,0:T(8,128)(2,1)}, bf16[128,256]{1,0:T(8,128)(2,1)S(1)}, u32[]{:S(2)}, u32[]{:S(2)}) %collective-permute-start.3) | collective-permute-done | bytes 65568 | tf_op jit(solution)/shard_map/cond/branch_1_fun/ppermute | solution.py:126
  18.9 1.6 %collective-permute-done.6 = bf16[64,1536]{1,0:T(8,128)(2,1)} collective-permute-done((bf16[64,1536]{1,0:T(8,128)(2,1)S(1)}, bf16[64,1536]{1,0:T(8,128)(2,1)}, u32[]{:S(2)}, u32[]{:S(2)}) %collective-permute-start.6) | collective-permute-done | bytes 196640 | tf_op jit(solution)/shard_map/cond/branch_1_fun/ppermute | solution.py:126
  20.6 22.7 %conditional.4 = (bf16[64,1536]{1,0:T(8,128)(2,1)}, bf16[64,1536]{1,0:T(8,128)(2,1)}, bf16[64,1536]{1,0:T(8,128)(2,1)}, bf16[64,1536]{1,0:T(8,128)(2,1)}, bf16[6...) conditional(s32[]{:T(128)} %convert_element_type.29, () %tuple.38, ...), branch_computations={%region_2.0_spmd, %region_3.0_spmd} | conditional | flops 6202899456 | bytes 30671880 | solution.py:119
  21.1 1.8 %fusion.2 = (bf16[64,1536]{1,0:T(8,128)(2,1)}, bf16[64,1536]{1,0:T(8,128)(2,1)}) fusion(bf16[128,6144]{1,0:T(8,128)(2,1)} %get-tuple-element.56.own, s32[]{:T(128)S(6)} %select_n.23, s32[]{:T(128)S(6)} %select_n.25, s32[]{:T(128)S(6)} %select_n.24), kind=kLoop, calls=%fused_computation.16 | loop fusion | bytes 786444 | tf_op jit(solution)/shard_map/cond/branch_1_fun/dynamic_slice | solution.py:242
  22.9 2.6 %collective-permute-start.8 = (bf16[64,1536]{1,0:T(8,128)(2,1)}, bf16[64,1536]{1,0:T(8,128)(2,1)}, u32[]{:S(2)}, u32[]{:S(2)}) collective-permute-start(bf16[64,1536]{1,0:T(8,128)(2,1)} %get-tuple-element.176), channel_id=1, source_target_pairs={{0,12},{4,0},{8,4},{12,8},{1,13},{5,1},{9,5},{13,9},{2,14},{6,2},{... | collective-permute-start | bytes 589832 | tf_op jit(solution)/shard_map/cond/branch_1_fun/ppermute | solution.py:126
  26.3 1.8 %add_convert_fusion.1 = bf16[128,1536]{1,0:T(8,128)(2,1)S(1)} fusion(bf16[256,1536]{1,0:T(8,128)(2,1)S(1)} %collective-permute-done.12, bf16[128,256]{1,0:T(8,128)(2,1)S(1)} %bitcast.44, bf16[1536,256]{1,0:T(8,128)(2,1)} %get-tuple-element.58.refs_6_), kind=kOutput, calls=%fused_computation.6 | convolution fusion | flops 101253120 | bytes 1638400 | tf_op jit(solution)/shard_map/cond/branch_1_fun/dot_general | solution.py:142
  29.7 2.3 %branch_1_fun.6 = (bf16[960,512]{1,0:T(8,128)(2,1)}, bf16[288,512]{1,0:T(8,128)(2,1)}) custom-call(bf16[3072,512]{1,0:T(8,128)(2,1)} %bitcast.31), custom_call_target="tpu_custom_call" | custom-call | flops 6000000000 | tf_op jit(solution)/shard_map/cond/branch_1_fun/pallas_call | solution.py:102
  32.6 5.3 %collective-permute-done.7.refs_1_ = bf16[64,1536]{1,0:T(8,128)(2,1)} collective-permute-done((bf16[64,1536]{1,0:T(8,128)(2,1)}, bf16[64,1536]{1,0:T(8,128)(2,1)}, u32[]{:S(2)}, u32[]{:S(2)}) %collective-permute-start.7) | collective-permute-done | bytes 196640 | tf_op jit(solution)/shard_map/cond/branch_1_fun/ppermute | solution.py:126
  39.9 3.4 %branch_1_fun.5 = (f32[128,256]{1,0:T(8,128)}, bf16[320,256]{1,0:T(8,128)(2,1)}, bf16[320,256]{1,0:T(8,128)(2,1)}, bf16[320,256]{1,0:T(8,128)(2,1)}) custom-call(s32[2]{0:T(128)S(1)} %pad_add_fusion.place, bf16[128,6144]{1,0:T(8,128)(2,1)S(1)} %copy-done.1, bf16[64,1536]{1,0:T(8,128)(2,1)} %get-tuple-element.57.refs_0_, ...), custom_call_target="tpu_custom_call" | custom-call | tf_op jit(solution)/shard_map/cond/branch_1_fun/pallas_call | solution.py:224
  46.7 20.2 %conditional.5 = (bf16[128,256]{1,0:T(8,128)(2,1)}, bf16[32,6144]{1,0:T(8,128)(2,1)}, f32[3072,512]{1,0:T(8,128)}, f32[3072,512]{1,0:T(8,128)}, bf16[1,1536,256]{2,1,0:T(8,128)(2,1)S(1)}) conditional(s32[]{:T(128)} %convert_element_type.29, () %tuple.37, (bf16[320,256]{1,0:T(8,128)(2,1)}, bf16[320,256]{1,0:T(8,128)(2,1)}, bf16[320,256]{1,0:T(8,128)(2,1)}, ...), branch_computations={%region_4.0_spmd, %region_5.0_spmd} | conditional | flops 13 | bytes 13828150 | solution.py:119
  46.7 3.5 %collective-permute-start = (bf16[320,256]{1,0:T(8,128)(2,1)}, bf16[320,256]{1,0:T(8,128)(2,1)S(1)}, u32[]{:S(2)}, u32[]{:S(2)}) collective-permute-start(bf16[320,256]{1,0:T(8,128)(2,1)} %get-tuple-element.70), channel_id=1, source_target_pairs={{0,12},{4,0},{8,4},{12,8},{1,13},{5,1},{9,5},{13,9},{2,14},{6,2},{... | collective-permute-start | bytes 491528 | tf_op jit(solution)/shard_map/cond/branch_1_fun/ppermute | solution.py:126
  50.4 1.9 %collective-permute-start.2 = (bf16[320,256]{1,0:T(8,128)(2,1)}, bf16[320,256]{1,0:T(8,128)(2,1)S(1)}, u32[]{:S(2)}, u32[]{:S(2)}) collective-permute-start(bf16[320,256]{1,0:T(8,128)(2,1)} %get-tuple-element.72), channel_id=1, source_target_pairs={{0,4},{4,8},{8,12},{12,0},{1,5},{5,9},{9,13},{13,1},{2,6},{6,10},{... | collective-permute-start | bytes 491528 | tf_op jit(solution)/shard_map/cond/branch_1_fun/ppermute | solution.py:126
  52.4 7.5 %branch_1_fun.8 = (f32[3072,512]{1,0:T(8,128)}, f32[3072,512]{1,0:T(8,128)}) custom-call(bf16[1824,512]{1,0:T(8,128)(2,1)} %get-tuple-element.75.theirs, bf16[3072,512]{1,0:T(8,128)(2,1)} %bitcast.32, f32[3072,512]{1,0:T(8,128)} %bitcast.35, f32[3072,512]{1,0:T(8,128)} %bitcast.38), custom_call_target="tpu_custom_call" | custom-call | tf_op jit(solution)/shard_map/cond/branch_1_fun/pallas_call | solution.py:62
  59.9 2.6 %branch_1_fun.9 = bf16[1536,256]{1,0:T(8,128)(2,1)S(1)} custom-call(s32[2]{0:T(128)S(1)} %pad_add_fusion.1.place, bf16[128,6144]{1,0:T(8,128)(2,1)S(1)} %copy-done.2, bf16[64,1536]{1,0:T(8,128)(2,1)} %get-tuple-element.82.refs_0_, bf16[64,1536]{1,0:T(8,128)(2,1)} %get-tuple-element.83.refs_1_, bf16[64,1536]{1,0:T(8,128)(2,1)} %get-tuple-element.84.refs_2_, ...), custom_call_target="tpu_custom_call" | custom-call | tf_op jit(solution)/shard_map/cond/branch_1_fun/pallas_call | solution.py:224
  62.5 1.9 %collective-permute-done.1.refs_1_ = bf16[320,256]{1,0:T(8,128)(2,1)S(1)} collective-permute-done((bf16[320,256]{1,0:T(8,128)(2,1)}, bf16[320,256]{1,0:T(8,128)(2,1)S(1)}, u32[]{:S(2)}, u32[]{:S(2)}) %collective-permute-start.1) | collective-permute-done | bytes 163872 | tf_op jit(solution)/shard_map/cond/branch_1_fun/ppermute | solution.py:126
  64.5 2.4 %branch_1_fun.7 = (bf16[128,256]{1,0:T(8,128)(2,1)}, bf16[32,6144]{1,0:T(8,128)(2,1)}) custom-call(s32[2]{0:T(128)S(1)} %pad_add_fusion.1.place, f32[128,256]{1,0:T(8,128)} %get-tuple-element.68.keys_own, bf16[128,1536]{1,0:T(8,128)(2,1)} %get-tuple-element.69.summed, bf16[320,256]{1,0:T(8,128)(2,1)S(1)} %collective-permute-done.refs_0_, ...), custom_call_target="tpu_custom_call" | custom-call | tf_op jit(solution)/shard_map/cond/branch_1_fun/pallas_call | solution.py:224
  68.1 4.5 %shard_map.103 = (f32[3072,512]{1,0:T(8,128)}, f32[3072,512]{1,0:T(8,128)}) custom-call(bf16[960,512]{1,0:T(8,128)(2,1)S(1)} %collective-permute-done.16.theirs, bf16[3072,512]{1,0:T(8,128)(2,1)} %bitcast.29, f32[3072,512]{1,0:T(8,128)} %bitcast.33, f32[3072,512]{1,0:T(8,128)} %bitcast.36, ...), custom_call_target="tpu_custom_call", output_to_operand_aliasing={{0}: (4, {}), {1}: (5, {})} | custom-call | tf_op jit(solution)/shard_map/pallas_call | solution.py:62
  73.7 2.6 %fusion.1 = (f32[3072,512]{1,0:T(8,128)}, f32[3072,512]{1,0:T(8,128)}) fusion(f32[3072,512]{1,0:T(8,128)} %get-tuple-element.171, f32[3072,512]{1,0:T(8,128)} %bitcast.37, bf16[288,512]{1,0:T(8,128)(2,1)S(1)} %collective-permute-done.15, bf16[3072,512]{1,0:T(8,128)(2,1)} %bitcast.30, f32[3072,512]{1,0:T(8,128)} %bitcast.34, f32[3072,512]{1,0:T(8,128)} %get-tuple-element.169), kind=kLoop, calls=%fused_computation.15 | loop fusion | flops 1622016 | bytes 2949120 | tf_op jit(solution)/shard_map/dynamic_update_slice | solution.py:59
  (45 shorter events, 16.9 us)
Async XLA Ops:
  2.5 44.2 %collective-permute-start.14 = (bf16[1824,512]{1,0:T(8,128)(2,1)S(1)}, bf16[1824,512]{1,0:T(8,128)(2,1)}, u32[]{:S(2)}, u32[]{:S(2)}) collective-permute-start(bf16[1824,512]{1,0:T(8,128)(2,1)S(1)} %shard_map.102), channel_id=1, source_target_pairs={{0,16},{16,0},{1,17},{17,1},{2,18},{18,2},{3,19},{19,3},{4,20},{20... | collective-permute-start | bytes 5603336 | tf_op jit(solution)/shard_map/ppermute | solution.py:114
  5.6 7.4 %collective-permute-start.4 = (bf16[128,256]{1,0:T(8,128)(2,1)}, bf16[128,256]{1,0:T(8,128)(2,1)S(1)}, u32[]{:S(2)}, u32[]{:S(2)}) collective-permute-start(bf16[128,256]{1,0:T(8,128)(2,1)} %get-tuple-element.173), channel_id=1, source_target_pairs={{0,8},{4,12},{8,0},{12,4},{1,9},{5,13},{9,1},{13,5},{2,10},{6,14},... | collective-permute-start | bytes 196616 | tf_op jit(solution)/shard_map/cond/branch_1_fun/ppermute | solution.py:126
  8.2 6.4 %collective-permute-start.3 = (bf16[128,256]{1,0:T(8,128)(2,1)}, bf16[128,256]{1,0:T(8,128)(2,1)S(1)}, u32[]{:S(2)}, u32[]{:S(2)}) collective-permute-start(bf16[128,256]{1,0:T(8,128)(2,1)} %get-tuple-element.173), channel_id=1, source_target_pairs={{0,4},{4,8},{8,12},{12,0},{1,5},{5,9},{9,13},{13,1},{2,6},{6,10},{... | collective-permute-start | bytes 196616 | tf_op jit(solution)/shard_map/cond/branch_1_fun/ppermute | solution.py:126
  9.7 5.2 %collective-permute-start.5 = (bf16[128,256]{1,0:T(8,128)(2,1)}, bf16[128,256]{1,0:T(8,128)(2,1)S(1)}, u32[]{:S(2)}, u32[]{:S(2)}) collective-permute-start(bf16[128,256]{1,0:T(8,128)(2,1)} %get-tuple-element.173), channel_id=1, source_target_pairs={{0,12},{4,0},{8,4},{12,8},{1,13},{5,1},{9,5},{13,9},{2,14},{6,2},{... | collective-permute-start | bytes 196616 | tf_op jit(solution)/shard_map/cond/branch_1_fun/ppermute | solution.py:126
  12.9 7.6 %collective-permute-start.6 = (bf16[64,1536]{1,0:T(8,128)(2,1)S(1)}, bf16[64,1536]{1,0:T(8,128)(2,1)}, u32[]{:S(2)}, u32[]{:S(2)}) collective-permute-start(bf16[64,1536]{1,0:T(8,128)(2,1)S(1)} %dynamic_slice.16), channel_id=1, source_target_pairs={{0,4},{4,8},{8,12},{12,0},{1,5},{5,9},{9,13},{13,1},{2,6},{6,10},{... | collective-permute-start | bytes 589832 | tf_op jit(solution)/shard_map/cond/branch_1_fun/ppermute | solution.py:126
  20.6 5.8 %collective-permute-start.12 = (bf16[256,1536]{1,0:T(8,128)(2,1)S(1)}, bf16[256,1536]{1,0:T(8,128)(2,1)S(1)}, u32[]{:S(2)}, u32[]{:S(2)}) collective-permute-start(bf16[256,1536]{1,0:T(8,128)(2,1)S(1)} %get-tuple-element.60), channel_id=1, source_target_pairs={{0,1},{1,0},{2,3},{3,2},{4,5},{5,4},{6,7},{7,6},{8,9},{9,8},{10,11... | collective-permute-start | bytes 2359304 | tf_op jit(solution)/shard_map/cond/branch_1_fun/ppermute | solution.py:130
  20.6 19.3 %collective-permute-start.9 = (bf16[64,1536]{1,0:T(8,128)(2,1)}, bf16[64,1536]{1,0:T(8,128)(2,1)}, u32[]{:S(2)}, u32[]{:S(2)}) collective-permute-start(bf16[64,1536]{1,0:T(8,128)(2,1)} %get-tuple-element.57.refs_0_), channel_id=1, source_target_pairs={{0,1},{1,0},{2,3},{3,2},{4,5},{5,4},{6,7},{7,6},{8,9},{9,8},{10,11... | collective-permute-start | bytes 589832 | tf_op jit(solution)/shard_map/cond/branch_1_fun/ppermute | solution.py:130
  22.9 9.6 %collective-permute-start.8 = (bf16[64,1536]{1,0:T(8,128)(2,1)}, bf16[64,1536]{1,0:T(8,128)(2,1)}, u32[]{:S(2)}, u32[]{:S(2)}) collective-permute-start(bf16[64,1536]{1,0:T(8,128)(2,1)} %get-tuple-element.176), channel_id=1, source_target_pairs={{0,12},{4,0},{8,4},{12,8},{1,13},{5,1},{9,5},{13,9},{2,14},{6,2},{... | collective-permute-start | bytes 589832 | tf_op jit(solution)/shard_map/cond/branch_1_fun/ppermute | solution.py:126
  25.4 12.4 %collective-permute-start.7 = (bf16[64,1536]{1,0:T(8,128)(2,1)}, bf16[64,1536]{1,0:T(8,128)(2,1)}, u32[]{:S(2)}, u32[]{:S(2)}) collective-permute-start(bf16[64,1536]{1,0:T(8,128)(2,1)} %get-tuple-element.177), channel_id=1, source_target_pairs={{0,8},{4,12},{8,0},{12,4},{1,9},{5,13},{9,1},{13,5},{2,10},{6,14},... | collective-permute-start | bytes 589832 | tf_op jit(solution)/shard_map/cond/branch_1_fun/ppermute | solution.py:126
  26.3 3.4 %copy-start.4 = (bf16[256,1536]{1,0:T(8,128)(2,1)}, bf16[256,1536]{1,0:T(8,128)(2,1)S(1)}, u32[]{:S(2)}) copy-start(bf16[256,1536]{1,0:T(8,128)(2,1)S(1)} %collective-permute-done.12) | copy-start | bytes 2359300 | tf_op jit(solution)/shard_map/cond
  28.1 10.9 %collective-permute-start.13 = (bf16[128,1536]{1,0:T(8,128)(2,1)S(1)}, bf16[128,1536]{1,0:T(8,128)(2,1)S(1)}, u32[]{:S(2)}, u32[]{:S(2)}) collective-permute-start(bf16[128,1536]{1,0:T(8,128)(2,1)S(1)} %add_convert_fusion.1), channel_id=1, source_target_pairs={{0,2},{1,3},{2,0},{3,1},{4,6},{5,7},{6,4},{7,5},{8,10},{9,11},{10,... | collective-permute-start | bytes 1179656 | tf_op jit(solution)/shard_map/cond/branch_1_fun/ppermute | solution.py:130
  29.7 2.4 %copy-start = (bf16[1536,256]{1,0:T(8,128)(2,1)S(1)}, bf16[1536,256]{1,0:T(8,128)(2,1)}, u32[]{:S(2)}) copy-start(bf16[1536,256]{1,0:T(8,128)(2,1)} %get-tuple-element.58.refs_6_) | copy-start | bytes 2359300 | tf_op jit(solution)/shard_map/cond
  29.7 9.3 %copy-start.5 = (bf16[256,1536]{1,0:T(8,128)(2,1)S(1)}, bf16[256,1536]{1,0:T(8,128)(2,1)}, u32[]{:S(2)}) copy-start(bf16[256,1536]{1,0:T(8,128)(2,1)} %copy-done.4) | copy-start | bytes 2359300 | tf_op jit(solution)/shard_map/cond
  29.7 10.2 %copy-start.1 = (bf16[128,6144]{1,0:T(8,128)(2,1)S(1)}, bf16[128,6144]{1,0:T(8,128)(2,1)}, u32[]{:S(2)}) copy-start(bf16[128,6144]{1,0:T(8,128)(2,1)} %get-tuple-element.56.own) | copy-start | bytes 4718596 | tf_op jit(solution)/shard_map/cond
  32.5 7.4 %collective-permute-start.11 = (bf16[64,1536]{1,0:T(8,128)(2,1)}, bf16[64,1536]{1,0:T(8,128)(2,1)}, u32[]{:S(2)}, u32[]{:S(2)}) collective-permute-start(bf16[64,1536]{1,0:T(8,128)(2,1)} %collective-permute-done.8.refs_2_), channel_id=1, source_target_pairs={{0,1},{1,0},{2,3},{3,2},{4,5},{5,4},{6,7},{7,6},{8,9},{9,8},{10,11... | collective-permute-start | bytes 589832 | tf_op jit(solution)/shard_map/cond/branch_1_fun/ppermute | solution.py:130
  37.9 2.0 %collective-permute-start.10 = (bf16[64,1536]{1,0:T(8,128)(2,1)}, bf16[64,1536]{1,0:T(8,128)(2,1)}, u32[]{:S(2)}, u32[]{:S(2)}) collective-permute-start(bf16[64,1536]{1,0:T(8,128)(2,1)} %collective-permute-done.7.refs_1_), channel_id=1, source_target_pairs={{0,1},{1,0},{2,3},{3,2},{4,5},{5,4},{6,7},{7,6},{8,9},{9,8},{10,11... | collective-permute-start | bytes 589832 | tf_op jit(solution)/shard_map/cond/branch_1_fun/ppermute | solution.py:130
  43.3 24.9 %collective-permute-start.16 = (bf16[960,512]{1,0:T(8,128)(2,1)}, bf16[960,512]{1,0:T(8,128)(2,1)S(1)}, u32[]{:S(2)}, u32[]{:S(2)}) collective-permute-start(bf16[960,512]{1,0:T(8,128)(2,1)} %get-tuple-element.161), channel_id=1, source_target_pairs={{0,16},{16,0},{1,17},{17,1},{2,18},{18,2},{3,19},{19,3},{4,20},{20... | collective-permute-start | bytes 2949128 | tf_op jit(solution)/shard_map/ppermute | solution.py:114
  43.8 29.9 %collective-permute-start.15 = (bf16[288,512]{1,0:T(8,128)(2,1)}, bf16[288,512]{1,0:T(8,128)(2,1)S(1)}, u32[]{:S(2)}, u32[]{:S(2)}) collective-permute-start(bf16[288,512]{1,0:T(8,128)(2,1)} %get-tuple-element.160), channel_id=1, source_target_pairs={{0,16},{16,0},{1,17},{17,1},{2,18},{18,2},{3,19},{19,3},{4,20},{20... | collective-permute-start | bytes 884744 | tf_op jit(solution)/shard_map/ppermute | solution.py:114
  46.7 15.8 %collective-permute-start = (bf16[320,256]{1,0:T(8,128)(2,1)}, bf16[320,256]{1,0:T(8,128)(2,1)S(1)}, u32[]{:S(2)}, u32[]{:S(2)}) collective-permute-start(bf16[320,256]{1,0:T(8,128)(2,1)} %get-tuple-element.70), channel_id=1, source_target_pairs={{0,12},{4,0},{8,4},{12,8},{1,13},{5,1},{9,5},{13,9},{2,14},{6,2},{... | collective-permute-start | bytes 491528 | tf_op jit(solution)/shard_map/cond/branch_1_fun/ppermute | solution.py:126
  50.2 14.2 %collective-permute-start.1 = (bf16[320,256]{1,0:T(8,128)(2,1)}, bf16[320,256]{1,0:T(8,128)(2,1)S(1)}, u32[]{:S(2)}, u32[]{:S(2)}) collective-permute-start(bf16[320,256]{1,0:T(8,128)(2,1)} %get-tuple-element.71), channel_id=1, source_target_pairs={{0,8},{4,12},{8,0},{12,4},{1,9},{5,13},{9,1},{13,5},{2,10},{6,14},... | collective-permute-start | bytes 491528 | tf_op jit(solution)/shard_map/cond/branch_1_fun/ppermute | solution.py:126
  50.4 14.0 %collective-permute-start.2 = (bf16[320,256]{1,0:T(8,128)(2,1)}, bf16[320,256]{1,0:T(8,128)(2,1)S(1)}, u32[]{:S(2)}, u32[]{:S(2)}) collective-permute-start(bf16[320,256]{1,0:T(8,128)(2,1)} %get-tuple-element.72), channel_id=1, source_target_pairs={{0,4},{4,8},{8,12},{12,0},{1,5},{5,9},{9,13},{13,1},{2,6},{6,10},{... | collective-permute-start | bytes 491528 | tf_op jit(solution)/shard_map/cond/branch_1_fun/ppermute | solution.py:126
  52.4 7.5 %copy-start.2 = (bf16[128,6144]{1,0:T(8,128)(2,1)S(1)}, bf16[128,6144]{1,0:T(8,128)(2,1)}, u32[]{:S(2)}) copy-start(bf16[128,6144]{1,0:T(8,128)(2,1)} %get-tuple-element.81.own) | copy-start | bytes 4718596 | tf_op jit(solution)/shard_map/cond
  66.9 5.8 %copy-start.3 = (bf16[1,1536,256]{2,1,0:T(8,128)(2,1)}, bf16[1,1536,256]{2,1,0:T(8,128)(2,1)S(1)}, u32[]{:S(2)}) copy-start(bf16[1,1536,256]{2,1,0:T(8,128)(2,1)S(1)} %get-tuple-element.130) | copy-start | bytes 2359300

commit v4 on v3

--- a/solution.py
+++ b/solution.py
@@ -47,16 +47,27 @@
             copy.wait()
 
 
+def own_terms(k, local_frag, outer_frag, momentum):
+    ours, outer, held = (a.reshape(-1, a.shape[-1]) for a in (local_frag, outer_frag, momentum))
+    unit = ours.shape[0] // units
+    first, size, _ = chunk_units[k]
+    ours, outer, held = (lax.slice_in_dim(a, first * unit, (first + size) * unit) for a in (ours, outer, held))
+    return nesterov(ours.astype(F32), outer, held, lax.axis_size("island"))
+
+
+def last_update(theirs, terms, done):
+    share = theirs.astype(F32) / lax.axis_size("island")
+    results = terms[0] + outer_rate * (1 + beta_outer) * share, terms[1] - share
+    first = done[0].shape[0] - theirs.shape[0]
+    return [lax.dynamic_update_slice(whole, part, (first, 0)) for whole, part in zip(done, results)]
+
+
 def update(k, theirs, local_frag, outer_frag, momentum, done):
     islands = lax.axis_size("island")
     ours, outer, held = (a.reshape(-1, a.shape[-1]) for a in (local_frag, outer_frag, momentum))
     unit = ours.shape[0] // units
     (first, size, parts), cols = chunk_units[k], ours.shape[1]
     first, rows = first * unit, size * unit
-    if parts is None:
-        ours, outer, held = (lax.slice_in_dim(a, first, first + rows) for a in (ours, outer, held))
-        results = nesterov(ours.astype(F32) + theirs.astype(F32), outer, held, islands)
-        return [lax.dynamic_update_slice(whole, part, (first, 0)) for whole, part in zip(done, results)]
     cuts = [rows * i // parts // 16 * 16 for i in range(parts)] + [rows]
     hbm = pl.BlockSpec(memory_space=pltpu.HBM)
     return pl.pallas_call(
@@ -74,19 +85,15 @@
 
 
 def piece_kernel(parts, ours, *refs):
-    pieces, buffers, loads, stores = refs[: len(parts)], refs[len(parts) : -2], refs[-2], refs[-1]
-    inward, outward = [], []
-    for (first, cuts), piece, buffer in zip(parts, pieces, buffers):
+    pieces, loads = refs[:-1], refs[-1]
+    copies = []
+    for (first, cuts), piece in zip(parts, pieces):
         for top, bottom in zip(cuts, cuts[1:]):
-            rows, k = pl.ds(top, bottom - top), len(inward)
-            inward.append(pltpu.make_async_copy(ours.at[pl.ds(first + top, bottom - top)], buffer.at[rows], loads.at[k]))
-            outward.append(pltpu.make_async_copy(buffer.at[rows], piece.at[rows], stores.at[k]))
-    for copy in inward:
+            source = ours.at[pl.ds(first + top, bottom - top)]
+            copies.append(pltpu.make_async_copy(source, piece.at[pl.ds(top, bottom - top)], loads.at[len(copies)]))
+    for copy in copies:
         copy.start()
-    for load, store in zip(inward, outward):
-        load.wait()
-        store.start()
-    for copy in outward:
+    for copy in copies:
         copy.wait()
 
 
@@ -96,15 +103,15 @@
     shapes = [(chunk_units[k][1] * unit, cols) for k in members]
     parts = []
     for k, (rows, _) in zip(members, shapes):
-        cuts = list(range(0, rows, 4 * unit)) + [rows]
+        cuts = list(range(0, rows, 5 * unit)) + [rows]
         parts.append((chunk_units[k][0] * unit, cuts))
     copies = sum(len(cuts) - 1 for _, cuts in parts)
     return pl.pallas_call(
         functools.partial(piece_kernel, parts),
         in_specs=[pl.BlockSpec(memory_space=pltpu.HBM)],
-        out_specs=[pl.BlockSpec(memory_space=pltpu.HBM)] * len(members),
-        out_shape=[jax.ShapeDtypeStruct(s, BF16) for s in shapes],
-        scratch_shapes=[pltpu.VMEM(s, BF16) for s in shapes] + [pltpu.SemaphoreType.DMA((copies,))] * 2,
+        out_specs=[pl.BlockSpec(memory_space=pltpu.VMEM)] * len(members),
+        out_shape=[pltpu.VMEM(s, BF16) if k == 0 else jax.ShapeDtypeStruct(s, BF16) for k, s in zip(members, shapes)],
+        scratch_shapes=[pltpu.SemaphoreType.DMA((copies,))],
         compiler_params=pltpu.CompilerParams(vmem_limit_bytes=16 * 1024 * 1024),
         cost_estimate=pl.CostEstimate(flops=hint, bytes_accessed=0, transcendentals=0),
     )(ours)
@@ -303,19 +310,21 @@
         return combine(cots, part, mine, tokens, weight), pieces_of(local_frag, range(1, len(chunk_units)), hint=6 * 10**9)
 
     state, pieces = together(step_two, cots, part, mine, tokens, weight, local_frag)
-    theirs += [swapped(piece) for piece in pieces]
+    theirs.append(swapped(pieces[0]))
     theirs[0], state = lax.optimization_barrier((theirs[0], state))
 
     def step_three(theirs, cots, mine, state, tokens, weight, *frag):
-        return finish(cots, mine, *state, tokens, weight), update(0, theirs, *frag, ())
-
-    results, done = together(
+        return finish(cots, mine, *state, tokens, weight), update(0, theirs, *frag, ()), own_terms(2, *frag)
+
+    results, done, terms = together(
         step_three, theirs[0], cots, mine, state, tokens, weight, local_frag, outer_frag, momentum
     )
     keys, input_grad, weight_grad = results
-    for k in range(1, len(theirs)):
-        theirs[k], done = lax.optimization_barrier((theirs[k], done))
-        done = update(k, theirs[k], local_frag, outer_frag, momentum, done)
+    piece, done = lax.optimization_barrier((pieces[1], done))
+    theirs.append(swapped(piece))
+    theirs[1], done = lax.optimization_barrier((theirs[1], done))
+    done = update(1, theirs[1], local_frag, outer_frag, momentum, done)
+    done = last_update(theirs[2], terms, done)
     new_outer, new_momentum = (a.reshape(outer_frag.shape) for a in done)
     return (keys, input_grad, weight_grad[None], new_outer, new_momentum)
 

time: 76.8 us -> 75 us (0.977)
  waiting for transfers between devices: 15.6 us -> 13.7 us
    ppermute x9, waiting for transfers between devices: 10.7 us -> 8.6 us  [shifted(): return lax.ppermute(x, axis, [(i, (i + step) % n) for i in range(n)])]
    sub x0 -> x1, other arithmetic: none -> 1.52 us  [nesterov(): outer - outer_rate * (average + beta_outer * new_momentum)]
    dynamic_update_slice x1, other arithmetic: 2.57 us -> 1.19 us  [last_update(): lax.dynamic_update_slice(whole, part, (first, 0))]
  transfers between devices with their start and end apart: 17 -> 17, of which waited for: 9 -> 7; matrix products, arithmetic and copies ran while one was open for 14% -> 17% of each run, Pallas kernels for 30% -> 31%
where the time goes in v4:
time: 75 us; the launch traced here: 74.5 us
  Pallas kernels  24.4 us (33%)
  starting transfers between devices  22 us (29%)
  waiting for transfers between devices  13.7 us (18%)
  other arithmetic  5.3 us (7%)
  local copies, waits for them, and re-layouts  4.52 us (6%)
  matrix products  3.73 us (5%)
    ppermute x9, starting transfers between devices, shifted(): return lax.ppermute(x, axis, [(i, (i + step) % n) for i in range(n)])  14.7 us
    pallas_call x2, Pallas kernels, update(): pl.pallas_call(functools.partial(update_kernel, islands, first, cuts), in...  12 us
    ppermute x9, waiting for transfers between devices, shifted(): return lax.ppermute(x, axis, [(i, (i + step) % n) for i in range(n)])  8.6 us
    pallas_call x3, Pallas kernels, local_call(): pl.pallas_call(kernel, grid_spec=pltpu.PrefetchScalarGridSpec(num_scalar_...  8.49 us
    ppermute x3, starting transfers between devices, swapped(): return lax.ppermute(piece, 'island', [(0, 1), (1, 0)])  5.12 us
    pallas_call x2, Pallas kernels, pieces_of(): pl.pallas_call(functools.partial(piece_kernel, parts), in_specs=[pl.Block...  3.97 us
    ppermute x3, waiting for transfers between devices, swapped(): return lax.ppermute(piece, 'island', [(0, 1), (1, 0)])  3.88 us
    dot_general x3, matrix products, part_of(): lax.dot_general(rows_of.reshape(-1, cots.shape[2]), weight, (((1,), (1,))...  3.73 us
  transfers between devices with their start and end apart: 17, of which 7 were waited for; matrix products, arithmetic and copies ran while one was open for 17% of the time, Pallas kernels for 31%

profile of v4, /device:TPU:0, one launch (start us, length us, event | category | flops | bytes accessed | tf_op | source)
XLA Modules:
  0.0 74.5 jit_solution(13210593799409000522)
XLA Ops:
  2.1 3.0 %collective-permute-start.14 = (bf16[1824,512]{1,0:T(8,128)(2,1)S(1)}, bf16[1824,512]{1,0:T(8,128)(2,1)}, u32[]{:S(2)}, u32[]{:S(2)}) collective-permute-start(bf16[1824,512]{1,0:T(8,128)(2,1)S(1)} %shard_map.102), channel_id=1, source_target_pairs={{0,16},{16,0},{1,17},{17,1},{2,18},{18,2},{3,19},{19,3},{4,20},{20... | collective-permute-start | bytes 5603336 | tf_op jit(solution)/shard_map/ppermute | solution.py:121
  5.1 15.0 %conditional.3 = (bf16[4,128,256]{2,1,0:T(8,128)(2,1)}, bf16[256,1536]{1,0:T(8,128)(2,1)S(1)}, bf16[64,1536]{1,0:T(8,128)(2,1)}) conditional(s32[]{:T(128)} %convert_element_type.29, () %tuple.39, (bf16[128,256]{1,0:T(8,128)(2,1)}, bf16[1536,256]{1,0:T(8,128)(2,1)}, bf16[128,6144]{1,0:T(8,128)(2,1)}) %tuple.58), branch_computations={%region_0.0_spmd, %region_1.0_spmd} | conditional | flops 202178576 | bytes 4719186 | solution.py:126
  5.1 2.6 %collective-permute-start.4 = (bf16[128,256]{1,0:T(8,128)(2,1)}, bf16[128,256]{1,0:T(8,128)(2,1)S(1)}, u32[]{:S(2)}, u32[]{:S(2)}) collective-permute-start(bf16[128,256]{1,0:T(8,128)(2,1)} %get-tuple-element.177), channel_id=1, source_target_pairs={{0,8},{4,12},{8,0},{12,4},{1,9},{5,13},{9,1},{13,5},{2,10},{6,14},... | collective-permute-start | bytes 196616 | tf_op jit(solution)/shard_map/cond/branch_1_fun/ppermute | solution.py:133
  7.7 1.6 %collective-permute-start.3 = (bf16[128,256]{1,0:T(8,128)(2,1)}, bf16[128,256]{1,0:T(8,128)(2,1)S(1)}, u32[]{:S(2)}, u32[]{:S(2)}) collective-permute-start(bf16[128,256]{1,0:T(8,128)(2,1)} %get-tuple-element.177), channel_id=1, source_target_pairs={{0,4},{4,8},{8,12},{12,0},{1,5},{5,9},{9,13},{13,1},{2,6},{6,10},{... | collective-permute-start | bytes 196616 | tf_op jit(solution)/shard_map/cond/branch_1_fun/ppermute | solution.py:133
  9.3 2.2 %collective-permute-start.5 = (bf16[128,256]{1,0:T(8,128)(2,1)}, bf16[128,256]{1,0:T(8,128)(2,1)S(1)}, u32[]{:S(2)}, u32[]{:S(2)}) collective-permute-start(bf16[128,256]{1,0:T(8,128)(2,1)} %get-tuple-element.177), channel_id=1, source_target_pairs={{0,12},{4,0},{8,4},{12,8},{1,13},{5,1},{9,5},{13,9},{2,14},{6,2},{... | collective-permute-start | bytes 196616 | tf_op jit(solution)/shard_map/cond/branch_1_fun/ppermute | solution.py:133
  12.6 1.6 %collective-permute-done.3 = bf16[128,256]{1,0:T(8,128)(2,1)S(1)} collective-permute-done((bf16[128,256]{1,0:T(8,128)(2,1)}, bf16[128,256]{1,0:T(8,128)(2,1)S(1)}, u32[]{:S(2)}, u32[]{:S(2)}) %collective-permute-start.3) | collective-permute-done | bytes 65568 | tf_op jit(solution)/shard_map/cond/branch_1_fun/ppermute | solution.py:133
  14.5 1.6 %pad_maximum_fusion = bf16[4,128,256]{2,1,0:T(8,128)(2,1)} fusion(bf16[1,128,256]{2,1,0:T(8,128)(2,1)S(1)} %bitcast.47, bf16[1,128,256]{2,1,0:T(8,128)(2,1)S(1)} %bitcast.45, bf16[1,128,256]{2,1,0:T(8,128)(2,1)S(1)} %bitcast.46, bf16[1,128,256]{2,1,0:T(8,128)(2,1)} %bitcast.44), kind=kLoop, calls=%fused_computation.1 | loop fusion | flops 393216 | bytes 524288 | tf_op jit(solution)/shard_map/cond/branch_1_fun/stack | solution.py:253
  18.5 1.6 %collective-permute-done.6 = bf16[64,1536]{1,0:T(8,128)(2,1)} collective-permute-done((bf16[64,1536]{1,0:T(8,128)(2,1)S(1)}, bf16[64,1536]{1,0:T(8,128)(2,1)}, u32[]{:S(2)}, u32[]{:S(2)}) %collective-permute-start.6) | collective-permute-done | bytes 196640 | tf_op jit(solution)/shard_map/cond/branch_1_fun/ppermute | solution.py:133
  20.1 22.7 %conditional.4 = (bf16[64,1536]{1,0:T(8,128)(2,1)}, bf16[64,1536]{1,0:T(8,128)(2,1)}, bf16[64,1536]{1,0:T(8,128)(2,1)}, bf16[64,1536]{1,0:T(8,128)(2,1)}, bf16[6...) conditional(s32[]{:T(128)} %convert_element_type.29, () %tuple.38, ...), branch_computations={%region_2.0_spmd, %region_3.0_spmd} | conditional | flops 6202899456 | bytes 30671880 | solution.py:126
  20.6 1.8 %fusion.6 = (bf16[64,1536]{1,0:T(8,128)(2,1)}, bf16[64,1536]{1,0:T(8,128)(2,1)}) fusion(bf16[128,6144]{1,0:T(8,128)(2,1)} %get-tuple-element.56.own, s32[]{:T(128)S(6)} %select_n.23, s32[]{:T(128)S(6)} %select_n.25, s32[]{:T(128)S(6)} %select_n.24), kind=kLoop, calls=%fused_computation.21 | loop fusion | bytes 786444 | tf_op jit(solution)/shard_map/cond/branch_1_fun/dynamic_slice | solution.py:249
  22.4 2.6 %collective-permute-start.8 = (bf16[64,1536]{1,0:T(8,128)(2,1)}, bf16[64,1536]{1,0:T(8,128)(2,1)}, u32[]{:S(2)}, u32[]{:S(2)}) collective-permute-start(bf16[64,1536]{1,0:T(8,128)(2,1)} %get-tuple-element.182), channel_id=1, source_target_pairs={{0,12},{4,0},{8,4},{12,8},{1,13},{5,1},{9,5},{13,9},{2,14},{6,2},{... | collective-permute-start | bytes 589832 | tf_op jit(solution)/shard_map/cond/branch_1_fun/ppermute | solution.py:133
  25.9 1.8 %add_convert_fusion.1 = bf16[128,1536]{1,0:T(8,128)(2,1)S(1)} fusion(bf16[256,1536]{1,0:T(8,128)(2,1)S(1)} %collective-permute-done.12, bf16[128,256]{1,0:T(8,128)(2,1)S(1)} %bitcast.43, bf16[1536,256]{1,0:T(8,128)(2,1)} %get-tuple-element.58.refs_6_), kind=kOutput, calls=%fused_computation.6 | convolution fusion | flops 101253120 | bytes 1638400 | tf_op jit(solution)/shard_map/cond/branch_1_fun/dot_general | solution.py:149
  29.3 2.5 %branch_1_fun.6 = (bf16[960,512]{1,0:T(8,128)(2,1)}, bf16[288,512]{1,0:T(8,128)(2,1)}) custom-call(bf16[3072,512]{1,0:T(8,128)(2,1)} %bitcast.30), custom_call_target="tpu_custom_call" | custom-call | flops 6000000000 | tf_op jit(solution)/shard_map/cond/branch_1_fun/pallas_call | solution.py:109
  32.4 5.1 %collective-permute-done.7.refs_1_ = bf16[64,1536]{1,0:T(8,128)(2,1)} collective-permute-done((bf16[64,1536]{1,0:T(8,128)(2,1)}, bf16[64,1536]{1,0:T(8,128)(2,1)}, u32[]{:S(2)}, u32[]{:S(2)}) %collective-permute-start.7) | collective-permute-done | bytes 196640 | tf_op jit(solution)/shard_map/cond/branch_1_fun/ppermute | solution.py:133
  39.5 3.4 %branch_1_fun.5 = (f32[128,256]{1,0:T(8,128)}, bf16[320,256]{1,0:T(8,128)(2,1)}, bf16[320,256]{1,0:T(8,128)(2,1)}, bf16[320,256]{1,0:T(8,128)(2,1)}) custom-call(s32[2]{0:T(128)S(1)} %pad_add_fusion.place, bf16[128,6144]{1,0:T(8,128)(2,1)S(1)} %copy-done.1, bf16[64,1536]{1,0:T(8,128)(2,1)} %get-tuple-element.57.refs_0_, ...), custom_call_target="tpu_custom_call" | custom-call | tf_op jit(solution)/shard_map/cond/branch_1_fun/pallas_call | solution.py:231
  43.4 2.9 %collective-permute-done.14 = bf16[1824,512]{1,0:T(8,128)(2,1)} collective-permute-done((bf16[1824,512]{1,0:T(8,128)(2,1)S(1)}, bf16[1824,512]{1,0:T(8,128)(2,1)}, u32[]{:S(2)}, u32[]{:S(2)}) %collective-permute-start.14) | collective-permute-done | bytes 1867808 | tf_op jit(solution)/shard_map/ppermute | solution.py:121
  46.3 19.9 %conditional.5 = (bf16[128,256]{1,0:T(8,128)(2,1)S(1)}, bf16[32,6144]{1,0:T(8,128)(2,1)S(1)}, f32[3072,512]{1,0:T(8,128)}, f32[3072,512]{1,0:T(8,128)}, f32[288,...) conditional(s32[]{:T(128)} %convert_element_type.29, () %tuple.37, ...), branch_computations={%region_4.0_spmd, %region_5.0_spmd} | conditional | flops 1327117 | bytes 15007822 | solution.py:126
  46.3 3.5 %collective-permute-start = (bf16[320,256]{1,0:T(8,128)(2,1)}, bf16[320,256]{1,0:T(8,128)(2,1)S(1)}, u32[]{:S(2)}, u32[]{:S(2)}) collective-permute-start(bf16[320,256]{1,0:T(8,128)(2,1)} %get-tuple-element.70), channel_id=1, source_target_pairs={{0,12},{4,0},{8,4},{12,8},{1,13},{5,1},{9,5},{13,9},{2,14},{6,2},{... | collective-permute-start | bytes 491528 | tf_op jit(solution)/shard_map/cond/branch_1_fun/ppermute | solution.py:133
  50.0 1.9 %collective-permute-start.2 = (bf16[320,256]{1,0:T(8,128)(2,1)}, bf16[320,256]{1,0:T(8,128)(2,1)S(1)}, u32[]{:S(2)}, u32[]{:S(2)}) collective-permute-start(bf16[320,256]{1,0:T(8,128)(2,1)} %get-tuple-element.72), channel_id=1, source_target_pairs={{0,4},{4,8},{8,12},{12,0},{1,5},{5,9},{9,13},{13,1},{2,6},{6,10},{... | collective-permute-start | bytes 491528 | tf_op jit(solution)/shard_map/cond/branch_1_fun/ppermute | solution.py:133
  52.0 7.5 %branch_1_fun.8 = (f32[3072,512]{1,0:T(8,128)}, f32[3072,512]{1,0:T(8,128)}) custom-call(bf16[1824,512]{1,0:T(8,128)(2,1)} %get-tuple-element.75.theirs, bf16[3072,512]{1,0:T(8,128)(2,1)} %bitcast.31, f32[3072,512]{1,0:T(8,128)} %bitcast.34, f32[3072,512]{1,0:T(8,128)} %bitcast.37), custom_call_target="tpu_custom_call" | custom-call | tf_op jit(solution)/shard_map/cond/branch_1_fun/pallas_call | solution.py:73
  59.5 3.5 %branch_1_fun.9 = bf16[1536,256]{1,0:T(8,128)(2,1)} custom-call(s32[2]{0:T(128)S(1)} %pad_add_fusion.1.place, bf16[128,6144]{1,0:T(8,128)(2,1)S(1)} %copy-done.2, bf16[64,1536]{1,0:T(8,128)(2,1)} %get-tuple-element.82.refs_0_, bf16[64,1536]{1,0:T(8,128)(2,1)} %get-tuple-element.83.refs_1_, bf16[64,1536]{1,0:T(8,128)(2,1)} %get-tuple-element.84.refs_2_, ...), custom_call_target="tpu_custom_call" | custom-call | tf_op jit(solution)/shard_map/cond/branch_1_fun/pallas_call | solution.py:231
  64.5 1.7 %branch_1_fun.7 = (bf16[128,256]{1,0:T(8,128)(2,1)S(1)}, bf16[32,6144]{1,0:T(8,128)(2,1)S(1)}) custom-call(s32[2]{0:T(128)S(1)} %pad_add_fusion.1.place, f32[128,256]{1,0:T(8,128)} %get-tuple-element.68.keys_own, bf16[128,1536]{1,0:T(8,128)(2,1)} %get-tuple-element.69.summed, bf16[320,256]{1,0:T(8,128)(2,1)S(1)} %collective-permute-done.refs_0_, ...), custom_call_target="tpu_custom_call" | custom-call | tf_op jit(solution)/shard_map/cond/branch_1_fun/pallas_call | solution.py:231
  66.2 1.6 %collective-permute-start.16 = (bf16[288,512]{1,0:T(8,128)(2,1)}, bf16[288,512]{1,0:T(8,128)(2,1)S(1)}, u32[]{:S(2)}, u32[]{:S(2)}) collective-permute-start(bf16[288,512]{1,0:T(8,128)(2,1)} %get-tuple-element.173), channel_id=1, source_target_pairs={{0,16},{16,0},{1,17},{17,1},{2,18},{18,2},{3,19},{19,3},{4,20},{20... | collective-permute-start | bytes 884744 | tf_op jit(solution)/shard_map/ppermute | solution.py:121
  67.8 4.5 %shard_map.103 = (f32[3072,512]{1,0:T(8,128)}, f32[3072,512]{1,0:T(8,128)}) custom-call(bf16[960,512]{1,0:T(8,128)(2,1)S(1)} %collective-permute-done.15.theirs, bf16[3072,512]{1,0:T(8,128)(2,1)} %bitcast.29, f32[3072,512]{1,0:T(8,128)} %bitcast.33, f32[3072,512]{1,0:T(8,128)} %bitcast.36, ...), custom_call_target="tpu_custom_call", output_to_operand_aliasing={{0}: (4, {}), {1}: (5, {})} | custom-call | tf_op jit(solution)/shard_map/pallas_call | solution.py:73
  (48 shorter events, 15.3 us)
Async XLA Ops:
  2.1 44.2 %collective-permute-start.14 = (bf16[1824,512]{1,0:T(8,128)(2,1)S(1)}, bf16[1824,512]{1,0:T(8,128)(2,1)}, u32[]{:S(2)}, u32[]{:S(2)}) collective-permute-start(bf16[1824,512]{1,0:T(8,128)(2,1)S(1)} %shard_map.102), channel_id=1, source_target_pairs={{0,16},{16,0},{1,17},{17,1},{2,18},{18,2},{3,19},{19,3},{4,20},{20... | collective-permute-start | bytes 5603336 | tf_op jit(solution)/shard_map/ppermute | solution.py:121
  5.1 7.4 %collective-permute-start.4 = (bf16[128,256]{1,0:T(8,128)(2,1)}, bf16[128,256]{1,0:T(8,128)(2,1)S(1)}, u32[]{:S(2)}, u32[]{:S(2)}) collective-permute-start(bf16[128,256]{1,0:T(8,128)(2,1)} %get-tuple-element.177), channel_id=1, source_target_pairs={{0,8},{4,12},{8,0},{12,4},{1,9},{5,13},{9,1},{13,5},{2,10},{6,14},... | collective-permute-start | bytes 196616 | tf_op jit(solution)/shard_map/cond/branch_1_fun/ppermute | solution.py:133
  7.7 6.4 %collective-permute-start.3 = (bf16[128,256]{1,0:T(8,128)(2,1)}, bf16[128,256]{1,0:T(8,128)(2,1)S(1)}, u32[]{:S(2)}, u32[]{:S(2)}) collective-permute-start(bf16[128,256]{1,0:T(8,128)(2,1)} %get-tuple-element.177), channel_id=1, source_target_pairs={{0,4},{4,8},{8,12},{12,0},{1,5},{5,9},{9,13},{13,1},{2,6},{6,10},{... | collective-permute-start | bytes 196616 | tf_op jit(solution)/shard_map/cond/branch_1_fun/ppermute | solution.py:133
  9.3 5.2 %collective-permute-start.5 = (bf16[128,256]{1,0:T(8,128)(2,1)}, bf16[128,256]{1,0:T(8,128)(2,1)S(1)}, u32[]{:S(2)}, u32[]{:S(2)}) collective-permute-start(bf16[128,256]{1,0:T(8,128)(2,1)} %get-tuple-element.177), channel_id=1, source_target_pairs={{0,12},{4,0},{8,4},{12,8},{1,13},{5,1},{9,5},{13,9},{2,14},{6,2},{... | collective-permute-start | bytes 196616 | tf_op jit(solution)/shard_map/cond/branch_1_fun/ppermute | solution.py:133
  12.5 7.6 %collective-permute-start.6 = (bf16[64,1536]{1,0:T(8,128)(2,1)S(1)}, bf16[64,1536]{1,0:T(8,128)(2,1)}, u32[]{:S(2)}, u32[]{:S(2)}) collective-permute-start(bf16[64,1536]{1,0:T(8,128)(2,1)S(1)} %dynamic_slice.16), channel_id=1, source_target_pairs={{0,4},{4,8},{8,12},{12,0},{1,5},{5,9},{9,13},{13,1},{2,6},{6,10},{... | collective-permute-start | bytes 589832 | tf_op jit(solution)/shard_map/cond/branch_1_fun/ppermute | solution.py:133
  20.1 5.8 %collective-permute-start.12 = (bf16[256,1536]{1,0:T(8,128)(2,1)S(1)}, bf16[256,1536]{1,0:T(8,128)(2,1)S(1)}, u32[]{:S(2)}, u32[]{:S(2)}) collective-permute-start(bf16[256,1536]{1,0:T(8,128)(2,1)S(1)} %get-tuple-element.60), channel_id=1, source_target_pairs={{0,1},{1,0},{2,3},{3,2},{4,5},{5,4},{6,7},{7,6},{8,9},{9,8},{10,11... | collective-permute-start | bytes 2359304 | tf_op jit(solution)/shard_map/cond/branch_1_fun/ppermute | solution.py:137
  20.1 19.4 %collective-permute-start.9 = (bf16[64,1536]{1,0:T(8,128)(2,1)}, bf16[64,1536]{1,0:T(8,128)(2,1)}, u32[]{:S(2)}, u32[]{:S(2)}) collective-permute-start(bf16[64,1536]{1,0:T(8,128)(2,1)} %get-tuple-element.57.refs_0_), channel_id=1, source_target_pairs={{0,1},{1,0},{2,3},{3,2},{4,5},{5,4},{6,7},{7,6},{8,9},{9,8},{10,11... | collective-permute-start | bytes 589832 | tf_op jit(solution)/shard_map/cond/branch_1_fun/ppermute | solution.py:137
  22.4 9.9 %collective-permute-start.8 = (bf16[64,1536]{1,0:T(8,128)(2,1)}, bf16[64,1536]{1,0:T(8,128)(2,1)}, u32[]{:S(2)}, u32[]{:S(2)}) collective-permute-start(bf16[64,1536]{1,0:T(8,128)(2,1)} %get-tuple-element.182), channel_id=1, source_target_pairs={{0,12},{4,0},{8,4},{12,8},{1,13},{5,1},{9,5},{13,9},{2,14},{6,2},{... | collective-permute-start | bytes 589832 | tf_op jit(solution)/shard_map/cond/branch_1_fun/ppermute | solution.py:133
  25.0 12.4 %collective-permute-start.7 = (bf16[64,1536]{1,0:T(8,128)(2,1)}, bf16[64,1536]{1,0:T(8,128)(2,1)}, u32[]{:S(2)}, u32[]{:S(2)}) collective-permute-start(bf16[64,1536]{1,0:T(8,128)(2,1)} %get-tuple-element.183), channel_id=1, source_target_pairs={{0,8},{4,12},{8,0},{12,4},{1,9},{5,13},{9,1},{13,5},{2,10},{6,14},... | collective-permute-start | bytes 589832 | tf_op jit(solution)/shard_map/cond/branch_1_fun/ppermute | solution.py:133
  25.9 3.4 %copy-start.3 = (bf16[256,1536]{1,0:T(8,128)(2,1)}, bf16[256,1536]{1,0:T(8,128)(2,1)S(1)}, u32[]{:S(2)}) copy-start(bf16[256,1536]{1,0:T(8,128)(2,1)S(1)} %collective-permute-done.12) | copy-start | bytes 2359300 | tf_op jit(solution)/shard_map/cond
  27.7 10.9 %collective-permute-start.13 = (bf16[128,1536]{1,0:T(8,128)(2,1)S(1)}, bf16[128,1536]{1,0:T(8,128)(2,1)S(1)}, u32[]{:S(2)}, u32[]{:S(2)}) collective-permute-start(bf16[128,1536]{1,0:T(8,128)(2,1)S(1)} %add_convert_fusion.1), channel_id=1, source_target_pairs={{0,2},{1,3},{2,0},{3,1},{4,6},{5,7},{6,4},{7,5},{8,10},{9,11},{10,... | collective-permute-start | bytes 1179656 | tf_op jit(solution)/shard_map/cond/branch_1_fun/ppermute | solution.py:137
  29.3 2.6 %copy-start = (bf16[1536,256]{1,0:T(8,128)(2,1)S(1)}, bf16[1536,256]{1,0:T(8,128)(2,1)}, u32[]{:S(2)}) copy-start(bf16[1536,256]{1,0:T(8,128)(2,1)} %get-tuple-element.58.refs_6_) | copy-start | bytes 2359300 | tf_op jit(solution)/shard_map/cond
  29.3 9.3 %copy-start.4 = (bf16[256,1536]{1,0:T(8,128)(2,1)S(1)}, bf16[256,1536]{1,0:T(8,128)(2,1)}, u32[]{:S(2)}) copy-start(bf16[256,1536]{1,0:T(8,128)(2,1)} %copy-done.3) | copy-start | bytes 2359300 | tf_op jit(solution)/shard_map/cond
  29.3 10.2 %copy-start.1 = (bf16[128,6144]{1,0:T(8,128)(2,1)S(1)}, bf16[128,6144]{1,0:T(8,128)(2,1)}, u32[]{:S(2)}) copy-start(bf16[128,6144]{1,0:T(8,128)(2,1)} %get-tuple-element.56.own) | copy-start | bytes 4718596 | tf_op jit(solution)/shard_map/cond
  32.3 7.2 %collective-permute-start.11 = (bf16[64,1536]{1,0:T(8,128)(2,1)}, bf16[64,1536]{1,0:T(8,128)(2,1)}, u32[]{:S(2)}, u32[]{:S(2)}) collective-permute-start(bf16[64,1536]{1,0:T(8,128)(2,1)} %collective-permute-done.8.refs_2_), channel_id=1, source_target_pairs={{0,1},{1,0},{2,3},{3,2},{4,5},{5,4},{6,7},{7,6},{8,9},{9,8},{10,11... | collective-permute-start | bytes 589832 | tf_op jit(solution)/shard_map/cond/branch_1_fun/ppermute | solution.py:137
  37.4 2.0 %collective-permute-start.10 = (bf16[64,1536]{1,0:T(8,128)(2,1)}, bf16[64,1536]{1,0:T(8,128)(2,1)}, u32[]{:S(2)}, u32[]{:S(2)}) collective-permute-start(bf16[64,1536]{1,0:T(8,128)(2,1)} %collective-permute-done.7.refs_1_), channel_id=1, source_target_pairs={{0,1},{1,0},{2,3},{3,2},{4,5},{5,4},{6,7},{7,6},{8,9},{9,8},{10,11... | collective-permute-start | bytes 589832 | tf_op jit(solution)/shard_map/cond/branch_1_fun/ppermute | solution.py:137
  42.9 25.0 %collective-permute-start.15 = (bf16[960,512]{1,0:T(8,128)(2,1)}, bf16[960,512]{1,0:T(8,128)(2,1)S(1)}, u32[]{:S(2)}, u32[]{:S(2)}) collective-permute-start(bf16[960,512]{1,0:T(8,128)(2,1)} %get-tuple-element.162), channel_id=1, source_target_pairs={{0,16},{16,0},{1,17},{17,1},{2,18},{18,2},{3,19},{19,3},{4,20},{20... | collective-permute-start | bytes 2949128 | tf_op jit(solution)/shard_map/ppermute | solution.py:121
  46.3 18.2 %collective-permute-start = (bf16[320,256]{1,0:T(8,128)(2,1)}, bf16[320,256]{1,0:T(8,128)(2,1)S(1)}, u32[]{:S(2)}, u32[]{:S(2)}) collective-permute-start(bf16[320,256]{1,0:T(8,128)(2,1)} %get-tuple-element.70), channel_id=1, source_target_pairs={{0,12},{4,0},{8,4},{12,8},{1,13},{5,1},{9,5},{13,9},{2,14},{6,2},{... | collective-permute-start | bytes 491528 | tf_op jit(solution)/shard_map/cond/branch_1_fun/ppermute | solution.py:133
  49.8 14.7 %collective-permute-start.1 = (bf16[320,256]{1,0:T(8,128)(2,1)}, bf16[320,256]{1,0:T(8,128)(2,1)S(1)}, u32[]{:S(2)}, u32[]{:S(2)}) collective-permute-start(bf16[320,256]{1,0:T(8,128)(2,1)} %get-tuple-element.71), channel_id=1, source_target_pairs={{0,8},{4,12},{8,0},{12,4},{1,9},{5,13},{9,1},{13,5},{2,10},{6,14},... | collective-permute-start | bytes 491528 | tf_op jit(solution)/shard_map/cond/branch_1_fun/ppermute | solution.py:133
  50.0 14.5 %collective-permute-start.2 = (bf16[320,256]{1,0:T(8,128)(2,1)}, bf16[320,256]{1,0:T(8,128)(2,1)S(1)}, u32[]{:S(2)}, u32[]{:S(2)}) collective-permute-start(bf16[320,256]{1,0:T(8,128)(2,1)} %get-tuple-element.72), channel_id=1, source_target_pairs={{0,4},{4,8},{8,12},{12,0},{1,5},{5,9},{9,13},{13,1},{2,6},{6,10},{... | collective-permute-start | bytes 491528 | tf_op jit(solution)/shard_map/cond/branch_1_fun/ppermute | solution.py:133
  52.0 7.5 %copy-start.2 = (bf16[128,6144]{1,0:T(8,128)(2,1)S(1)}, bf16[128,6144]{1,0:T(8,128)(2,1)}, u32[]{:S(2)}) copy-start(bf16[128,6144]{1,0:T(8,128)(2,1)} %get-tuple-element.81.own) | copy-start | bytes 4718596 | tf_op jit(solution)/shard_map/cond
  66.2 6.1 %copy-start.5 = (bf16[32,6144]{1,0:T(8,128)(2,1)}, bf16[32,6144]{1,0:T(8,128)(2,1)S(1)}, u32[]{:S(2)}) copy-start(bf16[32,6144]{1,0:T(8,128)(2,1)S(1)} %get-tuple-element.131) | copy-start | bytes 1179652
  66.2 6.1 %copy-start.6 = (bf16[128,256]{1,0:T(8,128)(2,1)}, bf16[128,256]{1,0:T(8,128)(2,1)S(1)}, u32[]{:S(2)}) copy-start(bf16[128,256]{1,0:T(8,128)(2,1)S(1)} %get-tuple-element.130) | copy-start | bytes 196612
  66.2 7.1 %collective-permute-start.16 = (bf16[288,512]{1,0:T(8,128)(2,1)}, bf16[288,512]{1,0:T(8,128)(2,1)S(1)}, u32[]{:S(2)}, u32[]{:S(2)}) collective-permute-start(bf16[288,512]{1,0:T(8,128)(2,1)} %get-tuple-element.173), channel_id=1, source_target_pairs={{0,16},{16,0},{1,17},{17,1},{2,18},{18,2},{3,19},{19,3},{4,20},{20... | collective-permute-start | bytes 884744 | tf_op jit(solution)/shard_map/ppermute | solution.py:121

commit v5 on v4

--- a/solution.py
+++ b/solution.py
@@ -12,7 +12,7 @@
 F32 = jnp.float32
 BF16 = jnp.bfloat16
 units = 32
-chunk_units = ((0, 19, 4), (19, 10, 2), (29, 3, None))
+chunk_units = ((0, 19, 6), (19, 10, 3), (29, 3, None))
 
 
 def nesterov(frag_sum, outer, momentum, islands):
@@ -79,7 +79,7 @@
         + [pltpu.VMEM((rows, cols), F32)] * 2
         + [pltpu.SemaphoreType.DMA((4, parts)), pltpu.SemaphoreType.DMA((2, parts))],
         input_output_aliases={4 + i: i for i in range(len(done))},
-        compiler_params=pltpu.CompilerParams(vmem_limit_bytes=32 * 1024 * 1024),
+        compiler_params=pltpu.CompilerParams(vmem_limit_bytes=(44 if done else 32) * 1024 * 1024),
         cost_estimate=pl.CostEstimate(flops=0, bytes_accessed=0, transcendentals=0),
     )(theirs, ours, outer, held, *done)
 
@@ -103,7 +103,7 @@
     shapes = [(chunk_units[k][1] * unit, cols) for k in members]
     parts = []
     for k, (rows, _) in zip(members, shapes):
-        cuts = list(range(0, rows, 5 * unit)) + [rows]
+        cuts = list(range(0, rows, 10 * unit)) + [rows]
         parts.append((chunk_units[k][0] * unit, cuts))
     copies = sum(len(cuts) - 1 for _, cuts in parts)
     return pl.pallas_call(
@@ -112,7 +112,7 @@
         out_specs=[pl.BlockSpec(memory_space=pltpu.VMEM)] * len(members),
         out_shape=[pltpu.VMEM(s, BF16) if k == 0 else jax.ShapeDtypeStruct(s, BF16) for k, s in zip(members, shapes)],
         scratch_shapes=[pltpu.SemaphoreType.DMA((copies,))],
-        compiler_params=pltpu.CompilerParams(vmem_limit_bytes=16 * 1024 * 1024),
+        compiler_params=pltpu.CompilerParams(vmem_limit_bytes=8 * 1024 * 1024),
         cost_estimate=pl.CostEstimate(flops=hint, bytes_accessed=0, transcendentals=0),
     )(ours)
 
@@ -234,7 +234,7 @@
             num_scalar_prefetch=1, grid=(1,), in_specs=columns + [whole] * len(operands), out_specs=[whole] * len(out_shape)
         ),
         out_shape=out_shape,
-        compiler_params=pltpu.CompilerParams(vmem_limit_bytes=32 * 1024 * 1024),
+        compiler_params=pltpu.CompilerParams(vmem_limit_bytes=12 * 1024 * 1024),
         cost_estimate=pl.CostEstimate(flops=flops, bytes_accessed=0, transcendentals=0),
     )(place, *first, *operands)
 

time: 75 us -> 75 us (level)
  waiting for transfers between devices: 13.7 us -> 15.4 us
  Pallas kernels: 24.4 us -> 22.7 us
    ppermute x3, waiting for transfers between devices: 3.88 us -> 4.92 us  [swapped(): return lax.ppermute(piece, 'island', [(0, 1), (1, 0)])]
    pallas_call x3, Pallas kernels: 8.49 us -> 7.59 us  [local_call(): pl.pallas_call(kernel, grid_spec=pltpu.PrefetchScalarGridSpec(num_scalar_...]
    pallas_call x2, Pallas kernels: 12 us -> 11.2 us  [update(): pl.pallas_call(functools.partial(update_kernel, islands, first, cuts), in...]
  transfers between devices with their start and end apart: 17 -> 17, of which waited for: 7 -> 8; matrix products, arithmetic and copies ran while one was open for 17% -> 17% of each run, Pallas kernels for 31% -> 29%
where the time goes in v5:
time: 75 us; the launch traced here: 74.5 us
  Pallas kernels  22.7 us (30%)
  starting transfers between devices  22 us (29%)
  waiting for transfers between devices  15.4 us (21%)
  other arithmetic  5.31 us (7%)
  local copies, waits for them, and re-layouts  4.53 us (6%)
  matrix products  3.73 us (5%)
    ppermute x9, starting transfers between devices, shifted(): return lax.ppermute(x, axis, [(i, (i + step) % n) for i in range(n)])  14.7 us
    pallas_call x2, Pallas kernels, update(): pl.pallas_call(functools.partial(update_kernel, islands, first, cuts), in...  11.2 us
    ppermute x9, waiting for transfers between devices, shifted(): return lax.ppermute(x, axis, [(i, (i + step) % n) for i in range(n)])  9.26 us
    pallas_call x3, Pallas kernels, local_call(): pl.pallas_call(kernel, grid_spec=pltpu.PrefetchScalarGridSpec(num_scalar_...  7.59 us
    ppermute x3, starting transfers between devices, swapped(): return lax.ppermute(piece, 'island', [(0, 1), (1, 0)])  5.12 us
    ppermute x3, waiting for transfers between devices, swapped(): return lax.ppermute(piece, 'island', [(0, 1), (1, 0)])  4.92 us
    pallas_call x2, Pallas kernels, pieces_of(): pl.pallas_call(functools.partial(piece_kernel, parts), in_specs=[pl.Block...  3.97 us
    dot_general x3, matrix products, part_of(): lax.dot_general(rows_of.reshape(-1, cots.shape[2]), weight, (((1,), (1,))...  3.73 us
  transfers between devices with their start and end apart: 17, of which 8 were waited for; matrix products, arithmetic and copies ran while one was open for 17% of the time, Pallas kernels for 29%

profile of v5, /device:TPU:0, one launch (start us, length us, event | category | flops | bytes accessed | tf_op | source)
XLA Modules:
  0.0 74.5 jit_solution(13006810826130146400)
XLA Ops:
  2.1 3.0 %collective-permute-start.14 = (bf16[1824,512]{1,0:T(8,128)(2,1)S(1)}, bf16[1824,512]{1,0:T(8,128)(2,1)}, u32[]{:S(2)}, u32[]{:S(2)}) collective-permute-start(bf16[1824,512]{1,0:T(8,128)(2,1)S(1)} %shard_map.102), channel_id=1, source_target_pairs={{0,16},{16,0},{1,17},{17,1},{2,18},{18,2},{3,19},{19,3},{4,20},{20... | collective-permute-start | bytes 5603336 | tf_op jit(solution)/shard_map/ppermute | solution.py:121
  5.2 15.0 %conditional.3 = (bf16[4,128,256]{2,1,0:T(8,128)(2,1)}, bf16[256,1536]{1,0:T(8,128)(2,1)S(1)}, bf16[64,1536]{1,0:T(8,128)(2,1)}) conditional(s32[]{:T(128)} %convert_element_type.29, () %tuple.39, (bf16[128,256]{1,0:T(8,128)(2,1)}, bf16[1536,256]{1,0:T(8,128)(2,1)}, bf16[128,6144]{1,0:T(8,128)(2,1)}) %tuple.58), branch_computations={%region_0.0_spmd, %region_1.0_spmd} | conditional | flops 202178576 | bytes 4719186 | solution.py:126
  5.2 2.6 %collective-permute-start.4 = (bf16[128,256]{1,0:T(8,128)(2,1)}, bf16[128,256]{1,0:T(8,128)(2,1)S(1)}, u32[]{:S(2)}, u32[]{:S(2)}) collective-permute-start(bf16[128,256]{1,0:T(8,128)(2,1)} %get-tuple-element.177), channel_id=1, source_target_pairs={{0,8},{4,12},{8,0},{12,4},{1,9},{5,13},{9,1},{13,5},{2,10},{6,14},... | collective-permute-start | bytes 196616 | tf_op jit(solution)/shard_map/cond/branch_1_fun/ppermute | solution.py:133
  7.7 1.6 %collective-permute-start.3 = (bf16[128,256]{1,0:T(8,128)(2,1)}, bf16[128,256]{1,0:T(8,128)(2,1)S(1)}, u32[]{:S(2)}, u32[]{:S(2)}) collective-permute-start(bf16[128,256]{1,0:T(8,128)(2,1)} %get-tuple-element.177), channel_id=1, source_target_pairs={{0,4},{4,8},{8,12},{12,0},{1,5},{5,9},{9,13},{13,1},{2,6},{6,10},{... | collective-permute-start | bytes 196616 | tf_op jit(solution)/shard_map/cond/branch_1_fun/ppermute | solution.py:133
  9.3 2.2 %collective-permute-start.5 = (bf16[128,256]{1,0:T(8,128)(2,1)}, bf16[128,256]{1,0:T(8,128)(2,1)S(1)}, u32[]{:S(2)}, u32[]{:S(2)}) collective-permute-start(bf16[128,256]{1,0:T(8,128)(2,1)} %get-tuple-element.177), channel_id=1, source_target_pairs={{0,12},{4,0},{8,4},{12,8},{1,13},{5,1},{9,5},{13,9},{2,14},{6,2},{... | collective-permute-start | bytes 196616 | tf_op jit(solution)/shard_map/cond/branch_1_fun/ppermute | solution.py:133
  12.6 1.6 %collective-permute-done.3 = bf16[128,256]{1,0:T(8,128)(2,1)S(1)} collective-permute-done((bf16[128,256]{1,0:T(8,128)(2,1)}, bf16[128,256]{1,0:T(8,128)(2,1)S(1)}, u32[]{:S(2)}, u32[]{:S(2)}) %collective-permute-start.3) | collective-permute-done | bytes 65568 | tf_op jit(solution)/shard_map/cond/branch_1_fun/ppermute | solution.py:133
  18.5 1.6 %collective-permute-done.6 = bf16[64,1536]{1,0:T(8,128)(2,1)} collective-permute-done((bf16[64,1536]{1,0:T(8,128)(2,1)S(1)}, bf16[64,1536]{1,0:T(8,128)(2,1)}, u32[]{:S(2)}, u32[]{:S(2)}) %collective-permute-start.6) | collective-permute-done | bytes 196640 | tf_op jit(solution)/shard_map/cond/branch_1_fun/ppermute | solution.py:133
  20.1 22.7 %conditional.4 = (bf16[64,1536]{1,0:T(8,128)(2,1)}, bf16[64,1536]{1,0:T(8,128)(2,1)}, bf16[64,1536]{1,0:T(8,128)(2,1)}, bf16[64,1536]{1,0:T(8,128)(2,1)}, bf16[6...) conditional(s32[]{:T(128)} %convert_element_type.29, () %tuple.38, ...), branch_computations={%region_2.0_spmd, %region_3.0_spmd} | conditional | flops 6202899456 | bytes 30671880 | solution.py:126
  20.6 1.8 %fusion.6 = (bf16[64,1536]{1,0:T(8,128)(2,1)}, bf16[64,1536]{1,0:T(8,128)(2,1)}) fusion(bf16[128,6144]{1,0:T(8,128)(2,1)} %get-tuple-element.56.own, s32[]{:T(128)S(6)} %select_n.23, s32[]{:T(128)S(6)} %select_n.25, s32[]{:T(128)S(6)} %select_n.24), kind=kLoop, calls=%fused_computation.21 | loop fusion | bytes 786444 | tf_op jit(solution)/shard_map/cond/branch_1_fun/dynamic_slice | solution.py:249
  22.4 2.6 %collective-permute-start.8 = (bf16[64,1536]{1,0:T(8,128)(2,1)}, bf16[64,1536]{1,0:T(8,128)(2,1)}, u32[]{:S(2)}, u32[]{:S(2)}) collective-permute-start(bf16[64,1536]{1,0:T(8,128)(2,1)} %get-tuple-element.182), channel_id=1, source_target_pairs={{0,12},{4,0},{8,4},{12,8},{1,13},{5,1},{9,5},{13,9},{2,14},{6,2},{... | collective-permute-start | bytes 589832 | tf_op jit(solution)/shard_map/cond/branch_1_fun/ppermute | solution.py:133
  25.9 1.8 %add_convert_fusion.1 = bf16[128,1536]{1,0:T(8,128)(2,1)S(1)} fusion(bf16[256,1536]{1,0:T(8,128)(2,1)S(1)} %collective-permute-done.12, bf16[128,256]{1,0:T(8,128)(2,1)S(1)} %bitcast.46, bf16[1536,256]{1,0:T(8,128)(2,1)} %get-tuple-element.58.refs_6_), kind=kOutput, calls=%fused_computation.6 | convolution fusion | flops 101253120 | bytes 1638400 | tf_op jit(solution)/shard_map/cond/branch_1_fun/dot_general | solution.py:149
  29.3 2.5 %branch_1_fun.6 = (bf16[960,512]{1,0:T(8,128)(2,1)}, bf16[288,512]{1,0:T(8,128)(2,1)}) custom-call(bf16[3072,512]{1,0:T(8,128)(2,1)} %bitcast.30), custom_call_target="tpu_custom_call" | custom-call | flops 6000000000 | tf_op jit(solution)/shard_map/cond/branch_1_fun/pallas_call | solution.py:109
  32.4 5.1 %collective-permute-done.7.refs_1_ = bf16[64,1536]{1,0:T(8,128)(2,1)} collective-permute-done((bf16[64,1536]{1,0:T(8,128)(2,1)}, bf16[64,1536]{1,0:T(8,128)(2,1)}, u32[]{:S(2)}, u32[]{:S(2)}) %collective-permute-start.7) | collective-permute-done | bytes 196640 | tf_op jit(solution)/shard_map/cond/branch_1_fun/ppermute | solution.py:133
  39.5 3.3 %branch_1_fun.5 = (f32[128,256]{1,0:T(8,128)}, bf16[320,256]{1,0:T(8,128)(2,1)}, bf16[320,256]{1,0:T(8,128)(2,1)}, bf16[320,256]{1,0:T(8,128)(2,1)}) custom-call(s32[2]{0:T(128)S(1)} %pad_add_fusion.place, bf16[128,6144]{1,0:T(8,128)(2,1)S(1)} %copy-done.1, bf16[64,1536]{1,0:T(8,128)(2,1)} %get-tuple-element.57.refs_0_, ...), custom_call_target="tpu_custom_call" | custom-call | tf_op jit(solution)/shard_map/cond/branch_1_fun/pallas_call | solution.py:231
  43.3 2.9 %collective-permute-done.14 = bf16[1824,512]{1,0:T(8,128)(2,1)} collective-permute-done((bf16[1824,512]{1,0:T(8,128)(2,1)S(1)}, bf16[1824,512]{1,0:T(8,128)(2,1)}, u32[]{:S(2)}, u32[]{:S(2)}) %collective-permute-start.14) | collective-permute-done | bytes 1867808 | tf_op jit(solution)/shard_map/ppermute | solution.py:121
  46.3 19.4 %conditional.5 = (bf16[128,256]{1,0:T(8,128)(2,1)S(1)}, bf16[32,6144]{1,0:T(8,128)(2,1)S(1)}, f32[3072,512]{1,0:T(8,128)}, f32[3072,512]{1,0:T(8,128)}, f32[288,...) conditional(s32[]{:T(128)} %convert_element_type.29, () %tuple.37, ...), branch_computations={%region_4.0_spmd, %region_5.0_spmd} | conditional | flops 1327117 | bytes 15007822 | solution.py:126
  46.3 3.5 %collective-permute-start = (bf16[320,256]{1,0:T(8,128)(2,1)}, bf16[320,256]{1,0:T(8,128)(2,1)S(1)}, u32[]{:S(2)}, u32[]{:S(2)}) collective-permute-start(bf16[320,256]{1,0:T(8,128)(2,1)} %get-tuple-element.70), channel_id=1, source_target_pairs={{0,12},{4,0},{8,4},{12,8},{1,13},{5,1},{9,5},{13,9},{2,14},{6,2},{... | collective-permute-start | bytes 491528 | tf_op jit(solution)/shard_map/cond/branch_1_fun/ppermute | solution.py:133
  50.1 1.9 %collective-permute-start.2 = (bf16[320,256]{1,0:T(8,128)(2,1)}, bf16[320,256]{1,0:T(8,128)(2,1)S(1)}, u32[]{:S(2)}, u32[]{:S(2)}) collective-permute-start(bf16[320,256]{1,0:T(8,128)(2,1)} %get-tuple-element.72), channel_id=1, source_target_pairs={{0,4},{4,8},{8,12},{12,0},{1,5},{5,9},{9,13},{13,1},{2,6},{6,10},{... | collective-permute-start | bytes 491528 | tf_op jit(solution)/shard_map/cond/branch_1_fun/ppermute | solution.py:133
  52.0 7.2 %branch_1_fun.8 = (f32[3072,512]{1,0:T(8,128)}, f32[3072,512]{1,0:T(8,128)}) custom-call(bf16[1824,512]{1,0:T(8,128)(2,1)} %get-tuple-element.75.theirs, bf16[3072,512]{1,0:T(8,128)(2,1)} %bitcast.31, f32[3072,512]{1,0:T(8,128)} %bitcast.34, f32[3072,512]{1,0:T(8,128)} %bitcast.37), custom_call_target="tpu_custom_call" | custom-call | tf_op jit(solution)/shard_map/cond/branch_1_fun/pallas_call | solution.py:73
  59.3 2.6 %branch_1_fun.9 = bf16[1536,256]{1,0:T(8,128)(2,1)S(1)} custom-call(s32[2]{0:T(128)S(1)} %pad_add_fusion.1.place, bf16[128,6144]{1,0:T(8,128)(2,1)S(1)} %copy-done.2, bf16[64,1536]{1,0:T(8,128)(2,1)} %get-tuple-element.82.refs_0_, bf16[64,1536]{1,0:T(8,128)(2,1)} %get-tuple-element.83.refs_1_, bf16[64,1536]{1,0:T(8,128)(2,1)} %get-tuple-element.84.refs_2_, ...), custom_call_target="tpu_custom_call" | custom-call | tf_op jit(solution)/shard_map/cond/branch_1_fun/pallas_call | solution.py:231
  64.0 1.7 %branch_1_fun.7 = (bf16[128,256]{1,0:T(8,128)(2,1)S(1)}, bf16[32,6144]{1,0:T(8,128)(2,1)S(1)}) custom-call(s32[2]{0:T(128)S(1)} %pad_add_fusion.1.place, f32[128,256]{1,0:T(8,128)} %get-tuple-element.68.keys_own, bf16[128,1536]{1,0:T(8,128)(2,1)} %get-tuple-element.69.summed, bf16[320,256]{1,0:T(8,128)(2,1)S(1)} %collective-permute-done.refs_0_, ...), custom_call_target="tpu_custom_call" | custom-call | tf_op jit(solution)/shard_map/cond/branch_1_fun/pallas_call | solution.py:231
  65.7 1.6 %collective-permute-start.16 = (bf16[288,512]{1,0:T(8,128)(2,1)}, bf16[288,512]{1,0:T(8,128)(2,1)S(1)}, u32[]{:S(2)}, u32[]{:S(2)}) collective-permute-start(bf16[288,512]{1,0:T(8,128)(2,1)} %get-tuple-element.173), channel_id=1, source_target_pairs={{0,16},{16,0},{1,17},{17,1},{2,18},{18,2},{3,19},{19,3},{4,20},{20... | collective-permute-start | bytes 884744 | tf_op jit(solution)/shard_map/ppermute | solution.py:121
  67.3 4.0 %shard_map.103 = (f32[3072,512]{1,0:T(8,128)}, f32[3072,512]{1,0:T(8,128)}) custom-call(bf16[960,512]{1,0:T(8,128)(2,1)S(1)} %collective-permute-done.15.theirs, bf16[3072,512]{1,0:T(8,128)(2,1)} %bitcast.29, f32[3072,512]{1,0:T(8,128)} %bitcast.33, f32[3072,512]{1,0:T(8,128)} %bitcast.36, ...), custom_call_target="tpu_custom_call", output_to_operand_aliasing={{0}: (4, {}), {1}: (5, {})} | custom-call | tf_op jit(solution)/shard_map/pallas_call | solution.py:73
  71.3 2.0 %collective-permute-done.16 = bf16[288,512]{1,0:T(8,128)(2,1)S(1)} collective-permute-done((bf16[288,512]{1,0:T(8,128)(2,1)}, bf16[288,512]{1,0:T(8,128)(2,1)S(1)}, u32[]{:S(2)}, u32[]{:S(2)}) %collective-permute-start.16) | collective-permute-done | bytes 294944 | tf_op jit(solution)/shard_map/ppermute | solution.py:121
  (50 shorter events, 16.5 us)
Async XLA Ops:
  2.1 44.2 %collective-permute-start.14 = (bf16[1824,512]{1,0:T(8,128)(2,1)S(1)}, bf16[1824,512]{1,0:T(8,128)(2,1)}, u32[]{:S(2)}, u32[]{:S(2)}) collective-permute-start(bf16[1824,512]{1,0:T(8,128)(2,1)S(1)} %shard_map.102), channel_id=1, source_target_pairs={{0,16},{16,0},{1,17},{17,1},{2,18},{18,2},{3,19},{19,3},{4,20},{20... | collective-permute-start | bytes 5603336 | tf_op jit(solution)/shard_map/ppermute | solution.py:121
  5.2 7.4 %collective-permute-start.4 = (bf16[128,256]{1,0:T(8,128)(2,1)}, bf16[128,256]{1,0:T(8,128)(2,1)S(1)}, u32[]{:S(2)}, u32[]{:S(2)}) collective-permute-start(bf16[128,256]{1,0:T(8,128)(2,1)} %get-tuple-element.177), channel_id=1, source_target_pairs={{0,8},{4,12},{8,0},{12,4},{1,9},{5,13},{9,1},{13,5},{2,10},{6,14},... | collective-permute-start | bytes 196616 | tf_op jit(solution)/shard_map/cond/branch_1_fun/ppermute | solution.py:133
  7.7 6.4 %collective-permute-start.3 = (bf16[128,256]{1,0:T(8,128)(2,1)}, bf16[128,256]{1,0:T(8,128)(2,1)S(1)}, u32[]{:S(2)}, u32[]{:S(2)}) collective-permute-start(bf16[128,256]{1,0:T(8,128)(2,1)} %get-tuple-element.177), channel_id=1, source_target_pairs={{0,4},{4,8},{8,12},{12,0},{1,5},{5,9},{9,13},{13,1},{2,6},{6,10},{... | collective-permute-start | bytes 196616 | tf_op jit(solution)/shard_map/cond/branch_1_fun/ppermute | solution.py:133
  9.3 5.2 %collective-permute-start.5 = (bf16[128,256]{1,0:T(8,128)(2,1)}, bf16[128,256]{1,0:T(8,128)(2,1)S(1)}, u32[]{:S(2)}, u32[]{:S(2)}) collective-permute-start(bf16[128,256]{1,0:T(8,128)(2,1)} %get-tuple-element.177), channel_id=1, source_target_pairs={{0,12},{4,0},{8,4},{12,8},{1,13},{5,1},{9,5},{13,9},{2,14},{6,2},{... | collective-permute-start | bytes 196616 | tf_op jit(solution)/shard_map/cond/branch_1_fun/ppermute | solution.py:133
  12.5 7.6 %collective-permute-start.6 = (bf16[64,1536]{1,0:T(8,128)(2,1)S(1)}, bf16[64,1536]{1,0:T(8,128)(2,1)}, u32[]{:S(2)}, u32[]{:S(2)}) collective-permute-start(bf16[64,1536]{1,0:T(8,128)(2,1)S(1)} %dynamic_slice.16), channel_id=1, source_target_pairs={{0,4},{4,8},{8,12},{12,0},{1,5},{5,9},{9,13},{13,1},{2,6},{6,10},{... | collective-permute-start | bytes 589832 | tf_op jit(solution)/shard_map/cond/branch_1_fun/ppermute | solution.py:133
  20.1 5.8 %collective-permute-start.12 = (bf16[256,1536]{1,0:T(8,128)(2,1)S(1)}, bf16[256,1536]{1,0:T(8,128)(2,1)S(1)}, u32[]{:S(2)}, u32[]{:S(2)}) collective-permute-start(bf16[256,1536]{1,0:T(8,128)(2,1)S(1)} %get-tuple-element.60), channel_id=1, source_target_pairs={{0,1},{1,0},{2,3},{3,2},{4,5},{5,4},{6,7},{7,6},{8,9},{9,8},{10,11... | collective-permute-start | bytes 2359304 | tf_op jit(solution)/shard_map/cond/branch_1_fun/ppermute | solution.py:137
  20.1 19.3 %collective-permute-start.9 = (bf16[64,1536]{1,0:T(8,128)(2,1)}, bf16[64,1536]{1,0:T(8,128)(2,1)}, u32[]{:S(2)}, u32[]{:S(2)}) collective-permute-start(bf16[64,1536]{1,0:T(8,128)(2,1)} %get-tuple-element.57.refs_0_), channel_id=1, source_target_pairs={{0,1},{1,0},{2,3},{3,2},{4,5},{5,4},{6,7},{7,6},{8,9},{9,8},{10,11... | collective-permute-start | bytes 589832 | tf_op jit(solution)/shard_map/cond/branch_1_fun/ppermute | solution.py:137
  22.4 9.8 %collective-permute-start.8 = (bf16[64,1536]{1,0:T(8,128)(2,1)}, bf16[64,1536]{1,0:T(8,128)(2,1)}, u32[]{:S(2)}, u32[]{:S(2)}) collective-permute-start(bf16[64,1536]{1,0:T(8,128)(2,1)} %get-tuple-element.182), channel_id=1, source_target_pairs={{0,12},{4,0},{8,4},{12,8},{1,13},{5,1},{9,5},{13,9},{2,14},{6,2},{... | collective-permute-start | bytes 589832 | tf_op jit(solution)/shard_map/cond/branch_1_fun/ppermute | solution.py:133
  25.0 12.4 %collective-permute-start.7 = (bf16[64,1536]{1,0:T(8,128)(2,1)}, bf16[64,1536]{1,0:T(8,128)(2,1)}, u32[]{:S(2)}, u32[]{:S(2)}) collective-permute-start(bf16[64,1536]{1,0:T(8,128)(2,1)} %get-tuple-element.183), channel_id=1, source_target_pairs={{0,8},{4,12},{8,0},{12,4},{1,9},{5,13},{9,1},{13,5},{2,10},{6,14},... | collective-permute-start | bytes 589832 | tf_op jit(solution)/shard_map/cond/branch_1_fun/ppermute | solution.py:133
  25.9 3.4 %copy-start.4 = (bf16[256,1536]{1,0:T(8,128)(2,1)}, bf16[256,1536]{1,0:T(8,128)(2,1)S(1)}, u32[]{:S(2)}) copy-start(bf16[256,1536]{1,0:T(8,128)(2,1)S(1)} %collective-permute-done.12) | copy-start | bytes 2359300 | tf_op jit(solution)/shard_map/cond
  27.7 10.9 %collective-permute-start.13 = (bf16[128,1536]{1,0:T(8,128)(2,1)S(1)}, bf16[128,1536]{1,0:T(8,128)(2,1)S(1)}, u32[]{:S(2)}, u32[]{:S(2)}) collective-permute-start(bf16[128,1536]{1,0:T(8,128)(2,1)S(1)} %add_convert_fusion.1), channel_id=1, source_target_pairs={{0,2},{1,3},{2,0},{3,1},{4,6},{5,7},{6,4},{7,5},{8,10},{9,11},{10,... | collective-permute-start | bytes 1179656 | tf_op jit(solution)/shard_map/cond/branch_1_fun/ppermute | solution.py:137
  29.3 2.6 %copy-start = (bf16[1536,256]{1,0:T(8,128)(2,1)S(1)}, bf16[1536,256]{1,0:T(8,128)(2,1)}, u32[]{:S(2)}) copy-start(bf16[1536,256]{1,0:T(8,128)(2,1)} %get-tuple-element.58.refs_6_) | copy-start | bytes 2359300 | tf_op jit(solution)/shard_map/cond
  29.3 9.3 %copy-start.5 = (bf16[256,1536]{1,0:T(8,128)(2,1)S(1)}, bf16[256,1536]{1,0:T(8,128)(2,1)}, u32[]{:S(2)}) copy-start(bf16[256,1536]{1,0:T(8,128)(2,1)} %copy-done.4) | copy-start | bytes 2359300 | tf_op jit(solution)/shard_map/cond
  29.3 10.2 %copy-start.1 = (bf16[128,6144]{1,0:T(8,128)(2,1)S(1)}, bf16[128,6144]{1,0:T(8,128)(2,1)}, u32[]{:S(2)}) copy-start(bf16[128,6144]{1,0:T(8,128)(2,1)} %get-tuple-element.56.own) | copy-start | bytes 4718596 | tf_op jit(solution)/shard_map/cond
  32.3 7.2 %collective-permute-start.11 = (bf16[64,1536]{1,0:T(8,128)(2,1)}, bf16[64,1536]{1,0:T(8,128)(2,1)}, u32[]{:S(2)}, u32[]{:S(2)}) collective-permute-start(bf16[64,1536]{1,0:T(8,128)(2,1)} %collective-permute-done.8.refs_2_), channel_id=1, source_target_pairs={{0,1},{1,0},{2,3},{3,2},{4,5},{5,4},{6,7},{7,6},{8,9},{9,8},{10,11... | collective-permute-start | bytes 589832 | tf_op jit(solution)/shard_map/cond/branch_1_fun/ppermute | solution.py:137
  37.5 2.0 %collective-permute-start.10 = (bf16[64,1536]{1,0:T(8,128)(2,1)}, bf16[64,1536]{1,0:T(8,128)(2,1)}, u32[]{:S(2)}, u32[]{:S(2)}) collective-permute-start(bf16[64,1536]{1,0:T(8,128)(2,1)} %collective-permute-done.7.refs_1_), channel_id=1, source_target_pairs={{0,1},{1,0},{2,3},{3,2},{4,5},{5,4},{6,7},{7,6},{8,9},{9,8},{10,11... | collective-permute-start | bytes 589832 | tf_op jit(solution)/shard_map/cond/branch_1_fun/ppermute | solution.py:137
  42.8 24.5 %collective-permute-start.15 = (bf16[960,512]{1,0:T(8,128)(2,1)}, bf16[960,512]{1,0:T(8,128)(2,1)S(1)}, u32[]{:S(2)}, u32[]{:S(2)}) collective-permute-start(bf16[960,512]{1,0:T(8,128)(2,1)} %get-tuple-element.162), channel_id=1, source_target_pairs={{0,16},{16,0},{1,17},{17,1},{2,18},{18,2},{3,19},{19,3},{4,20},{20... | collective-permute-start | bytes 2949128 | tf_op jit(solution)/shard_map/ppermute | solution.py:121
  46.3 17.1 %collective-permute-start = (bf16[320,256]{1,0:T(8,128)(2,1)}, bf16[320,256]{1,0:T(8,128)(2,1)S(1)}, u32[]{:S(2)}, u32[]{:S(2)}) collective-permute-start(bf16[320,256]{1,0:T(8,128)(2,1)} %get-tuple-element.70), channel_id=1, source_target_pairs={{0,12},{4,0},{8,4},{12,8},{1,13},{5,1},{9,5},{13,9},{2,14},{6,2},{... | collective-permute-start | bytes 491528 | tf_op jit(solution)/shard_map/cond/branch_1_fun/ppermute | solution.py:133
  49.8 14.2 %collective-permute-start.1 = (bf16[320,256]{1,0:T(8,128)(2,1)}, bf16[320,256]{1,0:T(8,128)(2,1)S(1)}, u32[]{:S(2)}, u32[]{:S(2)}) collective-permute-start(bf16[320,256]{1,0:T(8,128)(2,1)} %get-tuple-element.71), channel_id=1, source_target_pairs={{0,8},{4,12},{8,0},{12,4},{1,9},{5,13},{9,1},{13,5},{2,10},{6,14},... | collective-permute-start | bytes 491528 | tf_op jit(solution)/shard_map/cond/branch_1_fun/ppermute | solution.py:133
  50.1 14.0 %collective-permute-start.2 = (bf16[320,256]{1,0:T(8,128)(2,1)}, bf16[320,256]{1,0:T(8,128)(2,1)S(1)}, u32[]{:S(2)}, u32[]{:S(2)}) collective-permute-start(bf16[320,256]{1,0:T(8,128)(2,1)} %get-tuple-element.72), channel_id=1, source_target_pairs={{0,4},{4,8},{8,12},{12,0},{1,5},{5,9},{9,13},{13,1},{2,6},{6,10},{... | collective-permute-start | bytes 491528 | tf_op jit(solution)/shard_map/cond/branch_1_fun/ppermute | solution.py:133
  52.0 7.2 %copy-start.2 = (bf16[128,6144]{1,0:T(8,128)(2,1)S(1)}, bf16[128,6144]{1,0:T(8,128)(2,1)}, u32[]{:S(2)}) copy-start(bf16[128,6144]{1,0:T(8,128)(2,1)} %get-tuple-element.81.own) | copy-start | bytes 4718596 | tf_op jit(solution)/shard_map/cond
  65.7 5.6 %copy-start.6 = (bf16[32,6144]{1,0:T(8,128)(2,1)}, bf16[32,6144]{1,0:T(8,128)(2,1)S(1)}, u32[]{:S(2)}) copy-start(bf16[32,6144]{1,0:T(8,128)(2,1)S(1)} %get-tuple-element.131) | copy-start | bytes 1179652
  65.7 5.6 %copy-start.7 = (bf16[128,256]{1,0:T(8,128)(2,1)}, bf16[128,256]{1,0:T(8,128)(2,1)S(1)}, u32[]{:S(2)}) copy-start(bf16[128,256]{1,0:T(8,128)(2,1)S(1)} %get-tuple-element.130) | copy-start | bytes 196612
  65.7 7.6 %collective-permute-start.16 = (bf16[288,512]{1,0:T(8,128)(2,1)}, bf16[288,512]{1,0:T(8,128)(2,1)S(1)}, u32[]{:S(2)}, u32[]{:S(2)}) collective-permute-start(bf16[288,512]{1,0:T(8,128)(2,1)} %get-tuple-element.173), channel_id=1, source_target_pairs={{0,16},{16,0},{1,17},{17,1},{2,18},{18,2},{3,19},{19,3},{4,20},{20... | collective-permute-start | bytes 884744 | tf_op jit(solution)/shard_map/ppermute | solution.py:121
  (1 other events, 1.6 us)

commit v6 on v5

--- a/solution.py
+++ b/solution.py
@@ -12,7 +12,8 @@
 F32 = jnp.float32
 BF16 = jnp.bfloat16
 units = 32
-chunk_units = ((0, 19, 6), (19, 10, 3), (29, 3, None))
+late_parts = 2
+chunk_units = ((0, 19, 6), (19, 9, 3), (28, 2, None), (30, 2, None))
 
 
 def nesterov(frag_sum, outer, momentum, islands):
@@ -55,11 +56,36 @@
     return nesterov(ours.astype(F32), outer, held, lax.axis_size("island"))
 
 
-def last_update(theirs, terms, done):
-    share = theirs.astype(F32) / lax.axis_size("island")
-    results = terms[0] + outer_rate * (1 + beta_outer) * share, terms[1] - share
-    first = done[0].shape[0] - theirs.shape[0]
-    return [lax.dynamic_update_slice(whole, part, (first, 0)) for whole, part in zip(done, results)]
+def late_kernel(islands, first, cuts, theirs, outer_terms, momentum_terms, *refs):
+    new_outer, new_momentum, outer_rows, momentum_rows, stores = refs[-5:]
+    leaving = []
+    for k, (top, bottom) in enumerate(zip(cuts, cuts[1:])):
+        rows, there = slice(top, bottom), pl.ds(first + top, bottom - top)
+        share = theirs[rows].astype(F32) / islands
+        outer_rows[rows] = outer_terms[rows] + outer_rate * (1 + beta_outer) * share
+        momentum_rows[rows] = momentum_terms[rows] - share
+        for i, (buffer, out) in enumerate(((outer_rows, new_outer), (momentum_rows, new_momentum))):
+            leaving.append(pltpu.make_async_copy(buffer.at[pl.ds(top, bottom - top)], out.at[there], stores.at[i, k]))
+            leaving[-1].start()
+    for copy in leaving:
+        copy.wait()
+
+
+def late_update(k, theirs, terms, done):
+    rows, cols = theirs.shape
+    first = chunk_units[k][0] * (done[0].shape[0] // units)
+    cuts = [rows * i // late_parts // 16 * 16 for i in range(late_parts)] + [rows]
+    hbm, vmem = pl.BlockSpec(memory_space=pltpu.HBM), pl.BlockSpec(memory_space=pltpu.VMEM)
+    return pl.pallas_call(
+        functools.partial(late_kernel, lax.axis_size("island"), first, cuts),
+        in_specs=[vmem] * 3 + [hbm] * 2,
+        out_specs=[hbm] * 2,
+        out_shape=[jax.ShapeDtypeStruct(a.shape, F32) for a in done],
+        scratch_shapes=[pltpu.VMEM((rows, cols), F32)] * 2 + [pltpu.SemaphoreType.DMA((2, late_parts))],
+        input_output_aliases={3: 0, 4: 1},
+        compiler_params=pltpu.CompilerParams(vmem_limit_bytes=44 * 1024 * 1024),
+        cost_estimate=pl.CostEstimate(flops=0, bytes_accessed=0, transcendentals=0),
+    )(theirs, *terms, *done)
 
 
 def update(k, theirs, local_frag, outer_frag, momentum, done):
@@ -306,25 +332,29 @@
     theirs = [swapped(*pieces_of(local_frag, [0]))]
     cots, part, mine = together(gather, tokens, weight, key_cotangent)
 
+    late = range(2, len(chunk_units))
+
     def step_two(cots, part, mine, tokens, weight, local_frag):
         return combine(cots, part, mine, tokens, weight), pieces_of(local_frag, range(1, len(chunk_units)), hint=6 * 10**9)
 
     state, pieces = together(step_two, cots, part, mine, tokens, weight, local_frag)
-    theirs.append(swapped(pieces[0]))
+    theirs += [swapped(piece) for piece in pieces[:-1]]
     theirs[0], state = lax.optimization_barrier((theirs[0], state))
 
     def step_three(theirs, cots, mine, state, tokens, weight, *frag):
-        return finish(cots, mine, *state, tokens, weight), update(0, theirs, *frag, ()), own_terms(2, *frag)
+        return finish(cots, mine, *state, tokens, weight), update(0, theirs, *frag, ()), [own_terms(k, *frag) for k in late]
 
     results, done, terms = together(
         step_three, theirs[0], cots, mine, state, tokens, weight, local_frag, outer_frag, momentum
     )
     keys, input_grad, weight_grad = results
-    piece, done = lax.optimization_barrier((pieces[1], done))
+    piece, done = lax.optimization_barrier((pieces[-1], done))
     theirs.append(swapped(piece))
     theirs[1], done = lax.optimization_barrier((theirs[1], done))
     done = update(1, theirs[1], local_frag, outer_frag, momentum, done)
-    done = last_update(theirs[2], terms, done)
+    for k in late:
+        theirs[k], done = lax.optimization_barrier((theirs[k], done))
+        done = late_update(k, theirs[k], terms[k - late[0]], done)
     new_outer, new_momentum = (a.reshape(outer_frag.shape) for a in done)
     return (keys, input_grad, weight_grad[None], new_outer, new_momentum)
 

time: 75 us -> 74.7 us (level)
  waiting for transfers between devices: 15.4 us -> 12.2 us
  Pallas kernels: 22.7 us -> 25.1 us
  starting transfers between devices: 22 us -> 23.5 us
  other arithmetic: 5.31 us -> 4.37 us
    ppermute x3 -> x4, waiting for transfers between devices: 4.92 us -> 1.99 us  [swapped(): return lax.ppermute(piece, 'island', [(0, 1), (1, 0)])]
    pallas_call x0 -> x2, Pallas kernels: none -> 1.87 us  [late_update(): pl.pallas_call(functools.partial(late_kernel, lax.axis_size('island'), fi...]
    ppermute x3 -> x4, starting transfers between devices: 5.12 us -> 6.58 us  [swapped(): return lax.ppermute(piece, 'island', [(0, 1), (1, 0)])]
    dynamic_update_slice x1 -> x0, other arithmetic: 1.19 us -> none  [last_update(): lax.dynamic_update_slice(whole, part, (first, 0))]
    pallas_call x3, Pallas kernels: 7.59 us -> 8.35 us  [local_call(): pl.pallas_call(kernel, grid_spec=pltpu.PrefetchScalarGridSpec(num_scalar_...]
  transfers between devices with their start and end apart: 17 -> 18, of which waited for: 8 -> 8; matrix products, arithmetic and copies ran while one was open for 17% -> 17% of each run, Pallas kernels for 29% -> 31%
where the time goes in v6:
time: 74.7 us; the launch traced here: 74.2 us
  Pallas kernels  25.1 us (34%)
  starting transfers between devices  23.5 us (31%)
  waiting for transfers between devices  12.2 us (16%)
  local copies, waits for them, and re-layouts  4.52 us (6%)
  other arithmetic  4.37 us (6%)
  matrix products  3.73 us (5%)
    ppermute x9, starting transfers between devices, shifted(): return lax.ppermute(x, axis, [(i, (i + step) % n) for i in range(n)])  14.7 us
    pallas_call x2, Pallas kernels, update(): pl.pallas_call(functools.partial(update_kernel, islands, first, cuts), in...  10.9 us
    ppermute x9, waiting for transfers between devices, shifted(): return lax.ppermute(x, axis, [(i, (i + step) % n) for i in range(n)])  9.01 us
    pallas_call x3, Pallas kernels, local_call(): pl.pallas_call(kernel, grid_spec=pltpu.PrefetchScalarGridSpec(num_scalar_...  8.35 us
    ppermute x4, starting transfers between devices, swapped(): return lax.ppermute(piece, 'island', [(0, 1), (1, 0)])  6.58 us
    pallas_call x2, Pallas kernels, pieces_of(): pl.pallas_call(functools.partial(piece_kernel, parts), in_specs=[pl.Block...  3.97 us
    dot_general x3, matrix products, part_of(): lax.dot_general(rows_of.reshape(-1, cots.shape[2]), weight, (((1,), (1,))...  3.73 us
    dynamic_slice x2, local copies, waits for them, and re-layouts, columns_for(): lax.dynamic_slice(tokens, (core * half, lax.rem(me + s, lax.axis_size('fs...  2.73 us
  transfers between devices with their start and end apart: 18, of which 8 were waited for; matrix products, arithmetic and copies ran while one was open for 17% of the time, Pallas kernels for 31%

profile of v6, /device:TPU:0, one launch (start us, length us, event | category | flops | bytes accessed | tf_op | source)
XLA Modules:
  0.0 74.2 jit_solution(10227262846927327007)
XLA Ops:
  2.1 3.0 %collective-permute-start.14 = (bf16[1824,512]{1,0:T(8,128)(2,1)S(1)}, bf16[1824,512]{1,0:T(8,128)(2,1)}, u32[]{:S(2)}, u32[]{:S(2)}) collective-permute-start(bf16[1824,512]{1,0:T(8,128)(2,1)S(1)} %shard_map.102), channel_id=1, source_target_pairs={{0,16},{16,0},{1,17},{17,1},{2,18},{18,2},{3,19},{19,3},{4,20},{20... | collective-permute-start | bytes 5603336 | tf_op jit(solution)/shard_map/ppermute | solution.py:147
  5.2 15.0 %conditional.3 = (bf16[4,128,256]{2,1,0:T(8,128)(2,1)}, bf16[256,1536]{1,0:T(8,128)(2,1)S(1)}, bf16[64,1536]{1,0:T(8,128)(2,1)}) conditional(s32[]{:T(128)} %convert_element_type.29, () %tuple.41, (bf16[128,256]{1,0:T(8,128)(2,1)}, bf16[1536,256]{1,0:T(8,128)(2,1)}, bf16[128,6144]{1,0:T(8,128)(2,1)}) %tuple.64), branch_computations={%region_0.0_spmd, %region_1.0_spmd} | conditional | flops 202178576 | bytes 4719186 | solution.py:152
  5.2 2.6 %collective-permute-start.4 = (bf16[128,256]{1,0:T(8,128)(2,1)}, bf16[128,256]{1,0:T(8,128)(2,1)S(1)}, u32[]{:S(2)}, u32[]{:S(2)}) collective-permute-start(bf16[128,256]{1,0:T(8,128)(2,1)} %get-tuple-element.204), channel_id=1, source_target_pairs={{0,8},{4,12},{8,0},{12,4},{1,9},{5,13},{9,1},{13,5},{2,10},{6,14},... | collective-permute-start | bytes 196616 | tf_op jit(solution)/shard_map/cond/branch_1_fun/ppermute | solution.py:159
  7.7 1.6 %collective-permute-start.3 = (bf16[128,256]{1,0:T(8,128)(2,1)}, bf16[128,256]{1,0:T(8,128)(2,1)S(1)}, u32[]{:S(2)}, u32[]{:S(2)}) collective-permute-start(bf16[128,256]{1,0:T(8,128)(2,1)} %get-tuple-element.204), channel_id=1, source_target_pairs={{0,4},{4,8},{8,12},{12,0},{1,5},{5,9},{9,13},{13,1},{2,6},{6,10},{... | collective-permute-start | bytes 196616 | tf_op jit(solution)/shard_map/cond/branch_1_fun/ppermute | solution.py:159
  9.3 2.2 %collective-permute-start.5 = (bf16[128,256]{1,0:T(8,128)(2,1)}, bf16[128,256]{1,0:T(8,128)(2,1)S(1)}, u32[]{:S(2)}, u32[]{:S(2)}) collective-permute-start(bf16[128,256]{1,0:T(8,128)(2,1)} %get-tuple-element.204), channel_id=1, source_target_pairs={{0,12},{4,0},{8,4},{12,8},{1,13},{5,1},{9,5},{13,9},{2,14},{6,2},{... | collective-permute-start | bytes 196616 | tf_op jit(solution)/shard_map/cond/branch_1_fun/ppermute | solution.py:159
  12.6 1.6 %collective-permute-done.3 = bf16[128,256]{1,0:T(8,128)(2,1)S(1)} collective-permute-done((bf16[128,256]{1,0:T(8,128)(2,1)}, bf16[128,256]{1,0:T(8,128)(2,1)S(1)}, u32[]{:S(2)}, u32[]{:S(2)}) %collective-permute-start.3) | collective-permute-done | bytes 65568 | tf_op jit(solution)/shard_map/cond/branch_1_fun/ppermute | solution.py:159
  14.5 1.6 %pad_maximum_fusion = bf16[4,128,256]{2,1,0:T(8,128)(2,1)} fusion(bf16[1,128,256]{2,1,0:T(8,128)(2,1)S(1)} %bitcast.50, bf16[1,128,256]{2,1,0:T(8,128)(2,1)S(1)} %bitcast.48, bf16[1,128,256]{2,1,0:T(8,128)(2,1)S(1)} %bitcast.49, bf16[1,128,256]{2,1,0:T(8,128)(2,1)} %bitcast.47), kind=kLoop, calls=%fused_computation.1 | loop fusion | flops 393216 | bytes 524288 | tf_op jit(solution)/shard_map/cond/branch_1_fun/stack | solution.py:279
  18.5 1.6 %collective-permute-done.6 = bf16[64,1536]{1,0:T(8,128)(2,1)} collective-permute-done((bf16[64,1536]{1,0:T(8,128)(2,1)S(1)}, bf16[64,1536]{1,0:T(8,128)(2,1)}, u32[]{:S(2)}, u32[]{:S(2)}) %collective-permute-start.6) | collective-permute-done | bytes 196640 | tf_op jit(solution)/shard_map/cond/branch_1_fun/ppermute | solution.py:159
  20.1 22.7 %conditional.4 = (bf16[64,1536]{1,0:T(8,128)(2,1)}, bf16[64,1536]{1,0:T(8,128)(2,1)}, bf16[64,1536]{1,0:T(8,128)(2,1)}, bf16[64,1536]{1,0:T(8,128)(2,1)}, bf16[6...) conditional(s32[]{:T(128)} %convert_element_type.29, () %tuple.40, ...), branch_computations={%region_2.0_spmd, %region_3.0_spmd} | conditional | flops 6202899456 | bytes 30671888 | solution.py:152
  20.6 1.8 %fusion.4 = (bf16[64,1536]{1,0:T(8,128)(2,1)}, bf16[64,1536]{1,0:T(8,128)(2,1)}) fusion(bf16[128,6144]{1,0:T(8,128)(2,1)} %get-tuple-element.56.own, s32[]{:T(128)S(6)} %select_n.23, s32[]{:T(128)S(6)} %select_n.25, s32[]{:T(128)S(6)} %select_n.24), kind=kLoop, calls=%fused_computation.19 | loop fusion | bytes 786444 | tf_op jit(solution)/shard_map/cond/branch_1_fun/dynamic_slice | solution.py:275
  22.4 2.6 %collective-permute-start.8 = (bf16[64,1536]{1,0:T(8,128)(2,1)}, bf16[64,1536]{1,0:T(8,128)(2,1)}, u32[]{:S(2)}, u32[]{:S(2)}) collective-permute-start(bf16[64,1536]{1,0:T(8,128)(2,1)} %get-tuple-element.211), channel_id=1, source_target_pairs={{0,12},{4,0},{8,4},{12,8},{1,13},{5,1},{9,5},{13,9},{2,14},{6,2},{... | collective-permute-start | bytes 589832 | tf_op jit(solution)/shard_map/cond/branch_1_fun/ppermute | solution.py:159
  25.9 1.8 %add_convert_fusion.1 = bf16[128,1536]{1,0:T(8,128)(2,1)S(1)} fusion(bf16[256,1536]{1,0:T(8,128)(2,1)S(1)} %collective-permute-done.12, bf16[128,256]{1,0:T(8,128)(2,1)S(1)} %bitcast.46, bf16[1536,256]{1,0:T(8,128)(2,1)} %get-tuple-element.58.refs_6_), kind=kOutput, calls=%fused_computation.6 | convolution fusion | flops 101253120 | bytes 1638400 | tf_op jit(solution)/shard_map/cond/branch_1_fun/dot_general | solution.py:175
  27.8 1.6 %collective-permute-start.13 = (bf16[128,1536]{1,0:T(8,128)(2,1)S(1)}, bf16[128,1536]{1,0:T(8,128)(2,1)S(1)}, u32[]{:S(2)}, u32[]{:S(2)}) collective-permute-start(bf16[128,1536]{1,0:T(8,128)(2,1)S(1)} %add_convert_fusion.1), channel_id=1, source_target_pairs={{0,2},{1,3},{2,0},{3,1},{4,6},{5,7},{6,4},{7,5},{8,10},{9,11},{10,... | collective-permute-start | bytes 1179656 | tf_op jit(solution)/shard_map/cond/branch_1_fun/ppermute | solution.py:163
  29.3 2.5 %branch_1_fun.6 = (bf16[864,512]{1,0:T(8,128)(2,1)}, bf16[192,512]{1,0:T(8,128)(2,1)}, bf16[192,512]{1,0:T(8,128)(2,1)}) custom-call(bf16[3072,512]{1,0:T(8,128)(2,1)} %bitcast.32), custom_call_target="tpu_custom_call" | custom-call | flops 6000000000 | tf_op jit(solution)/shard_map/cond/branch_1_fun/pallas_call | solution.py:135
  32.4 5.1 %collective-permute-done.7.refs_1_ = bf16[64,1536]{1,0:T(8,128)(2,1)} collective-permute-done((bf16[64,1536]{1,0:T(8,128)(2,1)}, bf16[64,1536]{1,0:T(8,128)(2,1)}, u32[]{:S(2)}, u32[]{:S(2)}) %collective-permute-start.7) | collective-permute-done | bytes 196640 | tf_op jit(solution)/shard_map/cond/branch_1_fun/ppermute | solution.py:159
  39.5 3.4 %branch_1_fun.5 = (f32[128,256]{1,0:T(8,128)}, bf16[320,256]{1,0:T(8,128)(2,1)}, bf16[320,256]{1,0:T(8,128)(2,1)}, bf16[320,256]{1,0:T(8,128)(2,1)}) custom-call(s32[2]{0:T(128)S(1)} %pad_add_fusion.place, bf16[128,6144]{1,0:T(8,128)(2,1)S(1)} %copy-done.1, bf16[64,1536]{1,0:T(8,128)(2,1)} %get-tuple-element.57.refs_0_, ...), custom_call_target="tpu_custom_call" | custom-call | tf_op jit(solution)/shard_map/cond/branch_1_fun/pallas_call | solution.py:257
  46.3 20.2 %conditional.5 = (bf16[128,256]{1,0:T(8,128)(2,1)S(1)}, bf16[32,6144]{1,0:T(8,128)(2,1)}, f32[3072,512]{1,0:T(8,128)}, f32[3072,512]{1,0:T(8,128)}, f32[192,512]...) conditional(s32[]{:T(128)} %convert_element_type.29, () %tuple.39, ...), branch_computations={%region_4.0_spmd, %region_5.0_spmd} | conditional | flops 1769485 | bytes 15401062 | solution.py:152
  46.3 3.5 %collective-permute-start = (bf16[320,256]{1,0:T(8,128)(2,1)}, bf16[320,256]{1,0:T(8,128)(2,1)S(1)}, u32[]{:S(2)}, u32[]{:S(2)}) collective-permute-start(bf16[320,256]{1,0:T(8,128)(2,1)} %get-tuple-element.71), channel_id=1, source_target_pairs={{0,12},{4,0},{8,4},{12,8},{1,13},{5,1},{9,5},{13,9},{2,14},{6,2},{... | collective-permute-start | bytes 491528 | tf_op jit(solution)/shard_map/cond/branch_1_fun/ppermute | solution.py:159
  50.0 1.9 %collective-permute-start.2 = (bf16[320,256]{1,0:T(8,128)(2,1)}, bf16[320,256]{1,0:T(8,128)(2,1)S(1)}, u32[]{:S(2)}, u32[]{:S(2)}) collective-permute-start(bf16[320,256]{1,0:T(8,128)(2,1)} %get-tuple-element.73), channel_id=1, source_target_pairs={{0,4},{4,8},{8,12},{12,0},{1,5},{5,9},{9,13},{13,1},{2,6},{6,10},{... | collective-permute-start | bytes 491528 | tf_op jit(solution)/shard_map/cond/branch_1_fun/ppermute | solution.py:159
  52.0 7.2 %branch_1_fun.8 = (f32[3072,512]{1,0:T(8,128)}, f32[3072,512]{1,0:T(8,128)}) custom-call(bf16[1824,512]{1,0:T(8,128)(2,1)} %get-tuple-element.76.theirs, bf16[3072,512]{1,0:T(8,128)(2,1)} %bitcast.33, f32[3072,512]{1,0:T(8,128)} %bitcast.36, f32[3072,512]{1,0:T(8,128)} %bitcast.39), custom_call_target="tpu_custom_call" | custom-call | tf_op jit(solution)/shard_map/cond/branch_1_fun/pallas_call | solution.py:99
  59.3 2.6 %branch_1_fun.9 = bf16[1536,256]{1,0:T(8,128)(2,1)S(1)} custom-call(s32[2]{0:T(128)S(1)} %pad_add_fusion.1.place, bf16[128,6144]{1,0:T(8,128)(2,1)S(1)} %copy-done.2, bf16[64,1536]{1,0:T(8,128)(2,1)} %get-tuple-element.83.refs_0_, bf16[64,1536]{1,0:T(8,128)(2,1)} %get-tuple-element.84.refs_1_, bf16[64,1536]{1,0:T(8,128)(2,1)} %get-tuple-element.85.refs_2_, ...), custom_call_target="tpu_custom_call" | custom-call | tf_op jit(solution)/shard_map/cond/branch_1_fun/pallas_call | solution.py:257
  61.9 1.8 %multiply_subtract_fusion = (f32[192,512]{1,0:T(8,128)S(1)}, f32[192,512]{1,0:T(8,128)S(1)}, f32[192,512]{1,0:T(8,128)S(1)}, f32[192,512]{1,0:T(8,128)S(1)}) fusion(f32[3072,512]{1,0:T(8,128)} %bitcast.37, bf16[3072,512]{1,0:T(8,128)(2,1)} %bitcast.34, f32[3072,512]{1,0:T(8,128)} %bitcast.40), kind=kLoop, calls=%fused_computation.14 | loop fusion | flops 1769472 | bytes 3538944 | tf_op jit(solution)/shard_map/cond/branch_1_fun/sub | solution.py:22
  64.0 2.4 %branch_1_fun.7 = (bf16[128,256]{1,0:T(8,128)(2,1)S(1)}, bf16[32,6144]{1,0:T(8,128)(2,1)}) custom-call(s32[2]{0:T(128)S(1)} %pad_add_fusion.1.place, f32[128,256]{1,0:T(8,128)} %get-tuple-element.69.keys_own, bf16[128,1536]{1,0:T(8,128)(2,1)} %get-tuple-element.70.summed, bf16[320,256]{1,0:T(8,128)(2,1)S(1)} %collective-permute-done.refs_0_, ...), custom_call_target="tpu_custom_call" | custom-call | tf_op jit(solution)/shard_map/cond/branch_1_fun/pallas_call | solution.py:257
  68.0 3.7 %shard_map.103 = (f32[3072,512]{1,0:T(8,128)}, f32[3072,512]{1,0:T(8,128)}) custom-call(bf16[864,512]{1,0:T(8,128)(2,1)S(1)} %collective-permute-done.17.theirs, bf16[3072,512]{1,0:T(8,128)(2,1)} %bitcast.31, f32[3072,512]{1,0:T(8,128)} %bitcast.35, f32[3072,512]{1,0:T(8,128)} %bitcast.38, ...), custom_call_target="tpu_custom_call", output_to_operand_aliasing={{0}: (4, {}), {1}: (5, {})} | custom-call | tf_op jit(solution)/shard_map/pallas_call | solution.py:99
  (51 shorter events, 17.4 us)
Async XLA Ops:
  2.1 44.2 %collective-permute-start.14 = (bf16[1824,512]{1,0:T(8,128)(2,1)S(1)}, bf16[1824,512]{1,0:T(8,128)(2,1)}, u32[]{:S(2)}, u32[]{:S(2)}) collective-permute-start(bf16[1824,512]{1,0:T(8,128)(2,1)S(1)} %shard_map.102), channel_id=1, source_target_pairs={{0,16},{16,0},{1,17},{17,1},{2,18},{18,2},{3,19},{19,3},{4,20},{20... | collective-permute-start | bytes 5603336 | tf_op jit(solution)/shard_map/ppermute | solution.py:147
  5.2 7.4 %collective-permute-start.4 = (bf16[128,256]{1,0:T(8,128)(2,1)}, bf16[128,256]{1,0:T(8,128)(2,1)S(1)}, u32[]{:S(2)}, u32[]{:S(2)}) collective-permute-start(bf16[128,256]{1,0:T(8,128)(2,1)} %get-tuple-element.204), channel_id=1, source_target_pairs={{0,8},{4,12},{8,0},{12,4},{1,9},{5,13},{9,1},{13,5},{2,10},{6,14},... | collective-permute-start | bytes 196616 | tf_op jit(solution)/shard_map/cond/branch_1_fun/ppermute | solution.py:159
  7.7 6.4 %collective-permute-start.3 = (bf16[128,256]{1,0:T(8,128)(2,1)}, bf16[128,256]{1,0:T(8,128)(2,1)S(1)}, u32[]{:S(2)}, u32[]{:S(2)}) collective-permute-start(bf16[128,256]{1,0:T(8,128)(2,1)} %get-tuple-element.204), channel_id=1, source_target_pairs={{0,4},{4,8},{8,12},{12,0},{1,5},{5,9},{9,13},{13,1},{2,6},{6,10},{... | collective-permute-start | bytes 196616 | tf_op jit(solution)/shard_map/cond/branch_1_fun/ppermute | solution.py:159
  9.3 5.2 %collective-permute-start.5 = (bf16[128,256]{1,0:T(8,128)(2,1)}, bf16[128,256]{1,0:T(8,128)(2,1)S(1)}, u32[]{:S(2)}, u32[]{:S(2)}) collective-permute-start(bf16[128,256]{1,0:T(8,128)(2,1)} %get-tuple-element.204), channel_id=1, source_target_pairs={{0,12},{4,0},{8,4},{12,8},{1,13},{5,1},{9,5},{13,9},{2,14},{6,2},{... | collective-permute-start | bytes 196616 | tf_op jit(solution)/shard_map/cond/branch_1_fun/ppermute | solution.py:159
  12.5 7.6 %collective-permute-start.6 = (bf16[64,1536]{1,0:T(8,128)(2,1)S(1)}, bf16[64,1536]{1,0:T(8,128)(2,1)}, u32[]{:S(2)}, u32[]{:S(2)}) collective-permute-start(bf16[64,1536]{1,0:T(8,128)(2,1)S(1)} %dynamic_slice.16), channel_id=1, source_target_pairs={{0,4},{4,8},{8,12},{12,0},{1,5},{5,9},{9,13},{13,1},{2,6},{6,10},{... | collective-permute-start | bytes 589832 | tf_op jit(solution)/shard_map/cond/branch_1_fun/ppermute | solution.py:159
  20.1 5.8 %collective-permute-start.12 = (bf16[256,1536]{1,0:T(8,128)(2,1)S(1)}, bf16[256,1536]{1,0:T(8,128)(2,1)S(1)}, u32[]{:S(2)}, u32[]{:S(2)}) collective-permute-start(bf16[256,1536]{1,0:T(8,128)(2,1)S(1)} %get-tuple-element.60), channel_id=1, source_target_pairs={{0,1},{1,0},{2,3},{3,2},{4,5},{5,4},{6,7},{7,6},{8,9},{9,8},{10,11... | collective-permute-start | bytes 2359304 | tf_op jit(solution)/shard_map/cond/branch_1_fun/ppermute | solution.py:163
  20.1 19.4 %collective-permute-start.9 = (bf16[64,1536]{1,0:T(8,128)(2,1)}, bf16[64,1536]{1,0:T(8,128)(2,1)}, u32[]{:S(2)}, u32[]{:S(2)}) collective-permute-start(bf16[64,1536]{1,0:T(8,128)(2,1)} %get-tuple-element.57.refs_0_), channel_id=1, source_target_pairs={{0,1},{1,0},{2,3},{3,2},{4,5},{5,4},{6,7},{7,6},{8,9},{9,8},{10,11... | collective-permute-start | bytes 589832 | tf_op jit(solution)/shard_map/cond/branch_1_fun/ppermute | solution.py:163
  22.4 9.8 %collective-permute-start.8 = (bf16[64,1536]{1,0:T(8,128)(2,1)}, bf16[64,1536]{1,0:T(8,128)(2,1)}, u32[]{:S(2)}, u32[]{:S(2)}) collective-permute-start(bf16[64,1536]{1,0:T(8,128)(2,1)} %get-tuple-element.211), channel_id=1, source_target_pairs={{0,12},{4,0},{8,4},{12,8},{1,13},{5,1},{9,5},{13,9},{2,14},{6,2},{... | collective-permute-start | bytes 589832 | tf_op jit(solution)/shard_map/cond/branch_1_fun/ppermute | solution.py:159
  25.0 12.4 %collective-permute-start.7 = (bf16[64,1536]{1,0:T(8,128)(2,1)}, bf16[64,1536]{1,0:T(8,128)(2,1)}, u32[]{:S(2)}, u32[]{:S(2)}) collective-permute-start(bf16[64,1536]{1,0:T(8,128)(2,1)} %get-tuple-element.212), channel_id=1, source_target_pairs={{0,8},{4,12},{8,0},{12,4},{1,9},{5,13},{9,1},{13,5},{2,10},{6,14},... | collective-permute-start | bytes 589832 | tf_op jit(solution)/shard_map/cond/branch_1_fun/ppermute | solution.py:159
  25.9 3.4 %copy-start.4 = (bf16[256,1536]{1,0:T(8,128)(2,1)}, bf16[256,1536]{1,0:T(8,128)(2,1)S(1)}, u32[]{:S(2)}) copy-start(bf16[256,1536]{1,0:T(8,128)(2,1)S(1)} %collective-permute-done.12) | copy-start | bytes 2359300 | tf_op jit(solution)/shard_map/cond
  27.8 10.9 %collective-permute-start.13 = (bf16[128,1536]{1,0:T(8,128)(2,1)S(1)}, bf16[128,1536]{1,0:T(8,128)(2,1)S(1)}, u32[]{:S(2)}, u32[]{:S(2)}) collective-permute-start(bf16[128,1536]{1,0:T(8,128)(2,1)S(1)} %add_convert_fusion.1), channel_id=1, source_target_pairs={{0,2},{1,3},{2,0},{3,1},{4,6},{5,7},{6,4},{7,5},{8,10},{9,11},{10,... | collective-permute-start | bytes 1179656 | tf_op jit(solution)/shard_map/cond/branch_1_fun/ppermute | solution.py:163
  29.3 2.6 %copy-start = (bf16[1536,256]{1,0:T(8,128)(2,1)S(1)}, bf16[1536,256]{1,0:T(8,128)(2,1)}, u32[]{:S(2)}) copy-start(bf16[1536,256]{1,0:T(8,128)(2,1)} %get-tuple-element.58.refs_6_) | copy-start | bytes 2359300 | tf_op jit(solution)/shard_map/cond
  29.3 9.3 %copy-start.5 = (bf16[256,1536]{1,0:T(8,128)(2,1)S(1)}, bf16[256,1536]{1,0:T(8,128)(2,1)}, u32[]{:S(2)}) copy-start(bf16[256,1536]{1,0:T(8,128)(2,1)} %copy-done.4) | copy-start | bytes 2359300 | tf_op jit(solution)/shard_map/cond
  29.3 10.2 %copy-start.1 = (bf16[128,6144]{1,0:T(8,128)(2,1)S(1)}, bf16[128,6144]{1,0:T(8,128)(2,1)}, u32[]{:S(2)}) copy-start(bf16[128,6144]{1,0:T(8,128)(2,1)} %get-tuple-element.56.own) | copy-start | bytes 4718596 | tf_op jit(solution)/shard_map/cond
  32.3 7.2 %collective-permute-start.11 = (bf16[64,1536]{1,0:T(8,128)(2,1)}, bf16[64,1536]{1,0:T(8,128)(2,1)}, u32[]{:S(2)}, u32[]{:S(2)}) collective-permute-start(bf16[64,1536]{1,0:T(8,128)(2,1)} %collective-permute-done.8.refs_2_), channel_id=1, source_target_pairs={{0,1},{1,0},{2,3},{3,2},{4,5},{5,4},{6,7},{7,6},{8,9},{9,8},{10,11... | collective-permute-start | bytes 589832 | tf_op jit(solution)/shard_map/cond/branch_1_fun/ppermute | solution.py:163
  37.5 2.0 %collective-permute-start.10 = (bf16[64,1536]{1,0:T(8,128)(2,1)}, bf16[64,1536]{1,0:T(8,128)(2,1)}, u32[]{:S(2)}, u32[]{:S(2)}) collective-permute-start(bf16[64,1536]{1,0:T(8,128)(2,1)} %collective-permute-done.7.refs_1_), channel_id=1, source_target_pairs={{0,1},{1,0},{2,3},{3,2},{4,5},{5,4},{6,7},{7,6},{8,9},{9,8},{10,11... | collective-permute-start | bytes 589832 | tf_op jit(solution)/shard_map/cond/branch_1_fun/ppermute | solution.py:163
  42.9 25.1 %collective-permute-start.17 = (bf16[864,512]{1,0:T(8,128)(2,1)}, bf16[864,512]{1,0:T(8,128)(2,1)S(1)}, u32[]{:S(2)}, u32[]{:S(2)}) collective-permute-start(bf16[864,512]{1,0:T(8,128)(2,1)} %get-tuple-element.181), channel_id=1, source_target_pairs={{0,16},{16,0},{1,17},{17,1},{2,18},{18,2},{3,19},{19,3},{4,20},{20... | collective-permute-start | bytes 2654216 | tf_op jit(solution)/shard_map/ppermute | solution.py:147
  43.4 28.3 %collective-permute-start.16 = (bf16[192,512]{1,0:T(8,128)(2,1)}, bf16[192,512]{1,0:T(8,128)(2,1)S(1)}, u32[]{:S(2)}, u32[]{:S(2)}) collective-permute-start(bf16[192,512]{1,0:T(8,128)(2,1)} %get-tuple-element.180), channel_id=1, source_target_pairs={{0,16},{16,0},{1,17},{17,1},{2,18},{18,2},{3,19},{19,3},{4,20},{20... | collective-permute-start | bytes 589832 | tf_op jit(solution)/shard_map/ppermute | solution.py:147
  46.3 17.3 %collective-permute-start = (bf16[320,256]{1,0:T(8,128)(2,1)}, bf16[320,256]{1,0:T(8,128)(2,1)S(1)}, u32[]{:S(2)}, u32[]{:S(2)}) collective-permute-start(bf16[320,256]{1,0:T(8,128)(2,1)} %get-tuple-element.71), channel_id=1, source_target_pairs={{0,12},{4,0},{8,4},{12,8},{1,13},{5,1},{9,5},{13,9},{2,14},{6,2},{... | collective-permute-start | bytes 491528 | tf_op jit(solution)/shard_map/cond/branch_1_fun/ppermute | solution.py:159
  49.8 14.2 %collective-permute-start.1 = (bf16[320,256]{1,0:T(8,128)(2,1)}, bf16[320,256]{1,0:T(8,128)(2,1)S(1)}, u32[]{:S(2)}, u32[]{:S(2)}) collective-permute-start(bf16[320,256]{1,0:T(8,128)(2,1)} %get-tuple-element.72), channel_id=1, source_target_pairs={{0,8},{4,12},{8,0},{12,4},{1,9},{5,13},{9,1},{13,5},{2,10},{6,14},... | collective-permute-start | bytes 491528 | tf_op jit(solution)/shard_map/cond/branch_1_fun/ppermute | solution.py:159
  50.0 14.0 %collective-permute-start.2 = (bf16[320,256]{1,0:T(8,128)(2,1)}, bf16[320,256]{1,0:T(8,128)(2,1)S(1)}, u32[]{:S(2)}, u32[]{:S(2)}) collective-permute-start(bf16[320,256]{1,0:T(8,128)(2,1)} %get-tuple-element.73), channel_id=1, source_target_pairs={{0,4},{4,8},{8,12},{12,0},{1,5},{5,9},{9,13},{13,1},{2,6},{6,10},{... | collective-permute-start | bytes 491528 | tf_op jit(solution)/shard_map/cond/branch_1_fun/ppermute | solution.py:159
  52.0 7.2 %copy-start.2 = (bf16[128,6144]{1,0:T(8,128)(2,1)S(1)}, bf16[128,6144]{1,0:T(8,128)(2,1)}, u32[]{:S(2)}) copy-start(bf16[128,6144]{1,0:T(8,128)(2,1)} %get-tuple-element.82.own) | copy-start | bytes 4718596 | tf_op jit(solution)/shard_map/cond
  66.4 5.2 %copy-start.6 = (bf16[128,256]{1,0:T(8,128)(2,1)}, bf16[128,256]{1,0:T(8,128)(2,1)S(1)}, u32[]{:S(2)}) copy-start(bf16[128,256]{1,0:T(8,128)(2,1)S(1)} %get-tuple-element.144) | copy-start | bytes 196612
  66.4 6.8 %collective-permute-start.15 = (bf16[192,512]{1,0:T(8,128)(2,1)}, bf16[192,512]{1,0:T(8,128)(2,1)S(1)}, u32[]{:S(2)}, u32[]{:S(2)}) collective-permute-start(bf16[192,512]{1,0:T(8,128)(2,1)} %get-tuple-element.179), channel_id=1, source_target_pairs={{0,16},{16,0},{1,17},{17,1},{2,18},{18,2},{3,19},{19,3},{4,20},{20... | collective-permute-start | bytes 589832 | tf_op jit(solution)/shard_map/ppermute | solution.py:147
  (1 other events, 1.5 us)

commit v7 on v6

--- a/solution.py
+++ b/solution.py
@@ -13,7 +13,7 @@
 BF16 = jnp.bfloat16
 units = 32
 late_parts = 2
-chunk_units = ((0, 19, 6), (19, 9, 3), (28, 2, None), (30, 2, None))
+chunk_units = ((0, 19, 6), (19, 9, 3), (28, 3, None), (31, 1, None))
 
 
 def nesterov(frag_sum, outer, momentum, islands):
@@ -48,22 +48,24 @@
             copy.wait()
 
 
-def own_terms(k, local_frag, outer_frag, momentum):
+def own_terms(late, local_frag, outer_frag, momentum):
     ours, outer, held = (a.reshape(-1, a.shape[-1]) for a in (local_frag, outer_frag, momentum))
     unit = ours.shape[0] // units
-    first, size, _ = chunk_units[k]
-    ours, outer, held = (lax.slice_in_dim(a, first * unit, (first + size) * unit) for a in (ours, outer, held))
+    first = chunk_units[late[0]][0]
+    last = first + sum(chunk_units[k][1] for k in late)
+    ours, outer, held = (lax.slice_in_dim(a, first * unit, last * unit) for a in (ours, outer, held))
     return nesterov(ours.astype(F32), outer, held, lax.axis_size("island"))
 
 
-def late_kernel(islands, first, cuts, theirs, outer_terms, momentum_terms, *refs):
+def late_kernel(islands, first, skipped, cuts, theirs, outer_terms, momentum_terms, *refs):
     new_outer, new_momentum, outer_rows, momentum_rows, stores = refs[-5:]
     leaving = []
     for k, (top, bottom) in enumerate(zip(cuts, cuts[1:])):
         rows, there = slice(top, bottom), pl.ds(first + top, bottom - top)
+        own = slice(skipped + top, skipped + bottom)
         share = theirs[rows].astype(F32) / islands
-        outer_rows[rows] = outer_terms[rows] + outer_rate * (1 + beta_outer) * share
-        momentum_rows[rows] = momentum_terms[rows] - share
+        outer_rows[rows] = outer_terms[own] + outer_rate * (1 + beta_outer) * share
+        momentum_rows[rows] = momentum_terms[own] - share
         for i, (buffer, out) in enumerate(((outer_rows, new_outer), (momentum_rows, new_momentum))):
             leaving.append(pltpu.make_async_copy(buffer.at[pl.ds(top, bottom - top)], out.at[there], stores.at[i, k]))
             leaving[-1].start()
@@ -77,7 +79,7 @@
     cuts = [rows * i // late_parts // 16 * 16 for i in range(late_parts)] + [rows]
     hbm, vmem = pl.BlockSpec(memory_space=pltpu.HBM), pl.BlockSpec(memory_space=pltpu.VMEM)
     return pl.pallas_call(
-        functools.partial(late_kernel, lax.axis_size("island"), first, cuts),
+        functools.partial(late_kernel, lax.axis_size("island"), first, first - done[0].shape[0] + terms[0].shape[0], cuts),
         in_specs=[vmem] * 3 + [hbm] * 2,
         out_specs=[hbm] * 2,
         out_shape=[jax.ShapeDtypeStruct(a.shape, F32) for a in done],
@@ -342,7 +344,7 @@
     theirs[0], state = lax.optimization_barrier((theirs[0], state))
 
     def step_three(theirs, cots, mine, state, tokens, weight, *frag):
-        return finish(cots, mine, *state, tokens, weight), update(0, theirs, *frag, ()), [own_terms(k, *frag) for k in late]
+        return finish(cots, mine, *state, tokens, weight), update(0, theirs, *frag, ()), own_terms(late, *frag)
 
     results, done, terms = together(
         step_three, theirs[0], cots, mine, state, tokens, weight, local_frag, outer_frag, momentum
@@ -354,7 +356,7 @@
     done = update(1, theirs[1], local_frag, outer_frag, momentum, done)
     for k in late:
         theirs[k], done = lax.optimization_barrier((theirs[k], done))
-        done = late_update(k, theirs[k], terms[k - late[0]], done)
+        done = late_update(k, theirs[k], terms, done)
     new_outer, new_momentum = (a.reshape(outer_frag.shape) for a in done)
     return (keys, input_grad, weight_grad[None], new_outer, new_momentum)
 

time: 74.7 us -> 74.6 us (level)
    pallas_call x3, Pallas kernels: 8.35 us -> 7.59 us  [local_call(): pl.pallas_call(kernel, grid_spec=pltpu.PrefetchScalarGridSpec(num_scalar_...]
  transfers between devices with their start and end apart: 18 -> 18, of which waited for: 8 -> 9; matrix products, arithmetic and copies ran while one was open for 17% -> 17% of each run, Pallas kernels for 31% -> 30%
where the time goes in v7:
time: 74.6 us; the launch traced here: 74 us
  Pallas kernels  24.4 us (33%)
  starting transfers between devices  23.5 us (32%)
  waiting for transfers between devices  12.6 us (17%)
  local copies, waits for them, and re-layouts  4.54 us (6%)
  other arithmetic  4.35 us (6%)
  matrix products  3.73 us (5%)
    ppermute x9, starting transfers between devices, shifted(): return lax.ppermute(x, axis, [(i, (i + step) % n) for i in range(n)])  14.7 us
    pallas_call x2, Pallas kernels, update(): pl.pallas_call(functools.partial(update_kernel, islands, first, cuts), in...  11 us
    ppermute x9, waiting for transfers between devices, shifted(): return lax.ppermute(x, axis, [(i, (i + step) % n) for i in range(n)])  9.05 us
    pallas_call x3, Pallas kernels, local_call(): pl.pallas_call(kernel, grid_spec=pltpu.PrefetchScalarGridSpec(num_scalar_...  7.59 us
    ppermute x4, starting transfers between devices, swapped(): return lax.ppermute(piece, 'island', [(0, 1), (1, 0)])  6.64 us
    pallas_call x2, Pallas kernels, pieces_of(): pl.pallas_call(functools.partial(piece_kernel, parts), in_specs=[pl.Block...  3.94 us
    dot_general x3, matrix products, part_of(): lax.dot_general(rows_of.reshape(-1, cots.shape[2]), weight, (((1,), (1,))...  3.73 us
    dynamic_slice x2, local copies, waits for them, and re-layouts, columns_for(): lax.dynamic_slice(tokens, (core * half, lax.rem(me + s, lax.axis_size('fs...  2.73 us
  transfers between devices with their start and end apart: 18, of which 9 were waited for; matrix products, arithmetic and copies ran while one was open for 17% of the time, Pallas kernels for 30%

profile of v7, /device:TPU:0, one launch (start us, length us, event | category | flops | bytes accessed | tf_op | source)
XLA Modules:
  0.0 74.0 jit_solution(9534906429157921441)
XLA Ops:
  2.1 3.0 %collective-permute-start.14 = (bf16[1824,512]{1,0:T(8,128)(2,1)S(1)}, bf16[1824,512]{1,0:T(8,128)(2,1)}, u32[]{:S(2)}, u32[]{:S(2)}) collective-permute-start(bf16[1824,512]{1,0:T(8,128)(2,1)S(1)} %shard_map.102), channel_id=1, source_target_pairs={{0,16},{16,0},{1,17},{17,1},{2,18},{18,2},{3,19},{19,3},{4,20},{20... | collective-permute-start | bytes 5603336 | tf_op jit(solution)/shard_map/ppermute | solution.py:149
  5.2 15.0 %conditional.3 = (bf16[4,128,256]{2,1,0:T(8,128)(2,1)}, bf16[256,1536]{1,0:T(8,128)(2,1)S(1)}, bf16[64,1536]{1,0:T(8,128)(2,1)}) conditional(s32[]{:T(128)} %convert_element_type.26, () %tuple.41, (bf16[128,256]{1,0:T(8,128)(2,1)}, bf16[1536,256]{1,0:T(8,128)(2,1)}, bf16[128,6144]{1,0:T(8,128)(2,1)}) %tuple.61), branch_computations={%region_0.0_spmd, %region_1.0_spmd} | conditional | flops 202178576 | bytes 4719186 | solution.py:154
  5.2 2.6 %collective-permute-start.4 = (bf16[128,256]{1,0:T(8,128)(2,1)}, bf16[128,256]{1,0:T(8,128)(2,1)S(1)}, u32[]{:S(2)}, u32[]{:S(2)}) collective-permute-start(bf16[128,256]{1,0:T(8,128)(2,1)} %get-tuple-element.200), channel_id=1, source_target_pairs={{0,8},{4,12},{8,0},{12,4},{1,9},{5,13},{9,1},{13,5},{2,10},{6,14},... | collective-permute-start | bytes 196616 | tf_op jit(solution)/shard_map/cond/branch_1_fun/ppermute | solution.py:161
  7.7 1.6 %collective-permute-start.3 = (bf16[128,256]{1,0:T(8,128)(2,1)}, bf16[128,256]{1,0:T(8,128)(2,1)S(1)}, u32[]{:S(2)}, u32[]{:S(2)}) collective-permute-start(bf16[128,256]{1,0:T(8,128)(2,1)} %get-tuple-element.200), channel_id=1, source_target_pairs={{0,4},{4,8},{8,12},{12,0},{1,5},{5,9},{9,13},{13,1},{2,6},{6,10},{... | collective-permute-start | bytes 196616 | tf_op jit(solution)/shard_map/cond/branch_1_fun/ppermute | solution.py:161
  9.3 2.2 %collective-permute-start.5 = (bf16[128,256]{1,0:T(8,128)(2,1)}, bf16[128,256]{1,0:T(8,128)(2,1)S(1)}, u32[]{:S(2)}, u32[]{:S(2)}) collective-permute-start(bf16[128,256]{1,0:T(8,128)(2,1)} %get-tuple-element.200), channel_id=1, source_target_pairs={{0,12},{4,0},{8,4},{12,8},{1,13},{5,1},{9,5},{13,9},{2,14},{6,2},{... | collective-permute-start | bytes 196616 | tf_op jit(solution)/shard_map/cond/branch_1_fun/ppermute | solution.py:161
  12.6 1.6 %collective-permute-done.3 = bf16[128,256]{1,0:T(8,128)(2,1)S(1)} collective-permute-done((bf16[128,256]{1,0:T(8,128)(2,1)}, bf16[128,256]{1,0:T(8,128)(2,1)S(1)}, u32[]{:S(2)}, u32[]{:S(2)}) %collective-permute-start.3) | collective-permute-done | bytes 65568 | tf_op jit(solution)/shard_map/cond/branch_1_fun/ppermute | solution.py:161
  14.5 1.6 %pad_maximum_fusion = bf16[4,128,256]{2,1,0:T(8,128)(2,1)} fusion(bf16[1,128,256]{2,1,0:T(8,128)(2,1)S(1)} %bitcast.50, bf16[1,128,256]{2,1,0:T(8,128)(2,1)S(1)} %bitcast.48, bf16[1,128,256]{2,1,0:T(8,128)(2,1)S(1)} %bitcast.49, bf16[1,128,256]{2,1,0:T(8,128)(2,1)} %bitcast.47), kind=kLoop, calls=%fused_computation.1 | loop fusion | flops 393216 | bytes 524288 | tf_op jit(solution)/shard_map/cond/branch_1_fun/stack | solution.py:281
  18.5 1.6 %collective-permute-done.6 = bf16[64,1536]{1,0:T(8,128)(2,1)} collective-permute-done((bf16[64,1536]{1,0:T(8,128)(2,1)S(1)}, bf16[64,1536]{1,0:T(8,128)(2,1)}, u32[]{:S(2)}, u32[]{:S(2)}) %collective-permute-start.6) | collective-permute-done | bytes 196640 | tf_op jit(solution)/shard_map/cond/branch_1_fun/ppermute | solution.py:161
  20.1 22.7 %conditional.4 = (bf16[64,1536]{1,0:T(8,128)(2,1)}, bf16[64,1536]{1,0:T(8,128)(2,1)}, bf16[64,1536]{1,0:T(8,128)(2,1)}, bf16[64,1536]{1,0:T(8,128)(2,1)}, bf16[6...) conditional(s32[]{:T(128)} %convert_element_type.26, () %tuple.40, ...), branch_computations={%region_2.0_spmd, %region_3.0_spmd} | conditional | flops 6202899456 | bytes 30671888 | solution.py:154
  20.6 1.8 %fusion.2 = (bf16[64,1536]{1,0:T(8,128)(2,1)}, bf16[64,1536]{1,0:T(8,128)(2,1)}) fusion(bf16[128,6144]{1,0:T(8,128)(2,1)} %get-tuple-element.56.own, s32[]{:T(128)S(6)} %select_n.23, s32[]{:T(128)S(6)} %select_n.25, s32[]{:T(128)S(6)} %select_n.24), kind=kLoop, calls=%fused_computation.15 | loop fusion | bytes 786444 | tf_op jit(solution)/shard_map/cond/branch_1_fun/dynamic_slice | solution.py:277
  22.4 2.6 %collective-permute-start.8 = (bf16[64,1536]{1,0:T(8,128)(2,1)}, bf16[64,1536]{1,0:T(8,128)(2,1)}, u32[]{:S(2)}, u32[]{:S(2)}) collective-permute-start(bf16[64,1536]{1,0:T(8,128)(2,1)} %get-tuple-element.205), channel_id=1, source_target_pairs={{0,12},{4,0},{8,4},{12,8},{1,13},{5,1},{9,5},{13,9},{2,14},{6,2},{... | collective-permute-start | bytes 589832 | tf_op jit(solution)/shard_map/cond/branch_1_fun/ppermute | solution.py:161
  25.9 1.8 %add_convert_fusion.1 = bf16[128,1536]{1,0:T(8,128)(2,1)S(1)} fusion(bf16[256,1536]{1,0:T(8,128)(2,1)S(1)} %collective-permute-done.12, bf16[128,256]{1,0:T(8,128)(2,1)S(1)} %bitcast.46, bf16[1536,256]{1,0:T(8,128)(2,1)} %get-tuple-element.58.refs_6_), kind=kOutput, calls=%fused_computation.6 | convolution fusion | flops 101253120 | bytes 1638400 | tf_op jit(solution)/shard_map/cond/branch_1_fun/dot_general | solution.py:177
  29.3 2.5 %branch_1_fun.6 = (bf16[864,512]{1,0:T(8,128)(2,1)}, bf16[288,512]{1,0:T(8,128)(2,1)}, bf16[96,512]{1,0:T(8,128)(2,1)S(1)}) custom-call(bf16[3072,512]{1,0:T(8,128)(2,1)} %bitcast.32), custom_call_target="tpu_custom_call" | custom-call | flops 6000000000 | tf_op jit(solution)/shard_map/cond/branch_1_fun/pallas_call | solution.py:137
  32.3 5.1 %collective-permute-done.7.refs_1_ = bf16[64,1536]{1,0:T(8,128)(2,1)} collective-permute-done((bf16[64,1536]{1,0:T(8,128)(2,1)}, bf16[64,1536]{1,0:T(8,128)(2,1)}, u32[]{:S(2)}, u32[]{:S(2)}) %collective-permute-start.7) | collective-permute-done | bytes 196640 | tf_op jit(solution)/shard_map/cond/branch_1_fun/ppermute | solution.py:161
  39.5 3.3 %branch_1_fun.5 = (f32[128,256]{1,0:T(8,128)}, bf16[320,256]{1,0:T(8,128)(2,1)}, bf16[320,256]{1,0:T(8,128)(2,1)}, bf16[320,256]{1,0:T(8,128)(2,1)}) custom-call(s32[2]{0:T(128)S(1)} %pad_add_fusion.place, bf16[128,6144]{1,0:T(8,128)(2,1)S(1)} %copy-done.1, bf16[64,1536]{1,0:T(8,128)(2,1)} %get-tuple-element.57.refs_0_, ...), custom_call_target="tpu_custom_call" | custom-call | tf_op jit(solution)/shard_map/cond/branch_1_fun/pallas_call | solution.py:259
  46.3 19.4 %conditional.5 = (bf16[128,256]{1,0:T(8,128)(2,1)S(1)}, bf16[32,6144]{1,0:T(8,128)(2,1)S(1)}, f32[3072,512]{1,0:T(8,128)}, f32[3072,512]{1,0:T(8,128)}, f32[384,...) conditional(s32[]{:T(128)} %convert_element_type.26, () %tuple.39, ...), branch_computations={%region_4.0_spmd, %region_5.0_spmd} | conditional | flops 1769485 | bytes 15401038 | solution.py:154
  46.3 3.5 %collective-permute-start = (bf16[320,256]{1,0:T(8,128)(2,1)}, bf16[320,256]{1,0:T(8,128)(2,1)S(1)}, u32[]{:S(2)}, u32[]{:S(2)}) collective-permute-start(bf16[320,256]{1,0:T(8,128)(2,1)} %get-tuple-element.71), channel_id=1, source_target_pairs={{0,12},{4,0},{8,4},{12,8},{1,13},{5,1},{9,5},{13,9},{2,14},{6,2},{... | collective-permute-start | bytes 491528 | tf_op jit(solution)/shard_map/cond/branch_1_fun/ppermute | solution.py:161
  50.0 1.9 %collective-permute-start.2 = (bf16[320,256]{1,0:T(8,128)(2,1)}, bf16[320,256]{1,0:T(8,128)(2,1)S(1)}, u32[]{:S(2)}, u32[]{:S(2)}) collective-permute-start(bf16[320,256]{1,0:T(8,128)(2,1)} %get-tuple-element.73), channel_id=1, source_target_pairs={{0,4},{4,8},{8,12},{12,0},{1,5},{5,9},{9,13},{13,1},{2,6},{6,10},{... | collective-permute-start | bytes 491528 | tf_op jit(solution)/shard_map/cond/branch_1_fun/ppermute | solution.py:161
  52.0 7.2 %branch_1_fun.8 = (f32[3072,512]{1,0:T(8,128)}, f32[3072,512]{1,0:T(8,128)}) custom-call(bf16[1824,512]{1,0:T(8,128)(2,1)} %get-tuple-element.76.theirs, bf16[3072,512]{1,0:T(8,128)(2,1)} %bitcast.33, f32[3072,512]{1,0:T(8,128)} %bitcast.36, f32[3072,512]{1,0:T(8,128)} %bitcast.39), custom_call_target="tpu_custom_call" | custom-call | tf_op jit(solution)/shard_map/cond/branch_1_fun/pallas_call | solution.py:101
  59.3 2.6 %branch_1_fun.9 = bf16[1536,256]{1,0:T(8,128)(2,1)S(1)} custom-call(s32[2]{0:T(128)S(1)} %pad_add_fusion.1.place, bf16[128,6144]{1,0:T(8,128)(2,1)S(1)} %copy-done.2, bf16[64,1536]{1,0:T(8,128)(2,1)} %get-tuple-element.83.refs_0_, bf16[64,1536]{1,0:T(8,128)(2,1)} %get-tuple-element.84.refs_1_, bf16[64,1536]{1,0:T(8,128)(2,1)} %get-tuple-element.85.refs_2_, ...), custom_call_target="tpu_custom_call" | custom-call | tf_op jit(solution)/shard_map/cond/branch_1_fun/pallas_call | solution.py:259
  61.9 1.7 %multiply_subtract_fusion = (f32[384,512]{1,0:T(8,128)S(1)}, f32[384,512]{1,0:T(8,128)S(1)}) fusion(f32[3072,512]{1,0:T(8,128)} %bitcast.37, bf16[3072,512]{1,0:T(8,128)(2,1)} %bitcast.34, f32[3072,512]{1,0:T(8,128)} %bitcast.40), kind=kLoop, calls=%fused_computation.12 | loop fusion | flops 1769472 | bytes 3538944 | tf_op jit(solution)/shard_map/cond/branch_1_fun/sub | solution.py:22
  64.0 1.7 %branch_1_fun.7 = (bf16[128,256]{1,0:T(8,128)(2,1)S(1)}, bf16[32,6144]{1,0:T(8,128)(2,1)S(1)}) custom-call(s32[2]{0:T(128)S(1)} %pad_add_fusion.1.place, f32[128,256]{1,0:T(8,128)} %get-tuple-element.69.keys_own, bf16[128,1536]{1,0:T(8,128)(2,1)} %get-tuple-element.70.summed, bf16[320,256]{1,0:T(8,128)(2,1)S(1)} %collective-permute-done.refs_0_, ...), custom_call_target="tpu_custom_call" | custom-call | tf_op jit(solution)/shard_map/cond/branch_1_fun/pallas_call | solution.py:259
  65.8 1.6 %collective-permute-start.15 = (bf16[96,512]{1,0:T(8,128)(2,1)S(1)}, bf16[96,512]{1,0:T(8,128)(2,1)S(1)}, u32[]{:S(2)}, u32[]{:S(2)}) collective-permute-start(bf16[96,512]{1,0:T(8,128)(2,1)S(1)} %get-tuple-element.177), channel_id=1, source_target_pairs={{0,16},{16,0},{1,17},{17,1},{2,18},{18,2},{3,19},{19,3},{4,20},{20... | collective-permute-start | bytes 294920 | tf_op jit(solution)/shard_map/ppermute | solution.py:149
  67.4 3.7 %shard_map.103 = (f32[3072,512]{1,0:T(8,128)}, f32[3072,512]{1,0:T(8,128)}) custom-call(bf16[864,512]{1,0:T(8,128)(2,1)S(1)} %collective-permute-done.17.theirs, bf16[3072,512]{1,0:T(8,128)(2,1)} %bitcast.31, f32[3072,512]{1,0:T(8,128)} %bitcast.35, f32[3072,512]{1,0:T(8,128)} %bitcast.38, ...), custom_call_target="tpu_custom_call", output_to_operand_aliasing={{0}: (4, {}), {1}: (5, {})} | custom-call | tf_op jit(solution)/shard_map/pallas_call | solution.py:101
  (57 shorter events, 17.9 us)
Async XLA Ops:
  2.1 44.2 %collective-permute-start.14 = (bf16[1824,512]{1,0:T(8,128)(2,1)S(1)}, bf16[1824,512]{1,0:T(8,128)(2,1)}, u32[]{:S(2)}, u32[]{:S(2)}) collective-permute-start(bf16[1824,512]{1,0:T(8,128)(2,1)S(1)} %shard_map.102), channel_id=1, source_target_pairs={{0,16},{16,0},{1,17},{17,1},{2,18},{18,2},{3,19},{19,3},{4,20},{20... | collective-permute-start | bytes 5603336 | tf_op jit(solution)/shard_map/ppermute | solution.py:149
  5.2 7.4 %collective-permute-start.4 = (bf16[128,256]{1,0:T(8,128)(2,1)}, bf16[128,256]{1,0:T(8,128)(2,1)S(1)}, u32[]{:S(2)}, u32[]{:S(2)}) collective-permute-start(bf16[128,256]{1,0:T(8,128)(2,1)} %get-tuple-element.200), channel_id=1, source_target_pairs={{0,8},{4,12},{8,0},{12,4},{1,9},{5,13},{9,1},{13,5},{2,10},{6,14},... | collective-permute-start | bytes 196616 | tf_op jit(solution)/shard_map/cond/branch_1_fun/ppermute | solution.py:161
  7.7 6.4 %collective-permute-start.3 = (bf16[128,256]{1,0:T(8,128)(2,1)}, bf16[128,256]{1,0:T(8,128)(2,1)S(1)}, u32[]{:S(2)}, u32[]{:S(2)}) collective-permute-start(bf16[128,256]{1,0:T(8,128)(2,1)} %get-tuple-element.200), channel_id=1, source_target_pairs={{0,4},{4,8},{8,12},{12,0},{1,5},{5,9},{9,13},{13,1},{2,6},{6,10},{... | collective-permute-start | bytes 196616 | tf_op jit(solution)/shard_map/cond/branch_1_fun/ppermute | solution.py:161
  9.3 5.2 %collective-permute-start.5 = (bf16[128,256]{1,0:T(8,128)(2,1)}, bf16[128,256]{1,0:T(8,128)(2,1)S(1)}, u32[]{:S(2)}, u32[]{:S(2)}) collective-permute-start(bf16[128,256]{1,0:T(8,128)(2,1)} %get-tuple-element.200), channel_id=1, source_target_pairs={{0,12},{4,0},{8,4},{12,8},{1,13},{5,1},{9,5},{13,9},{2,14},{6,2},{... | collective-permute-start | bytes 196616 | tf_op jit(solution)/shard_map/cond/branch_1_fun/ppermute | solution.py:161
  12.5 7.6 %collective-permute-start.6 = (bf16[64,1536]{1,0:T(8,128)(2,1)S(1)}, bf16[64,1536]{1,0:T(8,128)(2,1)}, u32[]{:S(2)}, u32[]{:S(2)}) collective-permute-start(bf16[64,1536]{1,0:T(8,128)(2,1)S(1)} %dynamic_slice.16), channel_id=1, source_target_pairs={{0,4},{4,8},{8,12},{12,0},{1,5},{5,9},{9,13},{13,1},{2,6},{6,10},{... | collective-permute-start | bytes 589832 | tf_op jit(solution)/shard_map/cond/branch_1_fun/ppermute | solution.py:161
  20.1 5.8 %collective-permute-start.12 = (bf16[256,1536]{1,0:T(8,128)(2,1)S(1)}, bf16[256,1536]{1,0:T(8,128)(2,1)S(1)}, u32[]{:S(2)}, u32[]{:S(2)}) collective-permute-start(bf16[256,1536]{1,0:T(8,128)(2,1)S(1)} %get-tuple-element.60), channel_id=1, source_target_pairs={{0,1},{1,0},{2,3},{3,2},{4,5},{5,4},{6,7},{7,6},{8,9},{9,8},{10,11... | collective-permute-start | bytes 2359304 | tf_op jit(solution)/shard_map/cond/branch_1_fun/ppermute | solution.py:165
  20.1 19.4 %collective-permute-start.9 = (bf16[64,1536]{1,0:T(8,128)(2,1)}, bf16[64,1536]{1,0:T(8,128)(2,1)}, u32[]{:S(2)}, u32[]{:S(2)}) collective-permute-start(bf16[64,1536]{1,0:T(8,128)(2,1)} %get-tuple-element.57.refs_0_), channel_id=1, source_target_pairs={{0,1},{1,0},{2,3},{3,2},{4,5},{5,4},{6,7},{7,6},{8,9},{9,8},{10,11... | collective-permute-start | bytes 589832 | tf_op jit(solution)/shard_map/cond/branch_1_fun/ppermute | solution.py:165
  22.4 9.8 %collective-permute-start.8 = (bf16[64,1536]{1,0:T(8,128)(2,1)}, bf16[64,1536]{1,0:T(8,128)(2,1)}, u32[]{:S(2)}, u32[]{:S(2)}) collective-permute-start(bf16[64,1536]{1,0:T(8,128)(2,1)} %get-tuple-element.205), channel_id=1, source_target_pairs={{0,12},{4,0},{8,4},{12,8},{1,13},{5,1},{9,5},{13,9},{2,14},{6,2},{... | collective-permute-start | bytes 589832 | tf_op jit(solution)/shard_map/cond/branch_1_fun/ppermute | solution.py:161
  25.0 12.4 %collective-permute-start.7 = (bf16[64,1536]{1,0:T(8,128)(2,1)}, bf16[64,1536]{1,0:T(8,128)(2,1)}, u32[]{:S(2)}, u32[]{:S(2)}) collective-permute-start(bf16[64,1536]{1,0:T(8,128)(2,1)} %get-tuple-element.206), channel_id=1, source_target_pairs={{0,8},{4,12},{8,0},{12,4},{1,9},{5,13},{9,1},{13,5},{2,10},{6,14},... | collective-permute-start | bytes 589832 | tf_op jit(solution)/shard_map/cond/branch_1_fun/ppermute | solution.py:161
  27.8 10.9 %collective-permute-start.13 = (bf16[128,1536]{1,0:T(8,128)(2,1)S(1)}, bf16[128,1536]{1,0:T(8,128)(2,1)S(1)}, u32[]{:S(2)}, u32[]{:S(2)}) collective-permute-start(bf16[128,1536]{1,0:T(8,128)(2,1)S(1)} %add_convert_fusion.1), channel_id=1, source_target_pairs={{0,2},{1,3},{2,0},{3,1},{4,6},{5,7},{6,4},{7,5},{8,10},{9,11},{10,... | collective-permute-start | bytes 1179656 | tf_op jit(solution)/shard_map/cond/branch_1_fun/ppermute | solution.py:165
  29.3 9.3 %copy-start.7 = (bf16[256,1536]{1,0:T(8,128)(2,1)S(1)}, bf16[256,1536]{1,0:T(8,128)(2,1)}, u32[]{:S(2)}) copy-start(bf16[256,1536]{1,0:T(8,128)(2,1)} %copy-done.6) | copy-start | bytes 2359300 | tf_op jit(solution)/shard_map/cond
  29.3 10.2 %copy-start.1 = (bf16[128,6144]{1,0:T(8,128)(2,1)S(1)}, bf16[128,6144]{1,0:T(8,128)(2,1)}, u32[]{:S(2)}) copy-start(bf16[128,6144]{1,0:T(8,128)(2,1)} %get-tuple-element.56.own) | copy-start | bytes 4718596 | tf_op jit(solution)/shard_map/cond
  32.3 7.2 %collective-permute-start.11 = (bf16[64,1536]{1,0:T(8,128)(2,1)}, bf16[64,1536]{1,0:T(8,128)(2,1)}, u32[]{:S(2)}, u32[]{:S(2)}) collective-permute-start(bf16[64,1536]{1,0:T(8,128)(2,1)} %collective-permute-done.8.refs_2_), channel_id=1, source_target_pairs={{0,1},{1,0},{2,3},{3,2},{4,5},{5,4},{6,7},{7,6},{8,9},{9,8},{10,11... | collective-permute-start | bytes 589832 | tf_op jit(solution)/shard_map/cond/branch_1_fun/ppermute | solution.py:165
  37.5 2.0 %collective-permute-start.10 = (bf16[64,1536]{1,0:T(8,128)(2,1)}, bf16[64,1536]{1,0:T(8,128)(2,1)}, u32[]{:S(2)}, u32[]{:S(2)}) collective-permute-start(bf16[64,1536]{1,0:T(8,128)(2,1)} %collective-permute-done.7.refs_1_), channel_id=1, source_target_pairs={{0,1},{1,0},{2,3},{3,2},{4,5},{5,4},{6,7},{7,6},{8,9},{9,8},{10,11... | collective-permute-start | bytes 589832 | tf_op jit(solution)/shard_map/cond/branch_1_fun/ppermute | solution.py:165
  42.9 24.5 %collective-permute-start.17 = (bf16[864,512]{1,0:T(8,128)(2,1)}, bf16[864,512]{1,0:T(8,128)(2,1)S(1)}, u32[]{:S(2)}, u32[]{:S(2)}) collective-permute-start(bf16[864,512]{1,0:T(8,128)(2,1)} %get-tuple-element.179), channel_id=1, source_target_pairs={{0,16},{16,0},{1,17},{17,1},{2,18},{18,2},{3,19},{19,3},{4,20},{20... | collective-permute-start | bytes 2654216 | tf_op jit(solution)/shard_map/ppermute | solution.py:149
  43.4 28.6 %collective-permute-start.16 = (bf16[288,512]{1,0:T(8,128)(2,1)}, bf16[288,512]{1,0:T(8,128)(2,1)S(1)}, u32[]{:S(2)}, u32[]{:S(2)}) collective-permute-start(bf16[288,512]{1,0:T(8,128)(2,1)} %get-tuple-element.178), channel_id=1, source_target_pairs={{0,16},{16,0},{1,17},{17,1},{2,18},{18,2},{3,19},{19,3},{4,20},{20... | collective-permute-start | bytes 884744 | tf_op jit(solution)/shard_map/ppermute | solution.py:149
  46.3 17.3 %collective-permute-start = (bf16[320,256]{1,0:T(8,128)(2,1)}, bf16[320,256]{1,0:T(8,128)(2,1)S(1)}, u32[]{:S(2)}, u32[]{:S(2)}) collective-permute-start(bf16[320,256]{1,0:T(8,128)(2,1)} %get-tuple-element.71), channel_id=1, source_target_pairs={{0,12},{4,0},{8,4},{12,8},{1,13},{5,1},{9,5},{13,9},{2,14},{6,2},{... | collective-permute-start | bytes 491528 | tf_op jit(solution)/shard_map/cond/branch_1_fun/ppermute | solution.py:161
  49.8 14.2 %collective-permute-start.1 = (bf16[320,256]{1,0:T(8,128)(2,1)}, bf16[320,256]{1,0:T(8,128)(2,1)S(1)}, u32[]{:S(2)}, u32[]{:S(2)}) collective-permute-start(bf16[320,256]{1,0:T(8,128)(2,1)} %get-tuple-element.72), channel_id=1, source_target_pairs={{0,8},{4,12},{8,0},{12,4},{1,9},{5,13},{9,1},{13,5},{2,10},{6,14},... | collective-permute-start | bytes 491528 | tf_op jit(solution)/shard_map/cond/branch_1_fun/ppermute | solution.py:161
  50.0 14.0 %collective-permute-start.2 = (bf16[320,256]{1,0:T(8,128)(2,1)}, bf16[320,256]{1,0:T(8,128)(2,1)S(1)}, u32[]{:S(2)}, u32[]{:S(2)}) collective-permute-start(bf16[320,256]{1,0:T(8,128)(2,1)} %get-tuple-element.73), channel_id=1, source_target_pairs={{0,4},{4,8},{8,12},{12,0},{1,5},{5,9},{9,13},{13,1},{2,6},{6,10},{... | collective-permute-start | bytes 491528 | tf_op jit(solution)/shard_map/cond/branch_1_fun/ppermute | solution.py:161
  52.0 7.2 %copy-start.2 = (bf16[128,6144]{1,0:T(8,128)(2,1)S(1)}, bf16[128,6144]{1,0:T(8,128)(2,1)}, u32[]{:S(2)}) copy-start(bf16[128,6144]{1,0:T(8,128)(2,1)} %get-tuple-element.82.own) | copy-start | bytes 4718596 | tf_op jit(solution)/shard_map/cond
  65.7 5.4 %copy-start.8 = (bf16[32,6144]{1,0:T(8,128)(2,1)}, bf16[32,6144]{1,0:T(8,128)(2,1)S(1)}, u32[]{:S(2)}) copy-start(bf16[32,6144]{1,0:T(8,128)(2,1)S(1)} %get-tuple-element.143) | copy-start | bytes 1179652
  65.7 5.4 %copy-start.9 = (bf16[128,256]{1,0:T(8,128)(2,1)}, bf16[128,256]{1,0:T(8,128)(2,1)S(1)}, u32[]{:S(2)}) copy-start(bf16[128,256]{1,0:T(8,128)(2,1)S(1)} %get-tuple-element.142) | copy-start | bytes 196612
  65.8 7.5 %collective-permute-start.15 = (bf16[96,512]{1,0:T(8,128)(2,1)S(1)}, bf16[96,512]{1,0:T(8,128)(2,1)S(1)}, u32[]{:S(2)}, u32[]{:S(2)}) collective-permute-start(bf16[96,512]{1,0:T(8,128)(2,1)S(1)} %get-tuple-element.177), channel_id=1, source_target_pairs={{0,16},{16,0},{1,17},{17,1},{2,18},{18,2},{3,19},{19,3},{4,20},{20... | collective-permute-start | bytes 294920 | tf_op jit(solution)/shard_map/ppermute | solution.py:149
  67.3 4.6 %copy-start.4 = (f32[384,512]{1,0:T(8,128)S(1)}, f32[384,512]{1,0:T(8,128)}, u32[]{:S(2)}) copy-start(f32[384,512]{1,0:T(8,128)} %copy-done.3) | copy-start | bytes 2359300
  (4 other events, 9.2 us)

commit v8 on v7

--- a/solution.py
+++ b/solution.py
@@ -13,7 +13,7 @@
 BF16 = jnp.bfloat16
 units = 32
 late_parts = 2
-chunk_units = ((0, 19, 6), (19, 9, 3), (28, 3, None), (31, 1, None))
+chunk_units = ((0, 19, 6), (19, 10, 4), (29, 2, None), (31, 1, None))
 
 
 def nesterov(frag_sum, outer, momentum, islands):

time: 74.6 us -> 74.6 us (level)
  no operation moved by 1% of the time
where the time goes in v8:
time: 74.6 us; the launch traced here: 74 us
  Pallas kernels  24.7 us (33%)
  starting transfers between devices  23.5 us (32%)
  waiting for transfers between devices  12.5 us (17%)
  local copies, waits for them, and re-layouts  4.53 us (6%)
  other arithmetic  4.14 us (6%)
  matrix products  3.73 us (5%)
    ppermute x9, starting transfers between devices, shifted(): return lax.ppermute(x, axis, [(i, (i + step) % n) for i in range(n)])  14.7 us
    pallas_call x2, Pallas kernels, update(): pl.pallas_call(functools.partial(update_kernel, islands, first, cuts), in...  11.4 us
    ppermute x9, waiting for transfers between devices, shifted(): return lax.ppermute(x, axis, [(i, (i + step) % n) for i in range(n)])  9.28 us
    pallas_call x3, Pallas kernels, local_call(): pl.pallas_call(kernel, grid_spec=pltpu.PrefetchScalarGridSpec(num_scalar_...  7.6 us
    ppermute x4, starting transfers between devices, swapped(): return lax.ppermute(piece, 'island', [(0, 1), (1, 0)])  6.64 us
    pallas_call x2, Pallas kernels, pieces_of(): pl.pallas_call(functools.partial(piece_kernel, parts), in_specs=[pl.Block...  3.92 us
    dot_general x3, matrix products, part_of(): lax.dot_general(rows_of.reshape(-1, cots.shape[2]), weight, (((1,), (1,))...  3.73 us
    dynamic_slice x2, local copies, waits for them, and re-layouts, columns_for(): lax.dynamic_slice(tokens, (core * half, lax.rem(me + s, lax.axis_size('fs...  2.73 us
  transfers between devices with their start and end apart: 18, of which 9 were waited for; matrix products, arithmetic and copies ran while one was open for 17% of the time, Pallas kernels for 30%

profile of v8, /device:TPU:0, one launch (start us, length us, event | category | flops | bytes accessed | tf_op | source)
XLA Modules:
  0.0 74.0 jit_solution(13555678566953525472)
XLA Ops:
  2.1 3.0 %collective-permute-start.14 = (bf16[1824,512]{1,0:T(8,128)(2,1)S(1)}, bf16[1824,512]{1,0:T(8,128)(2,1)}, u32[]{:S(2)}, u32[]{:S(2)}) collective-permute-start(bf16[1824,512]{1,0:T(8,128)(2,1)S(1)} %shard_map.102), channel_id=1, source_target_pairs={{0,16},{16,0},{1,17},{17,1},{2,18},{18,2},{3,19},{19,3},{4,20},{20... | collective-permute-start | bytes 5603336 | tf_op jit(solution)/shard_map/ppermute | solution.py:149
  5.2 15.0 %conditional.3 = (bf16[4,128,256]{2,1,0:T(8,128)(2,1)}, bf16[256,1536]{1,0:T(8,128)(2,1)S(1)}, bf16[64,1536]{1,0:T(8,128)(2,1)}) conditional(s32[]{:T(128)} %convert_element_type.26, () %tuple.41, (bf16[128,256]{1,0:T(8,128)(2,1)}, bf16[1536,256]{1,0:T(8,128)(2,1)}, bf16[128,6144]{1,0:T(8,128)(2,1)}) %tuple.61), branch_computations={%region_0.0_spmd, %region_1.0_spmd} | conditional | flops 202178576 | bytes 4719186 | solution.py:154
  5.2 2.6 %collective-permute-start.4 = (bf16[128,256]{1,0:T(8,128)(2,1)}, bf16[128,256]{1,0:T(8,128)(2,1)S(1)}, u32[]{:S(2)}, u32[]{:S(2)}) collective-permute-start(bf16[128,256]{1,0:T(8,128)(2,1)} %get-tuple-element.200), channel_id=1, source_target_pairs={{0,8},{4,12},{8,0},{12,4},{1,9},{5,13},{9,1},{13,5},{2,10},{6,14},... | collective-permute-start | bytes 196616 | tf_op jit(solution)/shard_map/cond/branch_1_fun/ppermute | solution.py:161
  7.7 1.6 %collective-permute-start.3 = (bf16[128,256]{1,0:T(8,128)(2,1)}, bf16[128,256]{1,0:T(8,128)(2,1)S(1)}, u32[]{:S(2)}, u32[]{:S(2)}) collective-permute-start(bf16[128,256]{1,0:T(8,128)(2,1)} %get-tuple-element.200), channel_id=1, source_target_pairs={{0,4},{4,8},{8,12},{12,0},{1,5},{5,9},{9,13},{13,1},{2,6},{6,10},{... | collective-permute-start | bytes 196616 | tf_op jit(solution)/shard_map/cond/branch_1_fun/ppermute | solution.py:161
  9.3 2.2 %collective-permute-start.5 = (bf16[128,256]{1,0:T(8,128)(2,1)}, bf16[128,256]{1,0:T(8,128)(2,1)S(1)}, u32[]{:S(2)}, u32[]{:S(2)}) collective-permute-start(bf16[128,256]{1,0:T(8,128)(2,1)} %get-tuple-element.200), channel_id=1, source_target_pairs={{0,12},{4,0},{8,4},{12,8},{1,13},{5,1},{9,5},{13,9},{2,14},{6,2},{... | collective-permute-start | bytes 196616 | tf_op jit(solution)/shard_map/cond/branch_1_fun/ppermute | solution.py:161
  12.6 1.6 %collective-permute-done.3 = bf16[128,256]{1,0:T(8,128)(2,1)S(1)} collective-permute-done((bf16[128,256]{1,0:T(8,128)(2,1)}, bf16[128,256]{1,0:T(8,128)(2,1)S(1)}, u32[]{:S(2)}, u32[]{:S(2)}) %collective-permute-start.3) | collective-permute-done | bytes 65568 | tf_op jit(solution)/shard_map/cond/branch_1_fun/ppermute | solution.py:161
  14.5 1.6 %pad_maximum_fusion = bf16[4,128,256]{2,1,0:T(8,128)(2,1)} fusion(bf16[1,128,256]{2,1,0:T(8,128)(2,1)S(1)} %bitcast.50, bf16[1,128,256]{2,1,0:T(8,128)(2,1)S(1)} %bitcast.48, bf16[1,128,256]{2,1,0:T(8,128)(2,1)S(1)} %bitcast.49, bf16[1,128,256]{2,1,0:T(8,128)(2,1)} %bitcast.47), kind=kLoop, calls=%fused_computation.1 | loop fusion | flops 393216 | bytes 524288 | tf_op jit(solution)/shard_map/cond/branch_1_fun/stack | solution.py:281
  18.5 1.6 %collective-permute-done.6 = bf16[64,1536]{1,0:T(8,128)(2,1)} collective-permute-done((bf16[64,1536]{1,0:T(8,128)(2,1)S(1)}, bf16[64,1536]{1,0:T(8,128)(2,1)}, u32[]{:S(2)}, u32[]{:S(2)}) %collective-permute-start.6) | collective-permute-done | bytes 196640 | tf_op jit(solution)/shard_map/cond/branch_1_fun/ppermute | solution.py:161
  20.1 22.7 %conditional.4 = (bf16[64,1536]{1,0:T(8,128)(2,1)}, bf16[64,1536]{1,0:T(8,128)(2,1)}, bf16[64,1536]{1,0:T(8,128)(2,1)}, bf16[64,1536]{1,0:T(8,128)(2,1)}, bf16[6...) conditional(s32[]{:T(128)} %convert_element_type.26, () %tuple.40, ...), branch_computations={%region_2.0_spmd, %region_3.0_spmd} | conditional | flops 6202899456 | bytes 30671888 | solution.py:154
  20.6 1.8 %fusion.2 = (bf16[64,1536]{1,0:T(8,128)(2,1)}, bf16[64,1536]{1,0:T(8,128)(2,1)}) fusion(bf16[128,6144]{1,0:T(8,128)(2,1)} %get-tuple-element.56.own, s32[]{:T(128)S(6)} %select_n.23, s32[]{:T(128)S(6)} %select_n.25, s32[]{:T(128)S(6)} %select_n.24), kind=kLoop, calls=%fused_computation.15 | loop fusion | bytes 786444 | tf_op jit(solution)/shard_map/cond/branch_1_fun/dynamic_slice | solution.py:277
  22.4 2.6 %collective-permute-start.8 = (bf16[64,1536]{1,0:T(8,128)(2,1)}, bf16[64,1536]{1,0:T(8,128)(2,1)}, u32[]{:S(2)}, u32[]{:S(2)}) collective-permute-start(bf16[64,1536]{1,0:T(8,128)(2,1)} %get-tuple-element.205), channel_id=1, source_target_pairs={{0,12},{4,0},{8,4},{12,8},{1,13},{5,1},{9,5},{13,9},{2,14},{6,2},{... | collective-permute-start | bytes 589832 | tf_op jit(solution)/shard_map/cond/branch_1_fun/ppermute | solution.py:161
  25.9 1.8 %add_convert_fusion.1 = bf16[128,1536]{1,0:T(8,128)(2,1)S(1)} fusion(bf16[256,1536]{1,0:T(8,128)(2,1)S(1)} %collective-permute-done.12, bf16[128,256]{1,0:T(8,128)(2,1)S(1)} %bitcast.46, bf16[1536,256]{1,0:T(8,128)(2,1)} %get-tuple-element.58.refs_6_), kind=kOutput, calls=%fused_computation.6 | convolution fusion | flops 101253120 | bytes 1638400 | tf_op jit(solution)/shard_map/cond/branch_1_fun/dot_general | solution.py:177
  27.8 1.6 %collective-permute-start.13 = (bf16[128,1536]{1,0:T(8,128)(2,1)S(1)}, bf16[128,1536]{1,0:T(8,128)(2,1)S(1)}, u32[]{:S(2)}, u32[]{:S(2)}) collective-permute-start(bf16[128,1536]{1,0:T(8,128)(2,1)S(1)} %add_convert_fusion.1), channel_id=1, source_target_pairs={{0,2},{1,3},{2,0},{3,1},{4,6},{5,7},{6,4},{7,5},{8,10},{9,11},{10,... | collective-permute-start | bytes 1179656 | tf_op jit(solution)/shard_map/cond/branch_1_fun/ppermute | solution.py:165
  29.3 2.4 %branch_1_fun.6 = (bf16[960,512]{1,0:T(8,128)(2,1)}, bf16[192,512]{1,0:T(8,128)(2,1)}, bf16[96,512]{1,0:T(8,128)(2,1)S(1)}) custom-call(bf16[3072,512]{1,0:T(8,128)(2,1)} %bitcast.32), custom_call_target="tpu_custom_call" | custom-call | flops 6000000000 | tf_op jit(solution)/shard_map/cond/branch_1_fun/pallas_call | solution.py:137
  32.3 5.1 %collective-permute-done.7.refs_1_ = bf16[64,1536]{1,0:T(8,128)(2,1)} collective-permute-done((bf16[64,1536]{1,0:T(8,128)(2,1)}, bf16[64,1536]{1,0:T(8,128)(2,1)}, u32[]{:S(2)}, u32[]{:S(2)}) %collective-permute-start.7) | collective-permute-done | bytes 196640 | tf_op jit(solution)/shard_map/cond/branch_1_fun/ppermute | solution.py:161
  39.5 3.4 %branch_1_fun.5 = (f32[128,256]{1,0:T(8,128)}, bf16[320,256]{1,0:T(8,128)(2,1)}, bf16[320,256]{1,0:T(8,128)(2,1)}, bf16[320,256]{1,0:T(8,128)(2,1)}) custom-call(s32[2]{0:T(128)S(1)} %pad_add_fusion.place, bf16[128,6144]{1,0:T(8,128)(2,1)S(1)} %copy-done.1, bf16[64,1536]{1,0:T(8,128)(2,1)} %get-tuple-element.57.refs_0_, ...), custom_call_target="tpu_custom_call" | custom-call | tf_op jit(solution)/shard_map/cond/branch_1_fun/pallas_call | solution.py:259
  46.3 19.4 %conditional.5 = (bf16[128,256]{1,0:T(8,128)(2,1)S(1)}, bf16[32,6144]{1,0:T(8,128)(2,1)S(1)}, f32[3072,512]{1,0:T(8,128)}, f32[3072,512]{1,0:T(8,128)}, f32[288,...) conditional(s32[]{:T(128)} %convert_element_type.26, () %tuple.39, ...), branch_computations={%region_4.0_spmd, %region_5.0_spmd} | conditional | flops 1327117 | bytes 15007822 | solution.py:154
  46.3 3.5 %collective-permute-start = (bf16[320,256]{1,0:T(8,128)(2,1)}, bf16[320,256]{1,0:T(8,128)(2,1)S(1)}, u32[]{:S(2)}, u32[]{:S(2)}) collective-permute-start(bf16[320,256]{1,0:T(8,128)(2,1)} %get-tuple-element.71), channel_id=1, source_target_pairs={{0,12},{4,0},{8,4},{12,8},{1,13},{5,1},{9,5},{13,9},{2,14},{6,2},{... | collective-permute-start | bytes 491528 | tf_op jit(solution)/shard_map/cond/branch_1_fun/ppermute | solution.py:161
  50.0 1.9 %collective-permute-start.2 = (bf16[320,256]{1,0:T(8,128)(2,1)}, bf16[320,256]{1,0:T(8,128)(2,1)S(1)}, u32[]{:S(2)}, u32[]{:S(2)}) collective-permute-start(bf16[320,256]{1,0:T(8,128)(2,1)} %get-tuple-element.73), channel_id=1, source_target_pairs={{0,4},{4,8},{8,12},{12,0},{1,5},{5,9},{9,13},{13,1},{2,6},{6,10},{... | collective-permute-start | bytes 491528 | tf_op jit(solution)/shard_map/cond/branch_1_fun/ppermute | solution.py:161
  52.0 7.2 %branch_1_fun.8 = (f32[3072,512]{1,0:T(8,128)}, f32[3072,512]{1,0:T(8,128)}) custom-call(bf16[1824,512]{1,0:T(8,128)(2,1)} %get-tuple-element.76.theirs, bf16[3072,512]{1,0:T(8,128)(2,1)} %bitcast.33, f32[3072,512]{1,0:T(8,128)} %bitcast.36, f32[3072,512]{1,0:T(8,128)} %bitcast.39), custom_call_target="tpu_custom_call" | custom-call | tf_op jit(solution)/shard_map/cond/branch_1_fun/pallas_call | solution.py:101
  59.3 2.6 %branch_1_fun.9 = bf16[1536,256]{1,0:T(8,128)(2,1)S(1)} custom-call(s32[2]{0:T(128)S(1)} %pad_add_fusion.1.place, bf16[128,6144]{1,0:T(8,128)(2,1)S(1)} %copy-done.2, bf16[64,1536]{1,0:T(8,128)(2,1)} %get-tuple-element.83.refs_0_, bf16[64,1536]{1,0:T(8,128)(2,1)} %get-tuple-element.84.refs_1_, bf16[64,1536]{1,0:T(8,128)(2,1)} %get-tuple-element.85.refs_2_, ...), custom_call_target="tpu_custom_call" | custom-call | tf_op jit(solution)/shard_map/cond/branch_1_fun/pallas_call | solution.py:259
  64.0 1.7 %branch_1_fun.7 = (bf16[128,256]{1,0:T(8,128)(2,1)S(1)}, bf16[32,6144]{1,0:T(8,128)(2,1)S(1)}) custom-call(s32[2]{0:T(128)S(1)} %pad_add_fusion.1.place, f32[128,256]{1,0:T(8,128)} %get-tuple-element.69.keys_own, bf16[128,1536]{1,0:T(8,128)(2,1)} %get-tuple-element.70.summed, bf16[320,256]{1,0:T(8,128)(2,1)S(1)} %collective-permute-done.refs_0_, ...), custom_call_target="tpu_custom_call" | custom-call | tf_op jit(solution)/shard_map/cond/branch_1_fun/pallas_call | solution.py:259
  65.7 1.6 %collective-permute-start.15 = (bf16[96,512]{1,0:T(8,128)(2,1)S(1)}, bf16[96,512]{1,0:T(8,128)(2,1)S(1)}, u32[]{:S(2)}, u32[]{:S(2)}) collective-permute-start(bf16[96,512]{1,0:T(8,128)(2,1)S(1)} %get-tuple-element.177), channel_id=1, source_target_pairs={{0,16},{16,0},{1,17},{17,1},{2,18},{18,2},{3,19},{19,3},{4,20},{20... | collective-permute-start | bytes 294920 | tf_op jit(solution)/shard_map/ppermute | solution.py:149
  67.7 4.2 %shard_map.103 = (f32[3072,512]{1,0:T(8,128)}, f32[3072,512]{1,0:T(8,128)}) custom-call(bf16[960,512]{1,0:T(8,128)(2,1)S(1)} %collective-permute-done.17.theirs, bf16[3072,512]{1,0:T(8,128)(2,1)} %bitcast.31, f32[3072,512]{1,0:T(8,128)} %bitcast.35, f32[3072,512]{1,0:T(8,128)} %bitcast.38, ...), custom_call_target="tpu_custom_call", output_to_operand_aliasing={{0}: (4, {}), {1}: (5, {})} | custom-call | tf_op jit(solution)/shard_map/pallas_call | solution.py:101
  (53 shorter events, 17.5 us)
Async XLA Ops:
  2.1 44.2 %collective-permute-start.14 = (bf16[1824,512]{1,0:T(8,128)(2,1)S(1)}, bf16[1824,512]{1,0:T(8,128)(2,1)}, u32[]{:S(2)}, u32[]{:S(2)}) collective-permute-start(bf16[1824,512]{1,0:T(8,128)(2,1)S(1)} %shard_map.102), channel_id=1, source_target_pairs={{0,16},{16,0},{1,17},{17,1},{2,18},{18,2},{3,19},{19,3},{4,20},{20... | collective-permute-start | bytes 5603336 | tf_op jit(solution)/shard_map/ppermute | solution.py:149
  5.2 7.4 %collective-permute-start.4 = (bf16[128,256]{1,0:T(8,128)(2,1)}, bf16[128,256]{1,0:T(8,128)(2,1)S(1)}, u32[]{:S(2)}, u32[]{:S(2)}) collective-permute-start(bf16[128,256]{1,0:T(8,128)(2,1)} %get-tuple-element.200), channel_id=1, source_target_pairs={{0,8},{4,12},{8,0},{12,4},{1,9},{5,13},{9,1},{13,5},{2,10},{6,14},... | collective-permute-start | bytes 196616 | tf_op jit(solution)/shard_map/cond/branch_1_fun/ppermute | solution.py:161
  7.7 6.4 %collective-permute-start.3 = (bf16[128,256]{1,0:T(8,128)(2,1)}, bf16[128,256]{1,0:T(8,128)(2,1)S(1)}, u32[]{:S(2)}, u32[]{:S(2)}) collective-permute-start(bf16[128,256]{1,0:T(8,128)(2,1)} %get-tuple-element.200), channel_id=1, source_target_pairs={{0,4},{4,8},{8,12},{12,0},{1,5},{5,9},{9,13},{13,1},{2,6},{6,10},{... | collective-permute-start | bytes 196616 | tf_op jit(solution)/shard_map/cond/branch_1_fun/ppermute | solution.py:161
  9.3 5.2 %collective-permute-start.5 = (bf16[128,256]{1,0:T(8,128)(2,1)}, bf16[128,256]{1,0:T(8,128)(2,1)S(1)}, u32[]{:S(2)}, u32[]{:S(2)}) collective-permute-start(bf16[128,256]{1,0:T(8,128)(2,1)} %get-tuple-element.200), channel_id=1, source_target_pairs={{0,12},{4,0},{8,4},{12,8},{1,13},{5,1},{9,5},{13,9},{2,14},{6,2},{... | collective-permute-start | bytes 196616 | tf_op jit(solution)/shard_map/cond/branch_1_fun/ppermute | solution.py:161
  12.5 7.6 %collective-permute-start.6 = (bf16[64,1536]{1,0:T(8,128)(2,1)S(1)}, bf16[64,1536]{1,0:T(8,128)(2,1)}, u32[]{:S(2)}, u32[]{:S(2)}) collective-permute-start(bf16[64,1536]{1,0:T(8,128)(2,1)S(1)} %dynamic_slice.16), channel_id=1, source_target_pairs={{0,4},{4,8},{8,12},{12,0},{1,5},{5,9},{9,13},{13,1},{2,6},{6,10},{... | collective-permute-start | bytes 589832 | tf_op jit(solution)/shard_map/cond/branch_1_fun/ppermute | solution.py:161
  20.1 5.8 %collective-permute-start.12 = (bf16[256,1536]{1,0:T(8,128)(2,1)S(1)}, bf16[256,1536]{1,0:T(8,128)(2,1)S(1)}, u32[]{:S(2)}, u32[]{:S(2)}) collective-permute-start(bf16[256,1536]{1,0:T(8,128)(2,1)S(1)} %get-tuple-element.60), channel_id=1, source_target_pairs={{0,1},{1,0},{2,3},{3,2},{4,5},{5,4},{6,7},{7,6},{8,9},{9,8},{10,11... | collective-permute-start | bytes 2359304 | tf_op jit(solution)/shard_map/cond/branch_1_fun/ppermute | solution.py:165
  20.1 19.4 %collective-permute-start.9 = (bf16[64,1536]{1,0:T(8,128)(2,1)}, bf16[64,1536]{1,0:T(8,128)(2,1)}, u32[]{:S(2)}, u32[]{:S(2)}) collective-permute-start(bf16[64,1536]{1,0:T(8,128)(2,1)} %get-tuple-element.57.refs_0_), channel_id=1, source_target_pairs={{0,1},{1,0},{2,3},{3,2},{4,5},{5,4},{6,7},{7,6},{8,9},{9,8},{10,11... | collective-permute-start | bytes 589832 | tf_op jit(solution)/shard_map/cond/branch_1_fun/ppermute | solution.py:165
  22.4 9.8 %collective-permute-start.8 = (bf16[64,1536]{1,0:T(8,128)(2,1)}, bf16[64,1536]{1,0:T(8,128)(2,1)}, u32[]{:S(2)}, u32[]{:S(2)}) collective-permute-start(bf16[64,1536]{1,0:T(8,128)(2,1)} %get-tuple-element.205), channel_id=1, source_target_pairs={{0,12},{4,0},{8,4},{12,8},{1,13},{5,1},{9,5},{13,9},{2,14},{6,2},{... | collective-permute-start | bytes 589832 | tf_op jit(solution)/shard_map/cond/branch_1_fun/ppermute | solution.py:161
  25.0 12.4 %collective-permute-start.7 = (bf16[64,1536]{1,0:T(8,128)(2,1)}, bf16[64,1536]{1,0:T(8,128)(2,1)}, u32[]{:S(2)}, u32[]{:S(2)}) collective-permute-start(bf16[64,1536]{1,0:T(8,128)(2,1)} %get-tuple-element.206), channel_id=1, source_target_pairs={{0,8},{4,12},{8,0},{12,4},{1,9},{5,13},{9,1},{13,5},{2,10},{6,14},... | collective-permute-start | bytes 589832 | tf_op jit(solution)/shard_map/cond/branch_1_fun/ppermute | solution.py:161
  25.9 3.4 %copy-start.4 = (bf16[256,1536]{1,0:T(8,128)(2,1)}, bf16[256,1536]{1,0:T(8,128)(2,1)S(1)}, u32[]{:S(2)}) copy-start(bf16[256,1536]{1,0:T(8,128)(2,1)S(1)} %collective-permute-done.12) | copy-start | bytes 2359300 | tf_op jit(solution)/shard_map/cond
  27.8 10.9 %collective-permute-start.13 = (bf16[128,1536]{1,0:T(8,128)(2,1)S(1)}, bf16[128,1536]{1,0:T(8,128)(2,1)S(1)}, u32[]{:S(2)}, u32[]{:S(2)}) collective-permute-start(bf16[128,1536]{1,0:T(8,128)(2,1)S(1)} %add_convert_fusion.1), channel_id=1, source_target_pairs={{0,2},{1,3},{2,0},{3,1},{4,6},{5,7},{6,4},{7,5},{8,10},{9,11},{10,... | collective-permute-start | bytes 1179656 | tf_op jit(solution)/shard_map/cond/branch_1_fun/ppermute | solution.py:165
  29.3 9.3 %copy-start.5 = (bf16[256,1536]{1,0:T(8,128)(2,1)S(1)}, bf16[256,1536]{1,0:T(8,128)(2,1)}, u32[]{:S(2)}) copy-start(bf16[256,1536]{1,0:T(8,128)(2,1)} %copy-done.4) | copy-start | bytes 2359300 | tf_op jit(solution)/shard_map/cond
  29.3 10.2 %copy-start.1 = (bf16[128,6144]{1,0:T(8,128)(2,1)S(1)}, bf16[128,6144]{1,0:T(8,128)(2,1)}, u32[]{:S(2)}) copy-start(bf16[128,6144]{1,0:T(8,128)(2,1)} %get-tuple-element.56.own) | copy-start | bytes 4718596 | tf_op jit(solution)/shard_map/cond
  32.3 7.3 %collective-permute-start.11 = (bf16[64,1536]{1,0:T(8,128)(2,1)}, bf16[64,1536]{1,0:T(8,128)(2,1)}, u32[]{:S(2)}, u32[]{:S(2)}) collective-permute-start(bf16[64,1536]{1,0:T(8,128)(2,1)} %collective-permute-done.8.refs_2_), channel_id=1, source_target_pairs={{0,1},{1,0},{2,3},{3,2},{4,5},{5,4},{6,7},{7,6},{8,9},{9,8},{10,11... | collective-permute-start | bytes 589832 | tf_op jit(solution)/shard_map/cond/branch_1_fun/ppermute | solution.py:165
  37.5 2.0 %collective-permute-start.10 = (bf16[64,1536]{1,0:T(8,128)(2,1)}, bf16[64,1536]{1,0:T(8,128)(2,1)}, u32[]{:S(2)}, u32[]{:S(2)}) collective-permute-start(bf16[64,1536]{1,0:T(8,128)(2,1)} %collective-permute-done.7.refs_1_), channel_id=1, source_target_pairs={{0,1},{1,0},{2,3},{3,2},{4,5},{5,4},{6,7},{7,6},{8,9},{9,8},{10,11... | collective-permute-start | bytes 589832 | tf_op jit(solution)/shard_map/cond/branch_1_fun/ppermute | solution.py:165
  42.9 24.8 %collective-permute-start.17 = (bf16[960,512]{1,0:T(8,128)(2,1)}, bf16[960,512]{1,0:T(8,128)(2,1)S(1)}, u32[]{:S(2)}, u32[]{:S(2)}) collective-permute-start(bf16[960,512]{1,0:T(8,128)(2,1)} %get-tuple-element.179), channel_id=1, source_target_pairs={{0,16},{16,0},{1,17},{17,1},{2,18},{18,2},{3,19},{19,3},{4,20},{20... | collective-permute-start | bytes 2949128 | tf_op jit(solution)/shard_map/ppermute | solution.py:149
  43.4 28.6 %collective-permute-start.16 = (bf16[192,512]{1,0:T(8,128)(2,1)}, bf16[192,512]{1,0:T(8,128)(2,1)S(1)}, u32[]{:S(2)}, u32[]{:S(2)}) collective-permute-start(bf16[192,512]{1,0:T(8,128)(2,1)} %get-tuple-element.178), channel_id=1, source_target_pairs={{0,16},{16,0},{1,17},{17,1},{2,18},{18,2},{3,19},{19,3},{4,20},{20... | collective-permute-start | bytes 589832 | tf_op jit(solution)/shard_map/ppermute | solution.py:149
  46.3 17.1 %collective-permute-start = (bf16[320,256]{1,0:T(8,128)(2,1)}, bf16[320,256]{1,0:T(8,128)(2,1)S(1)}, u32[]{:S(2)}, u32[]{:S(2)}) collective-permute-start(bf16[320,256]{1,0:T(8,128)(2,1)} %get-tuple-element.71), channel_id=1, source_target_pairs={{0,12},{4,0},{8,4},{12,8},{1,13},{5,1},{9,5},{13,9},{2,14},{6,2},{... | collective-permute-start | bytes 491528 | tf_op jit(solution)/shard_map/cond/branch_1_fun/ppermute | solution.py:161
  49.8 14.2 %collective-permute-start.1 = (bf16[320,256]{1,0:T(8,128)(2,1)}, bf16[320,256]{1,0:T(8,128)(2,1)S(1)}, u32[]{:S(2)}, u32[]{:S(2)}) collective-permute-start(bf16[320,256]{1,0:T(8,128)(2,1)} %get-tuple-element.72), channel_id=1, source_target_pairs={{0,8},{4,12},{8,0},{12,4},{1,9},{5,13},{9,1},{13,5},{2,10},{6,14},... | collective-permute-start | bytes 491528 | tf_op jit(solution)/shard_map/cond/branch_1_fun/ppermute | solution.py:161
  50.0 14.0 %collective-permute-start.2 = (bf16[320,256]{1,0:T(8,128)(2,1)}, bf16[320,256]{1,0:T(8,128)(2,1)S(1)}, u32[]{:S(2)}, u32[]{:S(2)}) collective-permute-start(bf16[320,256]{1,0:T(8,128)(2,1)} %get-tuple-element.73), channel_id=1, source_target_pairs={{0,4},{4,8},{8,12},{12,0},{1,5},{5,9},{9,13},{13,1},{2,6},{6,10},{... | collective-permute-start | bytes 491528 | tf_op jit(solution)/shard_map/cond/branch_1_fun/ppermute | solution.py:161
  52.0 7.2 %copy-start.2 = (bf16[128,6144]{1,0:T(8,128)(2,1)S(1)}, bf16[128,6144]{1,0:T(8,128)(2,1)}, u32[]{:S(2)}) copy-start(bf16[128,6144]{1,0:T(8,128)(2,1)} %get-tuple-element.82.own) | copy-start | bytes 4718596 | tf_op jit(solution)/shard_map/cond
  65.7 6.3 %copy-start.6 = (bf16[32,6144]{1,0:T(8,128)(2,1)}, bf16[32,6144]{1,0:T(8,128)(2,1)S(1)}, u32[]{:S(2)}) copy-start(bf16[32,6144]{1,0:T(8,128)(2,1)S(1)} %get-tuple-element.143) | copy-start | bytes 1179652
  65.7 6.3 %copy-start.7 = (bf16[128,256]{1,0:T(8,128)(2,1)}, bf16[128,256]{1,0:T(8,128)(2,1)S(1)}, u32[]{:S(2)}) copy-start(bf16[128,256]{1,0:T(8,128)(2,1)S(1)} %get-tuple-element.142) | copy-start | bytes 196612
  65.7 7.5 %collective-permute-start.15 = (bf16[96,512]{1,0:T(8,128)(2,1)S(1)}, bf16[96,512]{1,0:T(8,128)(2,1)S(1)}, u32[]{:S(2)}, u32[]{:S(2)}) collective-permute-start(bf16[96,512]{1,0:T(8,128)(2,1)S(1)} %get-tuple-element.177), channel_id=1, source_target_pairs={{0,16},{16,0},{1,17},{17,1},{2,18},{18,2},{3,19},{19,3},{4,20},{20... | collective-permute-start | bytes 294920 | tf_op jit(solution)/shard_map/ppermute | solution.py:149
  (2 other events, 4.6 us)

commit v9 on v8

--- a/solution.py
+++ b/solution.py
@@ -131,7 +131,7 @@
     shapes = [(chunk_units[k][1] * unit, cols) for k in members]
     parts = []
     for k, (rows, _) in zip(members, shapes):
-        cuts = list(range(0, rows, 10 * unit)) + [rows]
+        cuts = list(range(0, rows, 7 * unit)) + [rows]
         parts.append((chunk_units[k][0] * unit, cuts))
     copies = sum(len(cuts) - 1 for _, cuts in parts)
     return pl.pallas_call(

time: 74.6 us -> 74.6 us (level)
  no operation moved by 1% of the time
where the time goes in v9:
time: 74.6 us; the launch traced here: 74 us
  Pallas kernels  24.7 us (33%)
  starting transfers between devices  23.5 us (32%)
  waiting for transfers between devices  12.5 us (17%)
  local copies, waits for them, and re-layouts  4.53 us (6%)
  other arithmetic  4.14 us (6%)
  matrix products  3.73 us (5%)
    ppermute x9, starting transfers between devices, shifted(): return lax.ppermute(x, axis, [(i, (i + step) % n) for i in range(n)])  14.7 us
    pallas_call x2, Pallas kernels, update(): pl.pallas_call(functools.partial(update_kernel, islands, first, cuts), in...  11.4 us
    ppermute x9, waiting for transfers between devices, shifted(): return lax.ppermute(x, axis, [(i, (i + step) % n) for i in range(n)])  9.28 us
    pallas_call x3, Pallas kernels, local_call(): pl.pallas_call(kernel, grid_spec=pltpu.PrefetchScalarGridSpec(num_scalar_...  7.61 us
    ppermute x4, starting transfers between devices, swapped(): return lax.ppermute(piece, 'island', [(0, 1), (1, 0)])  6.64 us
    pallas_call x2, Pallas kernels, pieces_of(): pl.pallas_call(functools.partial(piece_kernel, parts), in_specs=[pl.Block...  3.92 us
    dot_general x3, matrix products, part_of(): lax.dot_general(rows_of.reshape(-1, cots.shape[2]), weight, (((1,), (1,))...  3.73 us
    dynamic_slice x2, local copies, waits for them, and re-layouts, columns_for(): lax.dynamic_slice(tokens, (core * half, lax.rem(me + s, lax.axis_size('fs...  2.73 us
  transfers between devices with their start and end apart: 18, of which 9 were waited for; matrix products, arithmetic and copies ran while one was open for 17% of the time, Pallas kernels for 30%

profile of v9, /device:TPU:0, one launch (start us, length us, event | category | flops | bytes accessed | tf_op | source)
XLA Modules:
  0.0 74.0 jit_solution(7294455705861045776)
XLA Ops:
  2.1 3.0 %collective-permute-start.14 = (bf16[1824,512]{1,0:T(8,128)(2,1)S(1)}, bf16[1824,512]{1,0:T(8,128)(2,1)}, u32[]{:S(2)}, u32[]{:S(2)}) collective-permute-start(bf16[1824,512]{1,0:T(8,128)(2,1)S(1)} %shard_map.102), channel_id=1, source_target_pairs={{0,16},{16,0},{1,17},{17,1},{2,18},{18,2},{3,19},{19,3},{4,20},{20... | collective-permute-start | bytes 5603336 | tf_op jit(solution)/shard_map/ppermute | solution.py:149
  5.1 15.0 %conditional.3 = (bf16[4,128,256]{2,1,0:T(8,128)(2,1)}, bf16[256,1536]{1,0:T(8,128)(2,1)S(1)}, bf16[64,1536]{1,0:T(8,128)(2,1)}) conditional(s32[]{:T(128)} %convert_element_type.26, () %tuple.41, (bf16[128,256]{1,0:T(8,128)(2,1)}, bf16[1536,256]{1,0:T(8,128)(2,1)}, bf16[128,6144]{1,0:T(8,128)(2,1)}) %tuple.61), branch_computations={%region_0.0_spmd, %region_1.0_spmd} | conditional | flops 202178576 | bytes 4719186 | solution.py:154
  5.1 2.6 %collective-permute-start.4 = (bf16[128,256]{1,0:T(8,128)(2,1)}, bf16[128,256]{1,0:T(8,128)(2,1)S(1)}, u32[]{:S(2)}, u32[]{:S(2)}) collective-permute-start(bf16[128,256]{1,0:T(8,128)(2,1)} %get-tuple-element.200), channel_id=1, source_target_pairs={{0,8},{4,12},{8,0},{12,4},{1,9},{5,13},{9,1},{13,5},{2,10},{6,14},... | collective-permute-start | bytes 196616 | tf_op jit(solution)/shard_map/cond/branch_1_fun/ppermute | solution.py:161
  7.7 1.6 %collective-permute-start.3 = (bf16[128,256]{1,0:T(8,128)(2,1)}, bf16[128,256]{1,0:T(8,128)(2,1)S(1)}, u32[]{:S(2)}, u32[]{:S(2)}) collective-permute-start(bf16[128,256]{1,0:T(8,128)(2,1)} %get-tuple-element.200), channel_id=1, source_target_pairs={{0,4},{4,8},{8,12},{12,0},{1,5},{5,9},{9,13},{13,1},{2,6},{6,10},{... | collective-permute-start | bytes 196616 | tf_op jit(solution)/shard_map/cond/branch_1_fun/ppermute | solution.py:161
  9.3 2.2 %collective-permute-start.5 = (bf16[128,256]{1,0:T(8,128)(2,1)}, bf16[128,256]{1,0:T(8,128)(2,1)S(1)}, u32[]{:S(2)}, u32[]{:S(2)}) collective-permute-start(bf16[128,256]{1,0:T(8,128)(2,1)} %get-tuple-element.200), channel_id=1, source_target_pairs={{0,12},{4,0},{8,4},{12,8},{1,13},{5,1},{9,5},{13,9},{2,14},{6,2},{... | collective-permute-start | bytes 196616 | tf_op jit(solution)/shard_map/cond/branch_1_fun/ppermute | solution.py:161
  12.6 1.6 %collective-permute-done.3 = bf16[128,256]{1,0:T(8,128)(2,1)S(1)} collective-permute-done((bf16[128,256]{1,0:T(8,128)(2,1)}, bf16[128,256]{1,0:T(8,128)(2,1)S(1)}, u32[]{:S(2)}, u32[]{:S(2)}) %collective-permute-start.3) | collective-permute-done | bytes 65568 | tf_op jit(solution)/shard_map/cond/branch_1_fun/ppermute | solution.py:161
  14.5 1.6 %pad_maximum_fusion = bf16[4,128,256]{2,1,0:T(8,128)(2,1)} fusion(bf16[1,128,256]{2,1,0:T(8,128)(2,1)S(1)} %bitcast.50, bf16[1,128,256]{2,1,0:T(8,128)(2,1)S(1)} %bitcast.48, bf16[1,128,256]{2,1,0:T(8,128)(2,1)S(1)} %bitcast.49, bf16[1,128,256]{2,1,0:T(8,128)(2,1)} %bitcast.47), kind=kLoop, calls=%fused_computation.1 | loop fusion | flops 393216 | bytes 524288 | tf_op jit(solution)/shard_map/cond/branch_1_fun/stack | solution.py:281
  18.5 1.6 %collective-permute-done.6 = bf16[64,1536]{1,0:T(8,128)(2,1)} collective-permute-done((bf16[64,1536]{1,0:T(8,128)(2,1)S(1)}, bf16[64,1536]{1,0:T(8,128)(2,1)}, u32[]{:S(2)}, u32[]{:S(2)}) %collective-permute-start.6) | collective-permute-done | bytes 196640 | tf_op jit(solution)/shard_map/cond/branch_1_fun/ppermute | solution.py:161
  20.1 22.7 %conditional.4 = (bf16[64,1536]{1,0:T(8,128)(2,1)}, bf16[64,1536]{1,0:T(8,128)(2,1)}, bf16[64,1536]{1,0:T(8,128)(2,1)}, bf16[64,1536]{1,0:T(8,128)(2,1)}, bf16[6...) conditional(s32[]{:T(128)} %convert_element_type.26, () %tuple.40, ...), branch_computations={%region_2.0_spmd, %region_3.0_spmd} | conditional | flops 6202899456 | bytes 30671888 | solution.py:154
  20.6 1.8 %fusion.2 = (bf16[64,1536]{1,0:T(8,128)(2,1)}, bf16[64,1536]{1,0:T(8,128)(2,1)}) fusion(bf16[128,6144]{1,0:T(8,128)(2,1)} %get-tuple-element.56.own, s32[]{:T(128)S(6)} %select_n.23, s32[]{:T(128)S(6)} %select_n.25, s32[]{:T(128)S(6)} %select_n.24), kind=kLoop, calls=%fused_computation.15 | loop fusion | bytes 786444 | tf_op jit(solution)/shard_map/cond/branch_1_fun/dynamic_slice | solution.py:277
  22.4 2.6 %collective-permute-start.8 = (bf16[64,1536]{1,0:T(8,128)(2,1)}, bf16[64,1536]{1,0:T(8,128)(2,1)}, u32[]{:S(2)}, u32[]{:S(2)}) collective-permute-start(bf16[64,1536]{1,0:T(8,128)(2,1)} %get-tuple-element.205), channel_id=1, source_target_pairs={{0,12},{4,0},{8,4},{12,8},{1,13},{5,1},{9,5},{13,9},{2,14},{6,2},{... | collective-permute-start | bytes 589832 | tf_op jit(solution)/shard_map/cond/branch_1_fun/ppermute | solution.py:161
  25.9 1.8 %add_convert_fusion.1 = bf16[128,1536]{1,0:T(8,128)(2,1)S(1)} fusion(bf16[256,1536]{1,0:T(8,128)(2,1)S(1)} %collective-permute-done.12, bf16[128,256]{1,0:T(8,128)(2,1)S(1)} %bitcast.46, bf16[1536,256]{1,0:T(8,128)(2,1)} %get-tuple-element.58.refs_6_), kind=kOutput, calls=%fused_computation.6 | convolution fusion | flops 101253120 | bytes 1638400 | tf_op jit(solution)/shard_map/cond/branch_1_fun/dot_general | solution.py:177
  27.7 1.6 %collective-permute-start.13 = (bf16[128,1536]{1,0:T(8,128)(2,1)S(1)}, bf16[128,1536]{1,0:T(8,128)(2,1)S(1)}, u32[]{:S(2)}, u32[]{:S(2)}) collective-permute-start(bf16[128,1536]{1,0:T(8,128)(2,1)S(1)} %add_convert_fusion.1), channel_id=1, source_target_pairs={{0,2},{1,3},{2,0},{3,1},{4,6},{5,7},{6,4},{7,5},{8,10},{9,11},{10,... | collective-permute-start | bytes 1179656 | tf_op jit(solution)/shard_map/cond/branch_1_fun/ppermute | solution.py:165
  29.3 2.5 %branch_1_fun.6 = (bf16[960,512]{1,0:T(8,128)(2,1)}, bf16[192,512]{1,0:T(8,128)(2,1)}, bf16[96,512]{1,0:T(8,128)(2,1)S(1)}) custom-call(bf16[3072,512]{1,0:T(8,128)(2,1)} %bitcast.32), custom_call_target="tpu_custom_call" | custom-call | flops 6000000000 | tf_op jit(solution)/shard_map/cond/branch_1_fun/pallas_call | solution.py:137
  32.3 5.1 %collective-permute-done.7.refs_1_ = bf16[64,1536]{1,0:T(8,128)(2,1)} collective-permute-done((bf16[64,1536]{1,0:T(8,128)(2,1)}, bf16[64,1536]{1,0:T(8,128)(2,1)}, u32[]{:S(2)}, u32[]{:S(2)}) %collective-permute-start.7) | collective-permute-done | bytes 196640 | tf_op jit(solution)/shard_map/cond/branch_1_fun/ppermute | solution.py:161
  39.5 3.4 %branch_1_fun.5 = (f32[128,256]{1,0:T(8,128)}, bf16[320,256]{1,0:T(8,128)(2,1)}, bf16[320,256]{1,0:T(8,128)(2,1)}, bf16[320,256]{1,0:T(8,128)(2,1)}) custom-call(s32[2]{0:T(128)S(1)} %pad_add_fusion.place, bf16[128,6144]{1,0:T(8,128)(2,1)S(1)} %copy-done.1, bf16[64,1536]{1,0:T(8,128)(2,1)} %get-tuple-element.57.refs_0_, ...), custom_call_target="tpu_custom_call" | custom-call | tf_op jit(solution)/shard_map/cond/branch_1_fun/pallas_call | solution.py:259
  46.3 19.4 %conditional.5 = (bf16[128,256]{1,0:T(8,128)(2,1)S(1)}, bf16[32,6144]{1,0:T(8,128)(2,1)S(1)}, f32[3072,512]{1,0:T(8,128)}, f32[3072,512]{1,0:T(8,128)}, f32[288,...) conditional(s32[]{:T(128)} %convert_element_type.26, () %tuple.39, ...), branch_computations={%region_4.0_spmd, %region_5.0_spmd} | conditional | flops 1327117 | bytes 15007822 | solution.py:154
  46.3 3.5 %collective-permute-start = (bf16[320,256]{1,0:T(8,128)(2,1)}, bf16[320,256]{1,0:T(8,128)(2,1)S(1)}, u32[]{:S(2)}, u32[]{:S(2)}) collective-permute-start(bf16[320,256]{1,0:T(8,128)(2,1)} %get-tuple-element.71), channel_id=1, source_target_pairs={{0,12},{4,0},{8,4},{12,8},{1,13},{5,1},{9,5},{13,9},{2,14},{6,2},{... | collective-permute-start | bytes 491528 | tf_op jit(solution)/shard_map/cond/branch_1_fun/ppermute | solution.py:161
  50.0 1.9 %collective-permute-start.2 = (bf16[320,256]{1,0:T(8,128)(2,1)}, bf16[320,256]{1,0:T(8,128)(2,1)S(1)}, u32[]{:S(2)}, u32[]{:S(2)}) collective-permute-start(bf16[320,256]{1,0:T(8,128)(2,1)} %get-tuple-element.73), channel_id=1, source_target_pairs={{0,4},{4,8},{8,12},{12,0},{1,5},{5,9},{9,13},{13,1},{2,6},{6,10},{... | collective-permute-start | bytes 491528 | tf_op jit(solution)/shard_map/cond/branch_1_fun/ppermute | solution.py:161
  52.0 7.2 %branch_1_fun.8 = (f32[3072,512]{1,0:T(8,128)}, f32[3072,512]{1,0:T(8,128)}) custom-call(bf16[1824,512]{1,0:T(8,128)(2,1)} %get-tuple-element.76.theirs, bf16[3072,512]{1,0:T(8,128)(2,1)} %bitcast.33, f32[3072,512]{1,0:T(8,128)} %bitcast.36, f32[3072,512]{1,0:T(8,128)} %bitcast.39), custom_call_target="tpu_custom_call" | custom-call | tf_op jit(solution)/shard_map/cond/branch_1_fun/pallas_call | solution.py:101
  59.3 2.6 %branch_1_fun.9 = bf16[1536,256]{1,0:T(8,128)(2,1)S(1)} custom-call(s32[2]{0:T(128)S(1)} %pad_add_fusion.1.place, bf16[128,6144]{1,0:T(8,128)(2,1)S(1)} %copy-done.2, bf16[64,1536]{1,0:T(8,128)(2,1)} %get-tuple-element.83.refs_0_, bf16[64,1536]{1,0:T(8,128)(2,1)} %get-tuple-element.84.refs_1_, bf16[64,1536]{1,0:T(8,128)(2,1)} %get-tuple-element.85.refs_2_, ...), custom_call_target="tpu_custom_call" | custom-call | tf_op jit(solution)/shard_map/cond/branch_1_fun/pallas_call | solution.py:259
  64.0 1.7 %branch_1_fun.7 = (bf16[128,256]{1,0:T(8,128)(2,1)S(1)}, bf16[32,6144]{1,0:T(8,128)(2,1)S(1)}) custom-call(s32[2]{0:T(128)S(1)} %pad_add_fusion.1.place, f32[128,256]{1,0:T(8,128)} %get-tuple-element.69.keys_own, bf16[128,1536]{1,0:T(8,128)(2,1)} %get-tuple-element.70.summed, bf16[320,256]{1,0:T(8,128)(2,1)S(1)} %collective-permute-done.refs_0_, ...), custom_call_target="tpu_custom_call" | custom-call | tf_op jit(solution)/shard_map/cond/branch_1_fun/pallas_call | solution.py:259
  65.7 1.6 %collective-permute-start.15 = (bf16[96,512]{1,0:T(8,128)(2,1)S(1)}, bf16[96,512]{1,0:T(8,128)(2,1)S(1)}, u32[]{:S(2)}, u32[]{:S(2)}) collective-permute-start(bf16[96,512]{1,0:T(8,128)(2,1)S(1)} %get-tuple-element.177), channel_id=1, source_target_pairs={{0,16},{16,0},{1,17},{17,1},{2,18},{18,2},{3,19},{19,3},{4,20},{20... | collective-permute-start | bytes 294920 | tf_op jit(solution)/shard_map/ppermute | solution.py:149
  67.7 4.2 %shard_map.103 = (f32[3072,512]{1,0:T(8,128)}, f32[3072,512]{1,0:T(8,128)}) custom-call(bf16[960,512]{1,0:T(8,128)(2,1)S(1)} %collective-permute-done.17.theirs, bf16[3072,512]{1,0:T(8,128)(2,1)} %bitcast.31, f32[3072,512]{1,0:T(8,128)} %bitcast.35, f32[3072,512]{1,0:T(8,128)} %bitcast.38, ...), custom_call_target="tpu_custom_call", output_to_operand_aliasing={{0}: (4, {}), {1}: (5, {})} | custom-call | tf_op jit(solution)/shard_map/pallas_call | solution.py:101
  (53 shorter events, 17.5 us)
Async XLA Ops:
  2.1 44.2 %collective-permute-start.14 = (bf16[1824,512]{1,0:T(8,128)(2,1)S(1)}, bf16[1824,512]{1,0:T(8,128)(2,1)}, u32[]{:S(2)}, u32[]{:S(2)}) collective-permute-start(bf16[1824,512]{1,0:T(8,128)(2,1)S(1)} %shard_map.102), channel_id=1, source_target_pairs={{0,16},{16,0},{1,17},{17,1},{2,18},{18,2},{3,19},{19,3},{4,20},{20... | collective-permute-start | bytes 5603336 | tf_op jit(solution)/shard_map/ppermute | solution.py:149
  5.1 7.4 %collective-permute-start.4 = (bf16[128,256]{1,0:T(8,128)(2,1)}, bf16[128,256]{1,0:T(8,128)(2,1)S(1)}, u32[]{:S(2)}, u32[]{:S(2)}) collective-permute-start(bf16[128,256]{1,0:T(8,128)(2,1)} %get-tuple-element.200), channel_id=1, source_target_pairs={{0,8},{4,12},{8,0},{12,4},{1,9},{5,13},{9,1},{13,5},{2,10},{6,14},... | collective-permute-start | bytes 196616 | tf_op jit(solution)/shard_map/cond/branch_1_fun/ppermute | solution.py:161
  7.7 6.4 %collective-permute-start.3 = (bf16[128,256]{1,0:T(8,128)(2,1)}, bf16[128,256]{1,0:T(8,128)(2,1)S(1)}, u32[]{:S(2)}, u32[]{:S(2)}) collective-permute-start(bf16[128,256]{1,0:T(8,128)(2,1)} %get-tuple-element.200), channel_id=1, source_target_pairs={{0,4},{4,8},{8,12},{12,0},{1,5},{5,9},{9,13},{13,1},{2,6},{6,10},{... | collective-permute-start | bytes 196616 | tf_op jit(solution)/shard_map/cond/branch_1_fun/ppermute | solution.py:161
  9.3 5.2 %collective-permute-start.5 = (bf16[128,256]{1,0:T(8,128)(2,1)}, bf16[128,256]{1,0:T(8,128)(2,1)S(1)}, u32[]{:S(2)}, u32[]{:S(2)}) collective-permute-start(bf16[128,256]{1,0:T(8,128)(2,1)} %get-tuple-element.200), channel_id=1, source_target_pairs={{0,12},{4,0},{8,4},{12,8},{1,13},{5,1},{9,5},{13,9},{2,14},{6,2},{... | collective-permute-start | bytes 196616 | tf_op jit(solution)/shard_map/cond/branch_1_fun/ppermute | solution.py:161
  12.5 7.6 %collective-permute-start.6 = (bf16[64,1536]{1,0:T(8,128)(2,1)S(1)}, bf16[64,1536]{1,0:T(8,128)(2,1)}, u32[]{:S(2)}, u32[]{:S(2)}) collective-permute-start(bf16[64,1536]{1,0:T(8,128)(2,1)S(1)} %dynamic_slice.16), channel_id=1, source_target_pairs={{0,4},{4,8},{8,12},{12,0},{1,5},{5,9},{9,13},{13,1},{2,6},{6,10},{... | collective-permute-start | bytes 589832 | tf_op jit(solution)/shard_map/cond/branch_1_fun/ppermute | solution.py:161
  20.1 5.8 %collective-permute-start.12 = (bf16[256,1536]{1,0:T(8,128)(2,1)S(1)}, bf16[256,1536]{1,0:T(8,128)(2,1)S(1)}, u32[]{:S(2)}, u32[]{:S(2)}) collective-permute-start(bf16[256,1536]{1,0:T(8,128)(2,1)S(1)} %get-tuple-element.60), channel_id=1, source_target_pairs={{0,1},{1,0},{2,3},{3,2},{4,5},{5,4},{6,7},{7,6},{8,9},{9,8},{10,11... | collective-permute-start | bytes 2359304 | tf_op jit(solution)/shard_map/cond/branch_1_fun/ppermute | solution.py:165
  20.1 19.4 %collective-permute-start.9 = (bf16[64,1536]{1,0:T(8,128)(2,1)}, bf16[64,1536]{1,0:T(8,128)(2,1)}, u32[]{:S(2)}, u32[]{:S(2)}) collective-permute-start(bf16[64,1536]{1,0:T(8,128)(2,1)} %get-tuple-element.57.refs_0_), channel_id=1, source_target_pairs={{0,1},{1,0},{2,3},{3,2},{4,5},{5,4},{6,7},{7,6},{8,9},{9,8},{10,11... | collective-permute-start | bytes 589832 | tf_op jit(solution)/shard_map/cond/branch_1_fun/ppermute | solution.py:165
  22.4 9.8 %collective-permute-start.8 = (bf16[64,1536]{1,0:T(8,128)(2,1)}, bf16[64,1536]{1,0:T(8,128)(2,1)}, u32[]{:S(2)}, u32[]{:S(2)}) collective-permute-start(bf16[64,1536]{1,0:T(8,128)(2,1)} %get-tuple-element.205), channel_id=1, source_target_pairs={{0,12},{4,0},{8,4},{12,8},{1,13},{5,1},{9,5},{13,9},{2,14},{6,2},{... | collective-permute-start | bytes 589832 | tf_op jit(solution)/shard_map/cond/branch_1_fun/ppermute | solution.py:161
  25.0 12.4 %collective-permute-start.7 = (bf16[64,1536]{1,0:T(8,128)(2,1)}, bf16[64,1536]{1,0:T(8,128)(2,1)}, u32[]{:S(2)}, u32[]{:S(2)}) collective-permute-start(bf16[64,1536]{1,0:T(8,128)(2,1)} %get-tuple-element.206), channel_id=1, source_target_pairs={{0,8},{4,12},{8,0},{12,4},{1,9},{5,13},{9,1},{13,5},{2,10},{6,14},... | collective-permute-start | bytes 589832 | tf_op jit(solution)/shard_map/cond/branch_1_fun/ppermute | solution.py:161
  25.9 3.4 %copy-start.4 = (bf16[256,1536]{1,0:T(8,128)(2,1)}, bf16[256,1536]{1,0:T(8,128)(2,1)S(1)}, u32[]{:S(2)}) copy-start(bf16[256,1536]{1,0:T(8,128)(2,1)S(1)} %collective-permute-done.12) | copy-start | bytes 2359300 | tf_op jit(solution)/shard_map/cond
  27.7 10.9 %collective-permute-start.13 = (bf16[128,1536]{1,0:T(8,128)(2,1)S(1)}, bf16[128,1536]{1,0:T(8,128)(2,1)S(1)}, u32[]{:S(2)}, u32[]{:S(2)}) collective-permute-start(bf16[128,1536]{1,0:T(8,128)(2,1)S(1)} %add_convert_fusion.1), channel_id=1, source_target_pairs={{0,2},{1,3},{2,0},{3,1},{4,6},{5,7},{6,4},{7,5},{8,10},{9,11},{10,... | collective-permute-start | bytes 1179656 | tf_op jit(solution)/shard_map/cond/branch_1_fun/ppermute | solution.py:165
  29.3 9.3 %copy-start.5 = (bf16[256,1536]{1,0:T(8,128)(2,1)S(1)}, bf16[256,1536]{1,0:T(8,128)(2,1)}, u32[]{:S(2)}) copy-start(bf16[256,1536]{1,0:T(8,128)(2,1)} %copy-done.4) | copy-start | bytes 2359300 | tf_op jit(solution)/shard_map/cond
  29.3 10.2 %copy-start.1 = (bf16[128,6144]{1,0:T(8,128)(2,1)S(1)}, bf16[128,6144]{1,0:T(8,128)(2,1)}, u32[]{:S(2)}) copy-start(bf16[128,6144]{1,0:T(8,128)(2,1)} %get-tuple-element.56.own) | copy-start | bytes 4718596 | tf_op jit(solution)/shard_map/cond
  32.3 7.2 %collective-permute-start.11 = (bf16[64,1536]{1,0:T(8,128)(2,1)}, bf16[64,1536]{1,0:T(8,128)(2,1)}, u32[]{:S(2)}, u32[]{:S(2)}) collective-permute-start(bf16[64,1536]{1,0:T(8,128)(2,1)} %collective-permute-done.8.refs_2_), channel_id=1, source_target_pairs={{0,1},{1,0},{2,3},{3,2},{4,5},{5,4},{6,7},{7,6},{8,9},{9,8},{10,11... | collective-permute-start | bytes 589832 | tf_op jit(solution)/shard_map/cond/branch_1_fun/ppermute | solution.py:165
  37.5 2.0 %collective-permute-start.10 = (bf16[64,1536]{1,0:T(8,128)(2,1)}, bf16[64,1536]{1,0:T(8,128)(2,1)}, u32[]{:S(2)}, u32[]{:S(2)}) collective-permute-start(bf16[64,1536]{1,0:T(8,128)(2,1)} %collective-permute-done.7.refs_1_), channel_id=1, source_target_pairs={{0,1},{1,0},{2,3},{3,2},{4,5},{5,4},{6,7},{7,6},{8,9},{9,8},{10,11... | collective-permute-start | bytes 589832 | tf_op jit(solution)/shard_map/cond/branch_1_fun/ppermute | solution.py:165
  42.9 24.8 %collective-permute-start.17 = (bf16[960,512]{1,0:T(8,128)(2,1)}, bf16[960,512]{1,0:T(8,128)(2,1)S(1)}, u32[]{:S(2)}, u32[]{:S(2)}) collective-permute-start(bf16[960,512]{1,0:T(8,128)(2,1)} %get-tuple-element.179), channel_id=1, source_target_pairs={{0,16},{16,0},{1,17},{17,1},{2,18},{18,2},{3,19},{19,3},{4,20},{20... | collective-permute-start | bytes 2949128 | tf_op jit(solution)/shard_map/ppermute | solution.py:149
  43.4 28.6 %collective-permute-start.16 = (bf16[192,512]{1,0:T(8,128)(2,1)}, bf16[192,512]{1,0:T(8,128)(2,1)S(1)}, u32[]{:S(2)}, u32[]{:S(2)}) collective-permute-start(bf16[192,512]{1,0:T(8,128)(2,1)} %get-tuple-element.178), channel_id=1, source_target_pairs={{0,16},{16,0},{1,17},{17,1},{2,18},{18,2},{3,19},{19,3},{4,20},{20... | collective-permute-start | bytes 589832 | tf_op jit(solution)/shard_map/ppermute | solution.py:149
  46.3 17.1 %collective-permute-start = (bf16[320,256]{1,0:T(8,128)(2,1)}, bf16[320,256]{1,0:T(8,128)(2,1)S(1)}, u32[]{:S(2)}, u32[]{:S(2)}) collective-permute-start(bf16[320,256]{1,0:T(8,128)(2,1)} %get-tuple-element.71), channel_id=1, source_target_pairs={{0,12},{4,0},{8,4},{12,8},{1,13},{5,1},{9,5},{13,9},{2,14},{6,2},{... | collective-permute-start | bytes 491528 | tf_op jit(solution)/shard_map/cond/branch_1_fun/ppermute | solution.py:161
  49.8 14.2 %collective-permute-start.1 = (bf16[320,256]{1,0:T(8,128)(2,1)}, bf16[320,256]{1,0:T(8,128)(2,1)S(1)}, u32[]{:S(2)}, u32[]{:S(2)}) collective-permute-start(bf16[320,256]{1,0:T(8,128)(2,1)} %get-tuple-element.72), channel_id=1, source_target_pairs={{0,8},{4,12},{8,0},{12,4},{1,9},{5,13},{9,1},{13,5},{2,10},{6,14},... | collective-permute-start | bytes 491528 | tf_op jit(solution)/shard_map/cond/branch_1_fun/ppermute | solution.py:161
  50.0 14.0 %collective-permute-start.2 = (bf16[320,256]{1,0:T(8,128)(2,1)}, bf16[320,256]{1,0:T(8,128)(2,1)S(1)}, u32[]{:S(2)}, u32[]{:S(2)}) collective-permute-start(bf16[320,256]{1,0:T(8,128)(2,1)} %get-tuple-element.73), channel_id=1, source_target_pairs={{0,4},{4,8},{8,12},{12,0},{1,5},{5,9},{9,13},{13,1},{2,6},{6,10},{... | collective-permute-start | bytes 491528 | tf_op jit(solution)/shard_map/cond/branch_1_fun/ppermute | solution.py:161
  52.0 7.2 %copy-start.2 = (bf16[128,6144]{1,0:T(8,128)(2,1)S(1)}, bf16[128,6144]{1,0:T(8,128)(2,1)}, u32[]{:S(2)}) copy-start(bf16[128,6144]{1,0:T(8,128)(2,1)} %get-tuple-element.82.own) | copy-start | bytes 4718596 | tf_op jit(solution)/shard_map/cond
  65.7 6.2 %copy-start.6 = (bf16[32,6144]{1,0:T(8,128)(2,1)}, bf16[32,6144]{1,0:T(8,128)(2,1)S(1)}, u32[]{:S(2)}) copy-start(bf16[32,6144]{1,0:T(8,128)(2,1)S(1)} %get-tuple-element.143) | copy-start | bytes 1179652
  65.7 6.2 %copy-start.7 = (bf16[128,256]{1,0:T(8,128)(2,1)}, bf16[128,256]{1,0:T(8,128)(2,1)S(1)}, u32[]{:S(2)}) copy-start(bf16[128,256]{1,0:T(8,128)(2,1)S(1)} %get-tuple-element.142) | copy-start | bytes 196612
  65.7 7.5 %collective-permute-start.15 = (bf16[96,512]{1,0:T(8,128)(2,1)S(1)}, bf16[96,512]{1,0:T(8,128)(2,1)S(1)}, u32[]{:S(2)}, u32[]{:S(2)}) collective-permute-start(bf16[96,512]{1,0:T(8,128)(2,1)S(1)} %get-tuple-element.177), channel_id=1, source_target_pairs={{0,16},{16,0},{1,17},{17,1},{2,18},{18,2},{3,19},{19,3},{4,20},{20... | collective-permute-start | bytes 294920 | tf_op jit(solution)/shard_map/ppermute | solution.py:149
  (2 other events, 4.6 us)
